TPU v7x, 32 devices: a whole 2x2x4 slice. The times are simulated.
32 devices in a mesh: dp: 2 (over x), row: 4 (over y, core), col: 4 (over z).
Axes of the slice: x: 2, y: 2, z: 4, core: 2. Of those that a mesh axis runs over, the one named last changes fastest.
Arguments:
- tokens: bfloat16 [4096, 2048], P(('dp', 'col'), 'row'), may hold values from -60 to 60
- segments: int32 [4096], P('dp'), may hold values from 0 to 2047, as said below
- mix_gain: float32 [2048], P('row'), may hold values from 0.5 to 1.5
- w_mix: bfloat16 [2048, 4, 2048], P('row', None, 'col'), may hold values from -0.125 to 0.125
- lower_bound: float32 [2048], P('col'), may hold values from 0.25 to 1
- group_gain: float32 [128], replicated, may hold values from 0.5 to 1.5
- w_out: bfloat16 [2048, 2048], P('col', 'row'), may hold values from -0.21875 to 0.21875
- ffn_gain: float32 [2048], P('row'), may hold values from 0.5 to 1.5
- w_ffn_in: bfloat16 [2048, 2, 5632], P('row', None, 'col'), may hold values from -0.125 to 0.125
- w_down: bfloat16 [5632, 2048], P('col', 'row'), may hold values from -0.125 to 0.125
- cotangent: bfloat16 [4096, 2048], P(('dp', 'col'), 'row'), may hold values from -6 to 6
Outputs:
- output: bfloat16 [4096, 2048], P(('dp', 'col'), 'row')
- grad_tokens: float32 [4096, 2048], P(('dp', 'col'), 'row')
- grad_mix_gain: float32 [2048], P('row')
- grad_w_mix: float32 [2048, 4, 2048], P('row', None, 'col')
- grad_lower_bound: float32 [2048], P('col')
- grad_group_gain: float32 [128], replicated
- grad_w_out: float32 [2048, 2048], P('col', 'row')
- grad_ffn_gain: float32 [2048], P('row')
- grad_w_ffn_in: float32 [2048, 2, 5632], P('row', None, 'col')
- grad_w_down: float32 [5632, 2048], P('col', 'row')
Inputs may be any that keep to these rules, and one draw needn't show every extreme that they name: `segments`: within each packed sequence of 2048 tokens the ids start at 0 and never fall; a document is a run of equal ids, and the last document of every sequence has the id 2048 - 1. In every sequence one document starts within the sequence's first 512 tokens, after its first token, and ends within its last 512 tokens.
All inputs are finite; a program needn't handle non-finite values.
Results may differ from a plain program's by a relative error of at most 0.013.
Values may be sent and summed in bfloat16 or wider, within the bound.
No kernel may reach another device: no remote copies, remote signals or barrier semaphores. Data moves between devices by JAX's collectives and lax.ppermute only.
A program may use at most 256 MiB of HBM per device.

v0:
```python
from functools import partial
import math

import jax
import jax.numpy as jnp
from jax import lax
from jax.sharding import PartitionSpec as P

D = 2048
HEADS = 16


norm_eps = 1e-06
exact_result = lax.Precision.HIGHEST


def carried_in(value, axis, join, neutral):
    count, mine = (lax.axis_size(axis), lax.axis_index(axis))
    pieces = jax.tree.map(lambda part: lax.all_gather(part, axis), value)
    so_far = jax.tree.map(
        lambda part, zero: jnp.full_like(part, 0) + jnp.asarray(zero, part.dtype), value, neutral
    )

    def carried_step(position, so_far):
        longer = join(so_far, jax.tree.map(lambda part: part[position], pieces))
        return jax.tree.map(lambda new, old: jnp.where(position < mine, new, old), longer, so_far)

    return lax.fori_loop(0, count - 1, carried_step, so_far)


def entering_2(value, axis, combine, identity):
    count, here = (lax.axis_size(axis), lax.axis_index(axis))
    everything = jax.tree.map(
        lambda part, kind: lax.all_gather(part.astype(kind), axis),
        value,
        jax.tree.map(lambda a: jnp.bfloat16 if a.dtype == jnp.float32 else a.dtype, value),
    )
    start = jax.tree.map(
        lambda part, zero: jnp.broadcast_to(jnp.asarray(zero, part.dtype), part.shape),
        value,
        identity,
    )

    def entering_step(k, before):
        at = count - 1 - k
        reached = at > here
        new = combine(
            before, jax.tree.map(lambda part, own: part[at].astype(own.dtype), everything, value)
        )
        return jax.tree.map(lambda a, b: jnp.where(reached, a, b), new, before)

    return lax.fori_loop(0, count, entering_step, start)


def silu(value):
    return value * jax.nn.sigmoid(value)


def silu_slope(value):
    sigma = jax.nn.sigmoid(value)
    return sigma * (1.0 + value * (1.0 - sigma))


def gather_cols(local):
    return lax.all_gather(local, "col", axis=0, tiled=True)


def gather_rows(local):
    return lax.all_gather(local, "row", axis=0, tiled=True)


def feature_total(partial_sums):
    return lax.psum(partial_sums, "row")


def contract_term(left, right, contract):
    return lax.dot_general(
        left, right, (((1,), (contract,)), ((), ())), preferred_element_type=jnp.float32
    )


def sum_rows(left, right, contract):
    return lax.psum_scatter(
        contract_term(left, right, contract), "row", scatter_dimension=0, tiled=True
    )


def sum_cols(left, right, contract):
    return lax.psum_scatter(
        contract_term(left, right, contract), "col", scatter_dimension=0, tiled=True
    )


def token_grad(left, right):
    return lax.dot_general(
        left, right, (((0,), (0,)), ((), ())), preferred_element_type=jnp.float32
    )


def norm_forward(values, gain):
    scale = lax.rsqrt(feature_total(jnp.sum(values * values, axis=1)) / D + norm_eps)
    return (scale, (values * scale[:, None] * gain).astype(jnp.bfloat16))


def norm_backward(values, scale, gain, grad_normed):
    weighted = grad_normed * gain
    along = feature_total(jnp.sum(weighted * values, axis=1))
    grad_values = scale[:, None] * weighted - values * (scale * scale * scale * along / D)[:, None]
    grad_gain = jnp.sum(grad_normed * values * scale[:, None], axis=0)
    return (grad_values, grad_gain)


def chain(earlier, later):
    return (earlier[0] * later[0], later[0][:, :, None] * earlier[1] + later[1])


def local_parts(fresh, block, queries, keys, values, log_forget):
    length, heads, size = queries.shape
    count = length // block

    def blocked(array):
        return array.reshape(count, block, heads, size)

    queries = blocked(queries)
    keys = blocked(keys)
    values = blocked(values)
    running = jnp.cumsum(blocked(log_forget), axis=1)
    segment = jnp.cumsum(fresh.reshape(count, block), axis=1)
    places = jnp.arange(block)
    pairs = (segment[:, :, None] == segment[:, None, :]) & (places[:, None] >= places[None, :])[
        None
    ]
    pair_mask = pairs[:, :, :, None, None]
    spread = jnp.where(pair_mask, running[:, :, None] - running[:, None, :], 0.0)
    weights = jnp.where(pair_mask, jnp.exp(spread), 0.0)
    scores = jnp.einsum("nthk,nshk,ntshk->ntsh", queries, keys, weights, precision=exact_result)
    inner = jnp.einsum("ntsh,nshv->nthv", scores, values, precision=exact_result)
    closing = segment[:, -1:]
    tail_mask = (segment == closing)[:, :, None, None]
    tail = jnp.where(tail_mask, jnp.exp(jnp.where(tail_mask, running[:, -1:] - running, 0.0)), 0.0)
    fills = jnp.einsum("nshk,nshv->nhkv", keys * tail, values, precision=exact_result)
    carried = jnp.exp(running[:, -1]) * (closing == 0).astype(jnp.float32)[:, :, None]
    head_mask = (segment == 0)[:, :, None, None]
    opened = queries * jnp.where(head_mask, jnp.exp(running), 0.0)

    def advance(carried_state, item):
        state, kept = carried_state
        keep, fill = item
        return ((keep[:, :, None] * state + fill, kept * keep), (state, kept))

    initial = (jnp.zeros((heads, size, size), jnp.float32), jnp.ones((heads, size), jnp.float32))
    (final_state, total_keep), (states, prefix) = lax.scan(advance, initial, (carried, fills))
    inner = inner + jnp.einsum("nthk,nhkv->nthv", opened, states, precision=exact_result)
    passing_value = opened * prefix[:, None]
    return (
        inner.reshape(length, heads, size),
        final_state,
        total_keep,
        passing_value.reshape(length, heads, size),
    )


def shards(
    tokens,
    segments,
    mix_gain,
    w_mix,
    lower_bound,
    group_gain,
    w_out,
    ffn_gain,
    w_ffn_in,
    w_down,
    cotangent,
):
    size = D // HEADS
    width_row = tokens.shape[1]
    width_col = w_out.shape[0]
    units_col = w_down.shape[0]
    span = segments.shape[0]
    tokens_row = span // lax.axis_size("row")
    heads_here = width_col // size
    row_place = lax.axis_index("row")
    col_place = lax.axis_index("col")
    block = math.gcd(tokens_row, 32)

    def per_head(array):
        return array.reshape(tokens_row, heads_here, size)

    inputs = tokens.astype(jnp.float32)
    mix_scale, mixed_in = norm_forward(inputs, mix_gain)
    mixed_all = gather_cols(mixed_in)
    mix_flat = w_mix.reshape(width_row, 4 * width_col)
    projected = sum_rows(mixed_all, mix_flat, 0).reshape(tokens_row, 4, width_col)
    query_raw = projected[:, 0]
    forget_raw = projected[:, 1]
    input_raw = projected[:, 2]
    gate_raw = projected[:, 3]
    changed = jnp.concatenate(
        [jnp.ones((1,), jnp.int32), (segments[1:] != segments[:-1]).astype(jnp.int32)]
    )
    fresh = lax.dynamic_slice_in_dim(changed, row_place * tokens_row, tokens_row, 0)
    queries = silu(query_raw)
    closed = jax.nn.sigmoid(-forget_raw)
    keys = (1.0 - lower_bound) * closed
    log_forget = jnp.log1p(-keys)
    parts, pull_parts = jax.vjp(
        partial(local_parts, fresh, block),
        per_head(queries),
        per_head(keys),
        per_head(input_raw),
        per_head(log_forget),
    )
    inner_output, final_state, total_keep, passing_value = parts
    identity = (jnp.ones_like(total_keep), jnp.zeros_like(final_state))
    entering = carried_in((total_keep, final_state), "row", chain, identity)
    incoming_state = entering[1]
    recurrence_output = inner_output + jnp.einsum(
        "rua,uao->ruo", passing_value, incoming_state, precision=exact_result
    )
    head_scale = lax.rsqrt(
        jnp.mean(recurrence_output * recurrence_output, axis=2, keepdims=True) + norm_eps
    )
    normed = recurrence_output * head_scale
    gate_act = per_head(silu(gate_raw))
    gated = (normed * group_gain * gate_act).reshape(tokens_row, width_col).astype(jnp.bfloat16)
    gated_all = gather_rows(gated)
    mixer_out = sum_cols(gated_all, w_out, 0)
    hidden = inputs + mixer_out
    ffn_scale, ffn_in = norm_forward(hidden, ffn_gain)
    ffn_all = gather_cols(ffn_in)
    ffn_flat = w_ffn_in.reshape(width_row, 2 * units_col)
    local_both = jnp.dot(ffn_all, ffn_flat, preferred_element_type=jnp.float32)
    both_all = lax.psum(local_both, "row").reshape(span, 2, units_col)
    units_all = (silu(both_all[:, 0]) * both_all[:, 1]).astype(jnp.bfloat16)
    both = lax.dynamic_slice_in_dim(both_all, row_place * tokens_row, tokens_row, 0)
    ffn_out = sum_cols(units_all, w_down, 0)
    output = (hidden + ffn_out).astype(jnp.bfloat16)
    upstream = cotangent.astype(jnp.float32)
    upstream_all = gather_cols(cotangent)
    grad_w_down = token_grad(units_all, upstream_all)
    grad_units = sum_rows(upstream_all, w_down, 1)
    gate_part = both[:, 0]
    up_part = both[:, 1]
    grad_both = jnp.stack(
        [grad_units * up_part * silu_slope(gate_part), grad_units * silu(gate_part)], axis=1
    )
    grad_both_all = gather_rows(grad_both.reshape(tokens_row, 2 * units_col).astype(jnp.bfloat16))
    grad_w_ffn = token_grad(ffn_all, grad_both_all).reshape(width_row, 2, units_col)
    grad_ffn_in = sum_cols(grad_both_all, ffn_flat, 1)
    grad_hidden_norm, ffn_gain_part = norm_backward(hidden, ffn_scale, ffn_gain, grad_ffn_in)
    grad_hidden = upstream + grad_hidden_norm
    grad_mixer_all = gather_cols(grad_hidden.astype(jnp.bfloat16))
    grad_w_out = token_grad(gated_all, grad_mixer_all)
    grad_gated = per_head(sum_rows(grad_mixer_all, w_out, 1))
    grad_normed = grad_gated * group_gain * gate_act
    group_part = jnp.sum(grad_gated * normed * gate_act, axis=(0, 1))
    grad_gate_raw = grad_gated * normed * group_gain * per_head(silu_slope(gate_raw))
    recurrence_gradient = head_scale * (
        grad_normed - normed * jnp.mean(grad_normed * normed, axis=2, keepdims=True)
    )
    passing_gradient = jnp.einsum(
        "mxf,xuf->mxu", recurrence_gradient, incoming_state, precision=exact_result
    )
    toward_input = jnp.einsum(
        "fui,fuo->uio", passing_value, recurrence_gradient, precision=exact_result
    )
    leaving = entering_2((total_keep, toward_input), "row", chain, identity)
    grad_final = leaving[1]
    grad_keep = jnp.sum(grad_final * incoming_state, axis=2)
    grad_queries, grad_keys, grad_values, grad_log = pull_parts(
        (recurrence_gradient, grad_final, grad_keep, passing_gradient)
    )
    key_total = (grad_keys - grad_log / (1.0 - per_head(keys))).reshape(tokens_row, width_col)
    grad_forget_raw = -key_total * (1.0 - lower_bound) * closed * (1.0 - closed)
    bound_part = -jnp.sum(key_total * closed, axis=0)
    grad_query_raw = grad_queries.reshape(tokens_row, width_col) * silu_slope(query_raw)
    grad_projected = jnp.stack(
        [
            grad_query_raw,
            grad_forget_raw,
            grad_values.reshape(tokens_row, width_col),
            grad_gate_raw.reshape(tokens_row, width_col),
        ],
        axis=1,
    )
    grad_projected_all = gather_rows(
        grad_projected.reshape(tokens_row, 4 * width_col).astype(jnp.bfloat16)
    )
    grad_w_mix = token_grad(mixed_all, grad_projected_all).reshape(width_row, 4, width_col)
    grad_mixed_in = sum_cols(grad_projected_all, mix_flat, 1)
    grad_inputs_norm, mix_gain_part = norm_backward(inputs, mix_scale, mix_gain, grad_mixed_in)
    grad_tokens = grad_hidden + grad_inputs_norm
    grad_w_mix, grad_w_out, grad_w_ffn, grad_w_down = (
        lax.psum(grad_w_mix.astype(jnp.bfloat16), "dp").astype(jnp.float32),
        lax.psum(grad_w_out.astype(jnp.bfloat16), "dp").astype(jnp.float32),
        lax.psum(grad_w_ffn.astype(jnp.bfloat16), "dp").astype(jnp.float32),
        lax.psum(grad_w_down.astype(jnp.bfloat16), "dp").astype(jnp.float32),
    )
    row_offset = row_place * width_row
    col_offset = col_place * width_col
    empty = jnp.zeros((D,), jnp.float32)
    full_mix = lax.dynamic_update_slice_in_dim(empty, mix_gain_part, row_offset, 0)
    full_ffn = lax.dynamic_update_slice_in_dim(empty, ffn_gain_part, row_offset, 0)
    full_bound = lax.dynamic_update_slice_in_dim(empty, bound_part, col_offset, 0)
    full_mix, full_ffn, full_bound, group_total = lax.psum(
        (full_mix, full_ffn, full_bound, group_part), ("dp", "row", "col")
    )
    grad_mix_gain = lax.dynamic_slice_in_dim(full_mix, row_offset, width_row, 0)
    grad_ffn_gain = lax.dynamic_slice_in_dim(full_ffn, row_offset, width_row, 0)
    grad_bound = lax.dynamic_slice_in_dim(full_bound, col_offset, width_col, 0)
    return (
        output,
        grad_tokens,
        grad_mix_gain,
        grad_w_mix,
        grad_bound,
        group_total,
        grad_w_out,
        grad_ffn_gain,
        grad_w_ffn,
        grad_w_down,
    )


def solution(mesh):
    return jax.shard_map(
        shards,
        mesh=mesh,
        in_specs=(
            P(("dp", "col"), "row"),
            P("dp"),
            P("row"),
            P("row", None, "col"),
            P("col"),
            P(),
            P("col", "row"),
            P("row"),
            P("row", None, "col"),
            P("col", "row"),
            P(("dp", "col"), "row"),
        ),
        out_specs=(
            P(("dp", "col"), "row"),
            P(("dp", "col"), "row"),
            P("row"),
            P("row", None, "col"),
            P("col"),
            P(),
            P("col", "row"),
            P("row"),
            P("row", None, "col"),
            P("col", "row"),
        ),
        check_vma=False,
    )
```

profile of v0, /device:TPU:0, one launch (start us, length us, event | category | flops | bytes accessed | tf_op | source)
XLA Modules:
  0.0 1992.2 jit_solution(16262044494789156503)
XLA Ops:
  21.9 44.1 %all-gather.15.cloned.1.call-done = bf16[2048,512]{1,0:T(8,128)(2,1)} async-done(((bf16[512,512]{1,0:T(8,128)(2,1)}), bf16[2048,512]{1,0:T(8,128)(2,1)}) %all-gather.15.cloned.1.call-update) | async-done | bytes 2097168 | tf_op jit(solution)/shard_map/all_gather | solution.py:65
  79.7 120.9 %reduce-scatter.8.cloned.1.call-done = f32[512,2048]{1,0:T(8,128)} async-done(((f32[2048,2048]{1,0:T(8,128)}), f32[512,2048]{1,0:T(8,128)}) %reduce-scatter.8.cloned.1.call-update) | async-done | bytes 4194320 | tf_op jit(solution)/shard_map/reduce_scatter | solution.py:83
  235.5 95.9 %while.70 = (s32[]{:T(128)}, f32[4,128,128]{2,1,0:T(8,128)}, f32[4,128]{1,0:T(4,128)S(1)}, f32[16,4,128,128]{3,2,1,0:T(8,128)}, f32[16,4,128]{2,1,0:T(4,128)}, /...) while((s32[]{:T(128)}, f32[4,128,128]{2,1,0:T(8,128)}, ...), condition=%wide.region_6.7_spmd.clone, body=%wide.region_5.6_spmd.clone.sunk | while | flops 263683 | bytes 1330810 | solution.py:152
  337.4 15.8 fusion.14
  400.9 22.7 %all-gather.17.cloned.1.call-done = bf16[2048,512]{0,1:T(8,128)(2,1)} async-done(((bf16[512,512]{0,1:T(8,128)(2,1)}), bf16[2048,512]{0,1:T(8,128)(2,1)}) %all-gather.17.cloned.1.call-update) | async-done | bytes 2097168 | tf_op jit(solution)/shard_map/all_gather | solution.py:69
  429.2 76.3 %reduce-scatter.10.cloned.1.call-done = f32[512,512]{1,0:T(8,128)} async-done(((f32[2048,512]{1,0:T(8,128)}), f32[512,512]{1,0:T(8,128)}) %reduce-scatter.10.cloned.1.call-update) | async-done | bytes 1048592 | tf_op jit(solution)/shard_map/reduce_scatter | solution.py:89
  518.7 34.8 %all-gather.21.cloned.1.call-done = bf16[2048,512]{1,0:T(8,128)(2,1)} async-done(((bf16[512,512]{1,0:T(8,128)(2,1)}), bf16[2048,512]{1,0:T(8,128)(2,1)}) %all-gather.21.cloned.1.call-update) | async-done | bytes 2097168 | tf_op jit(solution)/shard_map/all_gather | solution.py:65
  565.2 35.0 %all-gather.19.cloned.1.call-done = bf16[2048,512]{1,0:T(8,128)(2,1)} async-done(((bf16[512,512]{1,0:T(8,128)(2,1)}), bf16[2048,512]{1,0:T(8,128)(2,1)}) %all-gather.19.cloned.1.call-update) | async-done | bytes 2097168 | tf_op jit(solution)/shard_map/all_gather | solution.py:65
  608.9 12.4 copy.386
  621.4 72.4 %reduce-scatter.14.cloned.1.call-done = f32[512,1408]{1,0:T(8,128)} async-done(((f32[2048,1408]{1,0:T(8,128)}), f32[512,1408]{1,0:T(8,128)}) %reduce-scatter.14.cloned.1.call-update) | async-done | bytes 2883600 | tf_op jit(solution)/shard_map/reduce_scatter | solution.py:83
  693.8 392.3 %all-reduce.7.cloned.1.call-done = f32[2048,2,1408]{2,0,1:T(8,128)} async-done(((f32[2048,2,1408]{2,0,1:T(8,128)}), f32[2048,2,1408]{2,0,1:T(8,128)}) %all-reduce.7.cloned.1.call-update) | async-done | bytes 23068688 | tf_op jit(solution)/shard_map/psum | solution.py:234
  1097.8 76.2 %all-gather.23.cloned.1.call-done = bf16[2048,2816]{0,1:T(8,128)(2,1)} async-done(((bf16[512,2816]{0,1:T(8,128)(2,1)}), bf16[2048,2816]{0,1:T(8,128)(2,1)}) %all-gather.23.cloned.1.call-update) | async-done | bytes 11534352 | tf_op jit(solution)/shard_map/all_gather | solution.py:69
  1185.3 76.9 %reduce-scatter.16.cloned.1.call-done = f32[512,512]{1,0:T(8,128)} async-done(((f32[2048,512]{1,0:T(8,128)}), f32[512,512]{1,0:T(8,128)}) %reduce-scatter.16.cloned.1.call-update) | async-done | bytes 1048592 | tf_op jit(solution)/shard_map/reduce_scatter | solution.py:89
  1275.6 45.6 %all-gather.25.cloned.1.call-done = bf16[2048,512]{1,0:T(8,128)(2,1)} async-done(((bf16[512,512]{1,0:T(8,128)(2,1)}), bf16[2048,512]{1,0:T(8,128)(2,1)}) %all-gather.25.cloned.1.call-update) | async-done | bytes 2097168 | tf_op jit(solution)/shard_map/all_gather | solution.py:65
  1331.4 38.2 %reduce-scatter.18.cloned.1.call-done = f32[512,512]{1,0:T(8,128)} async-done(((f32[2048,512]{1,0:T(8,128)}), f32[512,512]{1,0:T(8,128)}) %reduce-scatter.18.cloned.1.call-update) | async-done | bytes 1048592 | tf_op jit(solution)/shard_map/reduce_scatter | solution.py:83
  1397.8 14.7 fusion.12
  1412.5 19.6 fusion.21
  1432.1 16.1 fusion.13
  1466.4 65.5 %while.69 = (s32[]{:T(128)}, f32[4,128,128]{2,1,0:T(8,128)S(1)}, f32[4,128]{1,0:T(4,128)S(1)}, f32[16,4,128]{2,1,0:T(4,128)S(1)}, f32[16,4,128,128]{3,2,1,0:T(8,...) while((s32[]{:T(128)}, f32[4,128,128]{2,1,0:T(8,128)S(1)}, ...), condition=%wide.region_27.28_spmd, body=%wide.region_25.27_spmd.sunk | while | flops 263683 | bytes 1597597 | solution.py:152
  1621.1 21.1 %all-gather.27.cloned.1.call-done = bf16[2048,2048]{0,1:T(8,128)(2,1)} async-done(((bf16[512,2048]{0,1:T(8,128)(2,1)}), bf16[2048,2048]{0,1:T(8,128)(2,1)}) %all-gather.27.cloned.1.call-update) | async-done | bytes 8388624 | tf_op jit(solution)/shard_map/all_gather | solution.py:69
  1675.9 146.2 %all-reduce.9.cloned.1.call-done = (bf16[512,4,512]{2,1,0:T(4,128)(2,1)}, bf16[512,512]{1,0:T(8,128)(2,1)}, bf16[512,2,1408]{2,1,0:T(2,128)(2,1)}, bf16[1408,512]{1,0:T(8,128)(2,1)}) async-done(((bf16[512,4,512]{2,1,0:T(4,128)(2,1)}, bf16[512,512]{1,0:T(8,128)(2,1)}, bf16[512,2,1408]{2,1,0:T(2,128)(2,1)}, bf16[1408,512]{1,0:T(8,128)(2,1)}), (bf16[512,4,512]{2,1,0:T(4,128)(2,1)}, bf16[512,512]{1,0:T(8,128)(2,1)}, ...) | async-done | bytes 6946832 | tf_op jit(solution)/shard_map/psum | solution.py:295
  1834.6 66.6 %reduce-scatter.20.cloned.1.call-done = f32[512,512]{1,0:T(8,128)} async-done(((f32[2048,512]{1,0:T(8,128)}), f32[512,512]{1,0:T(8,128)}) %reduce-scatter.20.cloned.1.call-update) | async-done | bytes 1048592 | tf_op jit(solution)/shard_map/reduce_scatter | solution.py:89
  1904.3 46.5 %all-reduce.2 = (f32[2048]{0:T(1024)}, f32[2048]{0:T(1024)}, f32[128]{0:T(128)}, f32[2048]{0:T(1024)}) all-reduce(f32[2048]{0:T(1024)S(1)} %dynamic_update_slice.39, f32[2048]{0:T(1024)} %bitcast_dynamic-update-slice_fusion.4, f32[128]{0:T(128)} %get-tuple-element.574, ...), channel_id=1, replica_groups=mesh['dp'=2,'row'=4,'col'=4] {'dp','row','col'}, use_global_device_ids=true, to_apply=%region_36.37 | all-reduce | flops 6272 | bytes 50176 | tf_op jit(solution)/shard_map/psum | solution.py:306
  1961.9 19.7 reduce-scatter.12.cloned.1.call-done
  (502 shorter events, 572.9 us)
Async XLA Ops:
  7.2 546.2 %copy-start = (bf16[1408,512]{1,0:T(8,128)(2,1)S(1)}, bf16[1408,512]{1,0:T(8,128)(2,1)}, u32[]{:S(2)}) copy-start(bf16[1408,512]{1,0:T(8,128)(2,1)} %param.28) | copy-start | bytes 4325380
  7.2 58.8 %all-gather.15.cloned.1.call-start = ((), (), s32[]{:S(2)}) async-start(), calls=%async_computation.7 | async-start | bytes 2621440 | tf_op jit(solution)/shard_map/all_gather | solution.py:65
  19.6 181.1 %reduce-scatter.8.cloned.1.call-start = ((), (), s32[]{:S(2)}) async-start(), calls=%async_computation.8 | async-start | bytes 20971520 | tf_op jit(solution)/shard_map/reduce_scatter | solution.py:83
  75.6 313.0 %all-gather.29.cloned.1.call-start = ((), (), s32[]{:S(2)}) async-start(), calls=%async_computation.22 | async-start | bytes 1310720 | tf_op jit(solution)/shard_map/all_gather | solution.py:19
  77.0 254.5 %copy-start.60 = (pred[16,32]{1,0:T(8,128)(4,1)}, pred[16,32]{1,0:T(8,128)(4,1)S(1)}, u32[]{:S(2)}) copy-start(pred[16,32]{1,0:T(8,128)(4,1)S(1)} %get-tuple-element.672) | copy-start | bytes 1540
  334.2 89.4 %all-gather.17.cloned.1.call-start = ((), (), s32[]{:S(2)}) async-start(), calls=%async_computation.9 | async-start | bytes 2621440 | tf_op jit(solution)/shard_map/all_gather | solution.py:69
  400.8 104.7 %reduce-scatter.10.cloned.1.call-start = ((), (), s32[]{:S(2)}) async-start(), calls=%async_computation.10 | async-start | bytes 5242880 | tf_op jit(solution)/shard_map/reduce_scatter | solution.py:89
  428.6 124.8 %all-gather.21.cloned.1.call-start = ((), (), s32[]{:S(2)}) async-start(), calls=%async_computation.14 | async-start | bytes 2621440 | tf_op jit(solution)/shard_map/all_gather | solution.py:65
  429.2 171.1 %all-gather.19.cloned.1.call-start = ((), (), s32[]{:S(2)}) async-start(), calls=%async_computation.11 | async-start | bytes 2621440 | tf_op jit(solution)/shard_map/all_gather | solution.py:65
  507.6 764.9 %copy-start.7 = (f32[512,512]{1,0:T(8,128)}, f32[512,512]{1,0:T(8,128)S(1)}, u32[]{:S(2)}) copy-start(f32[512,512]{1,0:T(8,128)S(1)} %get-tuple-element.651) | copy-start | bytes 3145732
  518.1 175.6 %reduce-scatter.14.cloned.1.call-start = ((), (), s32[]{:S(2)}) async-start(), calls=%async_computation.15 | async-start | bytes 14417920 | tf_op jit(solution)/shard_map/reduce_scatter | solution.py:83
  561.2 524.9 %all-reduce.7.cloned.1.call-start = ((), (), s32[]{:S(2)}) async-start(), calls=%async_computation.12 | async-start | bytes 46137344 | tf_op jit(solution)/shard_map/psum | solution.py:234
  621.3 552.7 %all-gather.23.cloned.1.call-start = ((), (), s32[]{:S(2)}) async-start(), calls=%async_computation.16 | async-start | bytes 14417920 | tf_op jit(solution)/shard_map/all_gather | solution.py:69
  1097.6 164.6 %reduce-scatter.16.cloned.1.call-start = ((), (), s32[]{:S(2)}) async-start(), calls=%async_computation.17 | async-start | bytes 5242880 | tf_op jit(solution)/shard_map/reduce_scatter | solution.py:89
  1185.2 136.0 %all-gather.25.cloned.1.call-start = ((), (), s32[]{:S(2)}) async-start(), calls=%async_computation.18 | async-start | bytes 2621440 | tf_op jit(solution)/shard_map/all_gather | solution.py:65
  1275.6 94.1 %reduce-scatter.18.cloned.1.call-start = ((), (), s32[]{:S(2)}) async-start(), calls=%async_computation.19 | async-start | bytes 5242880 | tf_op jit(solution)/shard_map/reduce_scatter | solution.py:83
  1326.2 316.0 %all-gather.27.cloned.1.call-start = ((), (), s32[]{:S(2)}) async-start(), calls=%async_computation.20 | async-start | bytes 10485760 | tf_op jit(solution)/shard_map/all_gather | solution.py:69
  1583.4 238.7 %all-reduce.9.cloned.1.call-start = ((), (), s32[]{:S(2)}) async-start(), calls=%async_computation.23 | async-start | bytes 13893632 | tf_op jit(solution)/shard_map/psum | solution.py:295
  1653.6 247.6 %reduce-scatter.20.cloned.1.call-start = ((), (), s32[]{:S(2)}) async-start(), calls=%async_computation.21 | async-start | bytes 5242880 | tf_op jit(solution)/shard_map/reduce_scatter | solution.py:89
  1665.0 316.7 %reduce-scatter.12.cloned.1.call-start = ((), (), s32[]{:S(2)}) async-start(), calls=%async_computation.13 | async-start | bytes 5242880 | tf_op jit(solution)/shard_map/reduce_scatter | solution.py:89
  1673.9 154.7 %copy-start.62 = (f32[2048]{0:T(1024)}, f32[2048]{0:T(1024)S(1)}, u32[]{:S(2)}) copy-start(f32[2048]{0:T(1024)S(1)} %dynamic_update_slice.41) | copy-start | bytes 24580
  1831.4 150.2 %copy-start.8 = (f32[512,512]{1,0:T(8,128)S(1)}, f32[512,512]{1,0:T(8,128)}, u32[]{:S(2)}) copy-start(f32[512,512]{1,0:T(8,128)} %copy-done.7) | copy-start | bytes 3145732
  1831.4 150.2 %copy-start.28 = (bf16[512,512]{1,0:T(8,128)(2,1)S(1)}, bf16[512,512]{1,0:T(8,128)(2,1)}, u32[]{:S(2)}) copy-start(bf16[512,512]{1,0:T(8,128)(2,1)} %param.29) | copy-start | bytes 1572868
  1831.5 150.2 %copy-start.57 = (f32[512]{0:T(512)S(1)}, f32[512]{0:T(512)}, u32[]{:S(2)}) copy-start(f32[512]{0:T(512)} %copy-done.56) | copy-start | bytes 6148
  (71 other events, 1127.5 us)
Sparse Core Ops, SparseCore 0:
  19.7 46.2 all-gather.14
  75.8 124.8 reduce-scatter.7
  334.3 16.7 all-gather.28
  401.0 22.5 all-gather.16
  428.7 76.7 reduce-scatter.9
  506.9 46.4 all-gather.20
  555.6 44.6 all-gather.18
  602.8 90.8 reduce-scatter.13
  696.3 389.7 all-reduce.6
  1097.7 76.2 all-gather.22
  1185.3 76.7 reduce-scatter.15
  1275.7 45.5 all-gather.24
  1326.4 43.2 reduce-scatter.17
  1583.5 58.6 all-gather.26
  1653.7 168.3 all-reduce.8
  1824.4 76.7 reduce-scatter.19
  1903.3 78.3 reduce-scatter.11
where the time goes:
time: 2000 us; the launch traced here: 1990 us
  waiting for transfers between devices  1290 us (64%)
  other arithmetic  272 us (14%)
  local copies, waits for them, and re-layouts  165 us (8%)
  matrix products  153 us (8%)
  blocking collectives  94 us (5%)
    psum x1, waiting for transfers between devices, shards(): both_all = lax.psum(local_both, 'row').reshape(span, 2, units_col)  392 us
    reduce_scatter x4, waiting for transfers between devices, sum_cols(): lax.psum_scatter(contract_term(left, right, contract), 'col', scatter_dim...  240 us
    reduce_scatter x3, waiting for transfers between devices, sum_rows(): lax.psum_scatter(contract_term(left, right, contract), 'row', scatter_dim...  232 us
    all_gather x4, waiting for transfers between devices, gather_cols(): return lax.all_gather(local, 'col', axis=0, tiled=True)  160 us
    psum x1, waiting for transfers between devices, shards(): lax.psum(grad_w_mix.astype(jnp.bfloat16), 'dp').astype(jnp.float32)  146 us
    all_gather x3, waiting for transfers between devices, gather_rows(): return lax.all_gather(local, 'row', axis=0, tiled=True)  120 us
    dot_general x7, matrix products, contract_term(): lax.dot_general(left, right, (((1,), (contract,)), ((), ())), preferred_e...  56.4 us
    psum x1, blocking collectives, shards(): lax.psum((full_mix, full_ffn, full_bound, group_part), ('dp', 'row', 'col'))  46.5 us
  transfers between devices with their start and end apart: 17, of which 16 were waited for; matrix products, arithmetic and copies ran while one was open for 8% of the time, Pallas kernels for 0%

commit v1 on v0

v1 whole, which is shorter than its diff:
```python
from functools import partial

import jax
import jax.numpy as jnp
from jax import lax
from jax.experimental import pallas as pl
from jax.experimental.pallas import tpu as pltpu
from jax.sharding import PartitionSpec as P

D = 2048
HD = 128
BLOCK = 64
norm_eps = 1e-06
bf16 = jnp.bfloat16
f32 = jnp.float32

CORE = [(0, 1), (1, 0), (2, 3), (3, 2)]
CHIP = [(0, 2), (2, 0), (1, 3), (3, 1)]
UP = [(0, 1), (1, 2), (2, 3), (3, 0)]
DOWN = [(1, 0), (2, 1), (3, 2), (0, 3)]


def swap_core(x):
    return lax.ppermute(x, "row", CORE)


def swap_chip(x):
    return lax.ppermute(x, "row", CHIP)


def tie(x, *others):
    return lax.optimization_barrier((x, *others))[0]


def mm(left, right):
    return lax.dot_general(left, right, (((1,), (0,)), ((), ())), preferred_element_type=f32)


def mm_nt(left, right):
    return lax.dot_general(left, right, (((1,), (1,)), ((), ())), preferred_element_type=f32)


def mm_tn(left, right):
    return lax.dot_general(left, right, (((0,), (0,)), ((), ())), preferred_element_type=f32)


def silu_slope(value, sigma):
    return sigma * (1.0 + value * (1.0 - sigma))


def split_mm(left, value):
    high = value.astype(bf16)
    low = (value - high.astype(f32)).astype(bf16)
    return mm(left, high) + mm(left, low)


def run_masks(i, idc_ref, idr_ref, prev_ref):
    s = slice(i * BLOCK, (i + 1) * BLOCK)
    idc = idc_ref[s, :]
    idr = idr_ref[0, :, s]
    prev = prev_ref[s, :]
    before = prev[0:1, :]
    last = idc[BLOCK - 1 : BLOCK, :]
    t = lax.broadcasted_iota(jnp.int32, (BLOCK, BLOCK), 0)
    u = lax.broadcasted_iota(jnp.int32, (BLOCK, BLOCK), 1)
    same = idc == idr
    heads = (idc == before).astype(f32)
    tails = (idc == last).astype(f32)
    through = (last == before).astype(f32)
    old = (idc == prev).astype(f32)
    return t, u, same, heads, tails, through, old


def run_decays(f_raw, lb, t, u):
    closed = jax.nn.sigmoid(-f_raw)
    keys = (1.0 - lb) * closed
    total = split_mm((t >= u).astype(bf16), jnp.log1p(-keys))
    middle = total[BLOCK // 2 - 1 : BLOCK // 2, :]
    final = total[BLOCK - 1 : BLOCK, :]
    return closed, keys, total, middle, final


def local_kernel(
    kq, rq, kf, rf, ki, ri, lb_ref, idc_ref, idr_ref, prev_ref,
    inner_ref, qh_ref, kh_ref, vb_ref, keep_ref, seg_ref, segd_ref,
):
    lb = lb_ref[...]
    state = jnp.zeros((HD, HD), f32)
    passing = jnp.ones((1, HD), f32)
    for i in range(kq.shape[0] // BLOCK):
        s = slice(i * BLOCK, (i + 1) * BLOCK)
        t, u, same, heads, tails, through, _ = run_masks(i, idc_ref, idr_ref, prev_ref)
        q_raw = kq[s, :] + rq[s, :].astype(f32)
        f_raw = kf[s, :] + rf[s, :].astype(f32)
        vb = (ki[s, :] + ri[s, :].astype(f32)).astype(bf16)
        q = q_raw * jax.nn.sigmoid(q_raw)
        _, keys, total, middle, final = run_decays(f_raw, lb, t, u)
        qt = (q * jnp.exp(total - middle)).astype(bf16)
        kt = (keys * jnp.exp(middle - total)).astype(bf16)
        scores = jnp.where(same & (t >= u), mm_nt(qt, kt), 0.0).astype(bf16)
        inner_ref[s, :] = mm(scores, vb)
        qh_ref[s, :] = (q * jnp.exp(total) * heads).astype(bf16)
        kh = (keys * jnp.exp(final - total) * tails).astype(bf16)
        kh_ref[s, :] = kh
        vb_ref[s, :] = vb
        keep = jnp.exp(final) * through
        keep_ref[0, 0, i : i + 1, :] = keep
        state = keep * state + mm_tn(vb, kh)
        passing = passing * keep
    seg_ref[0, 0] = state.astype(bf16)
    segd_ref[0, 0] = passing


def finish_kernel(
    y_ref, inner_ref, qh_ref, kh_ref, vb_ref, keep_ref, pseg_ref, psegd_ref, kg, rg, gain_ref,
    gated_ref, rec_ref, st_ref, state_ref,
):
    j = pl.program_id(1)
    y = y_ref[0]

    @pl.when(j == 0)
    def _():
        state_ref[...] = jnp.zeros_like(state_ref)

    @pl.when(y == 1)
    def _():
        state_ref[...] = psegd_ref[0, 0] * state_ref[...] + pseg_ref[0, 0].astype(f32)

    state = state_ref[...]
    for i in range(qh_ref.shape[0] // BLOCK):
        s = slice(i * BLOCK, (i + 1) * BLOCK)
        low = state.astype(bf16)
        st_ref[0, i] = low
        rec = inner_ref[s, :] + mm_nt(qh_ref[s, :], low)
        rec_ref[s, :] = rec
        scale = lax.rsqrt(jnp.mean(rec * rec, axis=1, keepdims=True) + norm_eps)
        g_raw = kg[s, :] + rg[s, :].astype(f32)
        gate = g_raw * jax.nn.sigmoid(g_raw)
        gated_ref[s, :] = (rec * scale * gain_ref[...] * gate).astype(bf16)
        state = keep_ref[0, 0, i : i + 1, :] * state + mm_tn(vb_ref[s, :], kh_ref[s, :])
    state_ref[...] = state

    @pl.when(y == 0)
    def _():
        state_ref[...] = psegd_ref[0, 0] * state_ref[...] + pseg_ref[0, 0].astype(f32)


def back_local_kernel(
    kd, rd, rec_ref, kg, rg, gain_ref, qh_ref, keep_ref,
    do_ref, dg_ref, group_ref, seg_ref,
):
    @pl.when((pl.program_id(0) == 0) & (pl.program_id(1) == 0))
    def _():
        group_ref[...] = jnp.zeros_like(group_ref)

    gain = gain_ref[...]
    adjoint = jnp.zeros((HD, HD), f32)
    group = jnp.zeros((1, HD), f32)
    for i in reversed(range(qh_ref.shape[0] // BLOCK)):
        s = slice(i * BLOCK, (i + 1) * BLOCK)
        grad = kd[s, :] + rd[s, :].astype(f32)
        rec = rec_ref[s, :]
        scale = lax.rsqrt(jnp.mean(rec * rec, axis=1, keepdims=True) + norm_eps)
        normed = rec * scale
        g_raw = kg[s, :] + rg[s, :].astype(f32)
        sigma = jax.nn.sigmoid(g_raw)
        act = g_raw * sigma
        both = grad * normed
        group = group + jnp.sum(both * act, axis=0, keepdims=True)
        dg_ref[s, :] = (both * gain * silu_slope(g_raw, sigma)).astype(bf16)
        dn = grad * gain * act
        do = (scale * (dn - normed * jnp.mean(dn * normed, axis=1, keepdims=True))).astype(bf16)
        do_ref[s, :] = do
        adjoint = keep_ref[0, 0, i : i + 1, :] * adjoint + mm_tn(do, qh_ref[s, :])
    group_ref[...] += group
    seg_ref[0, 0] = adjoint.astype(bf16)


def back_finish_kernel(
    y_ref, kq, rq, kf, rf, lb_ref, idc_ref, idr_ref, prev_ref,
    qh_ref, kh_ref, vb_ref, keep_ref, st_ref, do_ref, pseg_ref, psegd_ref,
    dq_ref, df_ref, dv_ref, bound_ref, adj_ref,
):
    j = pl.program_id(1)
    y = y_ref[0]

    @pl.when(j == 0)
    def _():
        adj_ref[...] = jnp.zeros_like(adj_ref)
        bound_ref[...] = jnp.zeros_like(bound_ref)

    @pl.when(y == 0)
    def _():
        adj_ref[...] = psegd_ref[0, 0] * adj_ref[...] + pseg_ref[0, 0].astype(f32)

    lb = lb_ref[...]
    adjoint = adj_ref[...]
    bound = jnp.zeros((1, HD), f32)
    for i in reversed(range(kq.shape[0] // BLOCK)):
        s = slice(i * BLOCK, (i + 1) * BLOCK)
        t, u, same, heads, tails, through, old = run_masks(i, idc_ref, idr_ref, prev_ref)
        causal = same & (t >= u)
        q_raw = kq[s, :] + rq[s, :].astype(f32)
        f_raw = kf[s, :] + rf[s, :].astype(f32)
        sigma = jax.nn.sigmoid(q_raw)
        q = q_raw * sigma
        closed, keys, total, middle, final = run_decays(f_raw, lb, t, u)
        out = jnp.exp(total - middle)
        back = jnp.exp(middle - total)
        qt = (q * out).astype(bf16)
        kt = (keys * back).astype(bf16)
        scores = jnp.where(causal, mm_nt(qt, kt), 0.0).astype(bf16)
        vb = vb_ref[s, :]
        kh = kh_ref[s, :]
        qh = qh_ref[s, :]
        do = do_ref[s, :]
        st = st_ref[0, i]
        low = adjoint.astype(bf16)
        keep = keep_ref[0, 0, i : i + 1, :]
        ds = jnp.where(causal, mm_nt(do, vb), 0.0).astype(bf16)
        dq = mm(ds, kt) * out + mm(do, st) * (jnp.exp(total) * heads)
        dkh = mm(vb, low)
        dk = mm_tn(ds, qt) * back + dkh * (jnp.exp(final - total) * tails)
        dv_ref[s, :] = (mm_tn(scores, do) + mm_nt(kh, low)).astype(bf16)
        ends = keep * jnp.sum(adjoint * st.astype(f32), axis=0, keepdims=True) + jnp.sum(
            kh.astype(f32) * dkh, axis=0, keepdims=True
        )
        later = (same & (u >= t)).astype(bf16)
        dlog = split_mm(later, q * dq - keys * dk) + tails * ends
        key_total = dk - old * dlog / (1.0 - keys)
        bound = bound - jnp.sum(key_total * closed, axis=0, keepdims=True)
        df_ref[s, :] = (-key_total * keys * (1.0 - closed)).astype(bf16)
        dq_ref[s, :] = (dq * silu_slope(q_raw, sigma)).astype(bf16)
        adjoint = keep * adjoint + mm_tn(do, qh)
    bound_ref[...] += bound
    adj_ref[...] = adjoint

    @pl.when(y == 1)
    def _():
        adj_ref[...] = psegd_ref[0, 0] * adj_ref[...] + pseg_ref[0, 0].astype(f32)


def shape(dims, kind):
    return jax.ShapeDtypeStruct(dims, kind)


def cost(flops, moved):
    return pl.CostEstimate(flops=flops, bytes_accessed=moved, transcendentals=0)


def column(run, heads, part, turn):
    return pl.BlockSpec((run, HD), lambda h, j: (turn(j), part * heads + h))


def forward_turn(j):
    return j


def recurrence_local(keep, recv, bound, ids):
    idc, idr, prev = ids
    runs, _, run = idr.shape
    heads = keep.shape[1] // (4 * HD)
    chunks = run // BLOCK
    tokens = runs * run
    col = partial(column, run, heads, turn=forward_turn)
    one = pl.BlockSpec((run, 1), lambda h, j: (j, 0))
    seg = lambda *dims: pl.BlockSpec((1, 1, *dims), lambda h, j: (h, j, 0, 0))
    return pl.pallas_call(
        local_kernel,
        grid=(heads, runs),
        in_specs=[
            col(part=0), col(part=0), col(part=1), col(part=1), col(part=2), col(part=2),
            pl.BlockSpec((1, HD), lambda h, j: (0, h)),
            one,
            pl.BlockSpec((1, 1, run), lambda h, j: (j, 0, 0)),
            one,
        ],
        out_specs=[col(part=0)] * 4 + [seg(chunks, HD), seg(HD, HD), seg(1, HD)],
        out_shape=[
            shape((tokens, heads * HD), f32),
            shape((tokens, heads * HD), bf16),
            shape((tokens, heads * HD), bf16),
            shape((tokens, heads * HD), bf16),
            shape((heads, runs, chunks, HD), f32),
            shape((heads, runs, HD, HD), bf16),
            shape((heads, runs, 1, HD), f32),
        ],
        cost_estimate=cost(int(4e9), int(2e7)),
        name="recurrence_local",
    )(keep, recv, keep, recv, keep, recv, bound, idc, idr, prev)


def recurrence_finish(y, local, peer, keep, recv, gain):
    inner, qh, kh, vb, decay = local
    heads, runs, chunks, _ = decay.shape
    run = chunks * BLOCK
    tokens = runs * run
    col = partial(column, run, heads, turn=forward_turn)
    seg = lambda *dims: pl.BlockSpec((1, 1, *dims), lambda h, j: (h, j, 0, 0))
    return pl.pallas_call(
        finish_kernel,
        grid=(heads, runs),
        in_specs=[
            pl.BlockSpec(memory_space=pltpu.SMEM),
            col(part=0), col(part=0), col(part=0), col(part=0),
            seg(chunks, HD), seg(HD, HD), seg(1, HD),
            col(part=3), col(part=3),
            pl.BlockSpec((1, HD), lambda h, j: (0, 0)),
        ],
        out_specs=[
            col(part=0), col(part=0),
            pl.BlockSpec((1, chunks, HD, HD), lambda h, j: (h, j, 0, 0)),
        ],
        out_shape=[
            shape((tokens, heads * HD), bf16),
            shape((tokens, heads * HD), f32),
            shape((heads, runs * chunks, HD, HD), bf16),
        ],
        scratch_shapes=[pltpu.VMEM((HD, HD), f32)],
        cost_estimate=cost(int(3e9), int(1e7)),
        name="recurrence_finish",
    )(y, inner, qh, kh, vb, decay, *peer, keep, recv, gain)


def recurrence_back_local(kd, rd, rec, keep, recv, gain, qh, decay):
    heads, runs, chunks, _ = decay.shape
    run = chunks * BLOCK
    tokens = runs * run
    col = partial(column, run, heads, turn=forward_turn)
    seg = lambda *dims: pl.BlockSpec((1, 1, *dims), lambda h, j: (h, j, 0, 0))
    return pl.pallas_call(
        back_local_kernel,
        grid=(heads, runs),
        in_specs=[
            col(part=0), col(part=0), col(part=0), col(part=3), col(part=3),
            pl.BlockSpec((1, HD), lambda h, j: (0, 0)),
            col(part=0), seg(chunks, HD),
        ],
        out_specs=[
            col(part=0), col(part=0),
            pl.BlockSpec((1, HD), lambda h, j: (0, 0)),
            seg(HD, HD),
        ],
        out_shape=[
            shape((tokens, heads * HD), bf16),
            shape((tokens, heads * HD), bf16),
            shape((1, HD), f32),
            shape((heads, runs, HD, HD), bf16),
        ],
        cost_estimate=cost(int(3e9), int(1e7)),
        name="recurrence_back_local",
    )(kd, rd, rec, keep, recv, gain, qh, decay)


def recurrence_back_finish(y, keep, recv, bound, ids, local, states, do, peer):
    idc, idr, prev = ids
    _, qh, kh, vb, decay = local
    heads, runs, chunks, _ = decay.shape
    run = chunks * BLOCK
    tokens = runs * run
    turn = lambda j: runs - 1 - j
    col = partial(column, run, heads, turn=turn)
    one = pl.BlockSpec((run, 1), lambda h, j: (turn(j), 0))
    seg = lambda *dims: pl.BlockSpec((1, 1, *dims), lambda h, j: (h, turn(j), 0, 0))
    return pl.pallas_call(
        back_finish_kernel,
        grid=(heads, runs),
        in_specs=[
            pl.BlockSpec(memory_space=pltpu.SMEM),
            col(part=0), col(part=0), col(part=1), col(part=1),
            pl.BlockSpec((1, HD), lambda h, j: (0, h)),
            one,
            pl.BlockSpec((1, 1, run), lambda h, j: (turn(j), 0, 0)),
            one,
            col(part=0), col(part=0), col(part=0),
            seg(chunks, HD),
            pl.BlockSpec((1, chunks, HD, HD), lambda h, j: (h, turn(j), 0, 0)),
            col(part=0),
            seg(HD, HD), seg(1, HD),
        ],
        out_specs=[
            col(part=0), col(part=0), col(part=0),
            pl.BlockSpec((1, HD), lambda h, j: (0, h)),
        ],
        out_shape=[
            shape((tokens, heads * HD), bf16),
            shape((tokens, heads * HD), bf16),
            shape((tokens, heads * HD), bf16),
            shape((1, heads * HD), f32),
        ],
        scratch_shapes=[pltpu.VMEM((HD, HD), f32)],
        cost_estimate=cost(int(8e9), int(2e7)),
        name="recurrence_back_finish",
    )(y, keep, recv, keep, recv, bound, idc, idr, prev, qh, kh, vb, decay, states, do, *peer)


def gather_pair(own, other, z):
    count = lax.axis_size("col")
    rows, width = own.shape

    def put(whole, part, at):
        return lax.dynamic_update_slice(whole, part[None], (at % count, 0, 0))

    first = put(jnp.zeros((count, rows, width), own.dtype), own, z)
    second = put(jnp.zeros((count, rows, width), other.dtype), other, z)
    for k in range(1, count):
        own = lax.ppermute(own, "col", UP)
        other = lax.ppermute(other, "col", DOWN)
        first = put(first, own, z - k + count)
        second = put(second, other, z + k)
    return first.reshape(count * rows, width), second.reshape(count * rows, width)


def scatter_pair(own, other, z, offset):
    count = lax.axis_size("col")
    own = own.reshape(count, -1, own.shape[1])
    other = other.reshape(count, -1, other.shape[1])

    def block(whole, at):
        return lax.dynamic_index_in_dim(whole, (at + offset) % count, 0, keepdims=False)

    first = block(own, z - 1 + count)
    second = block(other, z + 1)
    for k in range(2, count + 1):
        moved = lax.ppermute(first.astype(bf16), "col", UP)
        first = moved.astype(f32) + block(own, z - k + count)
        moved = lax.ppermute(second.astype(bf16), "col", DOWN)
        second = moved.astype(f32) + block(other, z + k)
    return first, second


def sum_over(value, axis):
    count = lax.axis_size(axis)
    if count == 2:
        return value + lax.ppermute(value, axis, [(0, 1), (1, 0)])
    if count == 4:
        value = value + lax.ppermute(value, axis, [(0, 1), (1, 0), (2, 3), (3, 2)])
        return value + lax.ppermute(value, axis, [(0, 2), (2, 0), (1, 3), (3, 1)])
    return lax.psum(value, axis)


def sum_groups(grad):
    sent = grad.astype(bf16)
    if lax.axis_size("dp") == 2:
        return sent.astype(f32) + lax.ppermute(sent, "dp", [(0, 1), (1, 0)]).astype(f32)
    return lax.psum(sent, "dp").astype(f32)


def weight_grad(left_own, left_other, right):
    sent = swap_chip(mm_tn(left_other, right).astype(bf16))
    return sum_groups(mm_tn(left_own, right) + sent.astype(f32))


def shards(
    tokens,
    segments,
    mix_gain,
    w_mix,
    lower_bound,
    group_gain,
    w_out,
    ffn_gain,
    w_ffn_in,
    w_down,
    cotangent,
):
    row = lax.axis_index("row")
    core = row % 2
    y = row // 2
    z = lax.axis_index("col")
    count = lax.axis_size("col")
    span = segments.shape[0]
    half = tokens.shape[0] // 2
    width = tokens.shape[1]
    cols = w_mix.shape[2]
    hc = cols // 2
    units_col = w_down.shape[0]
    here = count * half
    hb = here // 2

    def mine(x, at, size, axis):
        return lax.dynamic_slice_in_dim(x, at * size, size, axis)

    def joined(first_if_zero, second_if_zero, flag, axis):
        return jnp.where(
            flag == 0,
            jnp.concatenate([first_if_zero, second_if_zero], axis),
            jnp.concatenate([second_if_zero, first_if_zero], axis),
        )

    tok_own = mine(tokens, y, half, 0)
    tok_other = swap_chip(mine(tokens, 1 - y, half, 0))
    x_own, x_other = gather_pair(tok_own, tok_other, z)

    gains = jnp.stack([mix_gain, ffn_gain])
    gains_other = swap_chip(gains)
    wm_keep = mine(w_mix, core, hc, 2).reshape(width, 4 * hc)
    wm_send = mine(w_mix, 1 - core, hc, 2).reshape(width, 4 * hc)
    wm_send_o = swap_chip(wm_send)
    wm_keep_o = swap_chip(wm_keep)
    wo_keep = mine(w_out, core, hc, 0)
    wo_send = mine(w_out, 1 - core, hc, 0)
    wo = tie(jnp.concatenate([wo_keep, wo_send], 0), wm_keep_o, wm_send_o)
    wo_o = swap_chip(wo)
    wo_keep_o, wo_send_o = wo_o[:hc], wo_o[hc:]
    wf = w_ffn_in.reshape(width, 2 * units_col)
    wf_o = swap_chip(tie(wf, wo_o))
    wd = w_down
    wd_o = swap_chip(tie(wd, wf_o))

    ids = segments.astype(f32)
    before = jnp.concatenate([jnp.full((1,), -1.0, f32), ids[:-1]])
    pick = lambda a: lax.dynamic_index_in_dim(a.reshape(count, 2, half), y, 1, keepdims=False)
    ids, before = pick(ids), pick(before)
    ids = (ids.reshape(here, 1), ids.reshape(count, 1, half), before.reshape(here, 1))

    xo = x_own.astype(f32)
    xp = x_other.astype(f32)
    squares = jnp.sum(xo * xo, axis=1) + jnp.sum(xp * xp, axis=1)
    squares = squares + swap_core(squares)
    mix_scale = lax.rsqrt(squares / D + norm_eps)[:, None]
    m_own = (xo * mix_scale * mix_gain).astype(bf16)
    m_other = (xp * mix_scale * gains_other[0]).astype(bf16)

    send = (mm(m_own, wm_send) + mm(m_other, wm_send_o)).astype(bf16)
    recv = swap_core(send)
    keep = mm(m_own, wm_keep) + mm(m_other, wm_keep_o)

    cot = tie(cotangent, m_own)
    cot_own = mine(cot, y, half, 0)
    cot_other = swap_chip(mine(cot, 1 - y, half, 0))
    c_own, c_other = gather_pair(cot_own, cot_other, z)

    y_here = y.astype(jnp.int32).reshape(1)
    bound = mine(lower_bound, core, hc, 0).reshape(1, hc)
    gain_row = group_gain.reshape(1, HD)
    *local, seg_state, seg_decay = recurrence_local(keep, recv, bound, ids)
    peer_state = swap_chip(seg_state)
    peer_decay = swap_chip(seg_decay)
    gated, rec, states = recurrence_finish(
        y_here, local, (peer_state, peer_decay), keep, recv, gain_row
    )
    gated_p = swap_core(gated)
    gated_all = jnp.concatenate([gated, gated_p], 1)
    mixed_own, mixed_other = scatter_pair(mm(gated_all, wo), mm(gated_all, wo_o), z, 0)
    h_own = tok_own.astype(f32) + mixed_own
    h_other = tok_other.astype(f32) + mixed_other

    squares = jnp.sum(h_own * h_own, axis=1) + jnp.sum(h_other * h_other, axis=1)
    squares = squares + swap_core(squares)
    ffn_scale = lax.rsqrt(squares / D + norm_eps)[:, None]
    n_own = (h_own * ffn_scale * ffn_gain).astype(bf16)
    n_other = (h_other * ffn_scale * gains_other[1]).astype(bf16)
    f_own, f_other = gather_pair(n_own, n_other, z)

    def rows(x, at):
        return mine(x, at, hb, 0)

    gu_send = (mm_nt(rows(c_own, 1 - core), wd) + mm_nt(rows(c_other, 1 - core), wd_o)).astype(bf16)
    gu_recv = swap_core(gu_send)
    gu = mm_nt(rows(c_own, core), wd) + mm_nt(rows(c_other, core), wd_o) + gu_recv.astype(f32)

    fk_own, fs_own = rows(f_own, core), rows(f_own, 1 - core)
    fk_other, fs_other = rows(f_other, core), rows(f_other, 1 - core)
    b_send = (mm(fs_own, wf) + mm(fs_other, wf_o)).astype(bf16)
    b_recv = swap_core(b_send)
    both = mm(fk_own, wf) + mm(fk_other, wf_o) + b_recv.astype(f32)
    gate, up = both[:, :units_col], both[:, units_col:]
    sigma = jax.nn.sigmoid(gate)
    act = gate * sigma
    units = (act * up).astype(bf16)
    grad_both = jnp.concatenate(
        [(gu * up * silu_slope(gate, sigma)).astype(bf16), (gu * act).astype(bf16)], 1
    )
    grad_both_p = swap_core(grad_both)
    gb = jnp.concatenate([grad_both, grad_both_p], 0)
    units_p = swap_core(tie(units, grad_both_p))
    un = jnp.concatenate([units, units_p], 0)
    shift = 2 * core

    df_own, df_other = scatter_pair(mm_nt(gb, wf), mm_nt(gb, wf_o), z, shift)

    gain_f, gain_fo = ffn_gain, gains_other[1]
    w_o, w_p = df_own * gain_f, df_other * gain_fo
    along = jnp.sum(w_o * h_own, axis=1) + jnp.sum(w_p * h_other, axis=1)
    along = along + swap_core(along)
    factor = ffn_scale**3 * along[:, None] / D
    cot_f_own = cot_own.astype(f32)
    cot_f_other = cot_other.astype(f32)
    gh_own = cot_f_own + ffn_scale * w_o - h_own * factor
    gh_other = cot_f_other + ffn_scale * w_p - h_other * factor
    ffn_part = jnp.sum(df_own * h_own * ffn_scale, axis=0)
    ffn_part_o = jnp.sum(df_other * h_other * ffn_scale, axis=0)
    g_own, g_other = gather_pair(gh_own.astype(bf16), gh_other.astype(bf16), z)

    gg_send = (mm_nt(g_own, wo_send) + mm_nt(g_other, wo_send_o)).astype(bf16)
    gg_recv = swap_core(gg_send)
    gg_keep = mm_nt(g_own, wo_keep) + mm_nt(g_other, wo_keep_o)
    do, d_gate, group_part, adj = recurrence_back_local(
        gg_keep, gg_recv, rec, keep, recv, gain_row, local[1], local[4]
    )
    peer_adj = swap_chip(adj)
    d_gate_p = swap_core(d_gate)
    d_query, d_forget, d_input, bound_part = recurrence_back_finish(
        y_here, keep, recv, bound, ids, local, states, do, (peer_adj, peer_decay)
    )
    d_three = jnp.concatenate([d_query, d_forget, d_input], 1)
    d_three_p = swap_core(d_three)
    dp_keep = jnp.concatenate([d_three, d_gate], 1)
    dp_send = jnp.concatenate([d_three_p, d_gate_p], 1)
    dx_own, dx_other = scatter_pair(
        mm_nt(dp_keep, wm_keep) + mm_nt(dp_send, wm_send),
        mm_nt(dp_keep, wm_keep_o) + mm_nt(dp_send, wm_send_o),
        z,
        0,
    )

    un = tie(un, g_own, g_other)
    out_own, out_other = scatter_pair(mm(un, wd), mm(un, wd_o), z, shift)
    out_own = (h_own + out_own).astype(bf16)
    out_other = (h_other + out_other).astype(bf16)
    output = joined(out_own, swap_chip(out_other), y, 0)

    ck = jnp.concatenate([rows(c_own, core), rows(c_own, 1 - core)], 0)
    ck_o = jnp.concatenate([rows(c_other, core), rows(c_other, 1 - core)], 0)
    sent = swap_chip(mm_tn(un, ck_o).astype(bf16))
    grad_w_down = sum_groups(mm_tn(un, ck) + sent.astype(f32))
    grad_w_ffn = weight_grad(
        jnp.concatenate([fk_own, fs_own], 0), jnp.concatenate([fk_other, fs_other], 0), gb
    ).reshape(width, 2, units_col)
    sent = swap_chip(mm_tn(gated_all, g_other).astype(bf16))
    grad_wo = sum_groups(mm_tn(gated_all, g_own) + sent.astype(f32))
    grad_w_out = joined(grad_wo[:hc], grad_wo[hc:], core, 0)
    gm_keep = weight_grad(m_own, m_other, dp_keep).reshape(width, 4, hc)
    gm_send = weight_grad(m_own, m_other, dp_send).reshape(width, 4, hc)
    grad_w_mix = joined(gm_keep, gm_send, core, 2)

    scale = lax.dynamic_slice_in_dim(mix_scale, z * half, half, 0)
    t_own, t_other = tok_own.astype(f32), tok_other.astype(f32)
    w_o, w_p = dx_own * mix_gain, dx_other * gains_other[0]
    along = jnp.sum(w_o * t_own, axis=1) + jnp.sum(w_p * t_other, axis=1)
    along = along + swap_core(along)
    factor = scale**3 * along[:, None] / D
    gt_own = gh_own + scale * w_o - t_own * factor
    gt_other = gh_other + scale * w_p - t_other * factor
    mix_part = jnp.sum(dx_own * t_own * scale, axis=0)
    mix_part_o = jnp.sum(dx_other * t_other * scale, axis=0)
    grad_tokens = joined(gt_own, swap_chip(gt_other), y, 0)

    small = jnp.stack([mix_part, ffn_part])
    small_o = jnp.stack([mix_part_o, ffn_part_o])
    small = small + swap_chip(small_o)
    small = sum_over(sum_over(small, "col"), "dp")
    bound_part = bound_part[0]
    bound_part = bound_part + swap_chip(bound_part)
    bound_part = sum_over(bound_part, "dp")
    bound_p = swap_core(bound_part)
    grad_bound = joined(bound_part, bound_p, core, 0)
    group = group_part[0]
    group = group + swap_core(group)
    group = group + swap_chip(group)
    group = sum_over(sum_over(group, "col"), "dp")
    return (
        output,
        grad_tokens,
        small[0],
        grad_w_mix,
        grad_bound,
        group,
        grad_w_out,
        small[1],
        grad_w_ffn,
        grad_w_down,
    )


def solution(mesh):
    return jax.shard_map(
        shards,
        mesh=mesh,
        in_specs=(
            P(("dp", "col"), "row"),
            P("dp"),
            P("row"),
            P("row", None, "col"),
            P("col"),
            P(),
            P("col", "row"),
            P("row"),
            P("row", None, "col"),
            P("col", "row"),
            P(("dp", "col"), "row"),
        ),
        out_specs=(
            P(("dp", "col"), "row"),
            P(("dp", "col"), "row"),
            P("row"),
            P("row", None, "col"),
            P("col"),
            P(),
            P("col", "row"),
            P("row"),
            P("row", None, "col"),
            P("col", "row"),
        ),
        check_vma=False,
    )
```

time: 2000 us -> 727 us (0.36)
  waiting for transfers between devices: 1290 us -> 331 us
  other arithmetic: 272 us -> 57.9 us
  starting transfers between devices: 1.81 us -> 135 us
  local copies, waits for them, and re-layouts: 165 us -> 50.5 us
  blocking collectives: 94 us -> 0 us
  matrix products: 153 us -> 89.5 us
  Pallas kernels: 0 us -> 50 us
    psum x2 -> x0, waiting for transfers between devices: 539 us -> none  [the longest x1 392 us: shards(): both_all = lax.psum(local_both, 'row').reshape(span, 2, units_col)]
    reduce_scatter x7 -> x0, waiting for transfers between devices: 471 us -> none  [the longest x4 240 us: sum_cols(): lax.psum_scatter(contract_term(left, right, contract), 'col', scatter_dim...]
    ppermute x0 -> x96, waiting for transfers between devices: none -> 331 us  [the longest x21 143 us: swap_chip(): return lax.ppermute(x, 'row', CHIP)]
    all_gather x8 -> x0, waiting for transfers between devices: 279 us -> none  [the longest x4 160 us: gather_cols(): return lax.all_gather(local, 'col', axis=0, tiled=True)]
    ppermute x0 -> x96, starting transfers between devices: none -> 135 us  [the longest x12 39.2 us: scatter_pair(): moved = lax.ppermute(second.astype(bf16), 'col', DOWN)]
    psum x5 -> x0, blocking collectives: 76.4 us -> none  [the longest x1 46.5 us: shards(): lax.psum((full_mix, full_ffn, full_bound, group_part), ('dp', 'row', 'col'))]
    dot_general x24 -> x36, matrix products: 153 us -> 89.5 us  [the longest x12 32.9 us: mm(): lax.dot_general(left, right, (((1,), (0,)), ((), ())), preferred_element_...]
    reduce_sum x25 -> x6, other arithmetic: 55.2 us -> 3.98 us  [the longest x1 1.57 us: shards(): ffn_part = jnp.sum(df_own * h_own * ffn_scale, axis=0)]
  transfers between devices with their start and end apart: 17 -> 96, of which waited for: 16 -> 50; matrix products, arithmetic and copies ran while one was open for 8% -> 23% of each run, Pallas kernels for 0% -> 4%
where the time goes in v1:
time: 727 us; the launch traced here: 716 us
  waiting for transfers between devices  331 us (46%)
  starting transfers between devices  135 us (19%)
  matrix products  89.5 us (12%)
  other arithmetic  57.9 us (8%)
  local copies, waits for them, and re-layouts  50.5 us (7%)
  Pallas kernels  50 us (7%)
    ppermute x21, waiting for transfers between devices, swap_chip(): return lax.ppermute(x, 'row', CHIP)  143 us
    ppermute x5, waiting for transfers between devices, sum_groups(): lax.ppermute(sent, 'dp', [(0, 1), (1, 0)]).astype(f32)  67.8 us
    ppermute x12, waiting for transfers between devices, gather_pair(): other = lax.ppermute(other, 'col', DOWN)  51.8 us
    ppermute x12, starting transfers between devices, scatter_pair(): moved = lax.ppermute(second.astype(bf16), 'col', DOWN)  39.2 us
    dot_general x12, matrix products, mm(): lax.dot_general(left, right, (((1,), (0,)), ((), ())), preferred_element_...  32.9 us
    ppermute x12, starting transfers between devices, gather_pair(): other = lax.ppermute(other, 'col', DOWN)  29.8 us
    dot_general x14, matrix products, mm_nt(): lax.dot_general(left, right, (((1,), (1,)), ((), ())), preferred_element_...  28.7 us
    ppermute x21, starting transfers between devices, swap_chip(): return lax.ppermute(x, 'row', CHIP)  28.5 us
  transfers between devices with their start and end apart: 96, of which 50 were waited for; matrix products, arithmetic and copies ran while one was open for 23% of the time, Pallas kernels for 4%

profile of v1, /device:TPU:0, one launch (start us, length us, event | category | flops | bytes accessed | tf_op | source)
XLA Modules:
  0.0 716.1 jit_solution(3391938268265542518)
XLA Ops:
  16.4 6.2 collective-permute-done.4
  64.1 19.2 %collective-permute-done.9 = bf16[512,1024]{1,0:T(8,128)(2,1)} collective-permute-done((bf16[512,1024]{1,0:T(8,128)(2,1)}, bf16[512,1024]{1,0:T(8,128)(2,1)}, u32[]{:S(2)}, u32[]{:S(2)}) %collective-permute-start.9) | collective-permute-done | bytes 1048608 | tf_op jit(solution)/shard_map/ppermute | solution.py:28
  89.2 15.6 %recurrence_local.1 = (f32[1024,256]{1,0:T(8,128)}, bf16[1024,256]{1,0:T(8,128)(2,1)}, bf16[1024,256]{1,0:T(8,128)(2,1)}, bf16[1024,256]{1,0:T(8,128)(2,1)}, f32...) custom-call(f32[1024,1024]{1,0:T(8,128)} %convolution_add_fusion.2.kq.kf.ki.kg, ...), custom_call_target="tpu_custom_call" | custom-call | flops 4000000000 | bytes 20000000 | tf_op jit(solution)/shard_map/recurrence_local/pallas_call | solution.py:268
  106.9 6.2 collective-permute-done.13.psegd_ref
  113.8 8.6 %recurrence_finish.1 = (bf16[1024,256]{1,0:T(8,128)(2,1)}, f32[1024,256]{1,0:T(8,128)}, bf16[2,16,128,128]{3,2,1,0:T(8,128)(2,1)}) custom-call(s32[1]{0:T(128)} %bitcast.y_ref, f32[1024,256]{1,0:T(8,128)} %get-tuple-element.34.inner_ref, bf16[1024,256]{1,0:T(8,128)(2,1)} %get-tuple-element.35.qh_ref, bf16[1024,256]{1,0:T(8,128)(2,1)} %get-tuple-element.36.kh_ref, ...), custom_call_target="tpu_custom_call" | custom-call | flops 3000000000 | bytes 10000000 | tf_op jit(solution)/shard_map/recurrence_finish/pallas_call | solution.py:300
  127.9 9.0 %collective-permute-done.18 = bf16[512,512]{1,0:T(8,128)(2,1)S(1)} collective-permute-done((bf16[512,512]{1,0:T(8,128)(2,1)S(1)}, bf16[512,512]{1,0:T(8,128)(2,1)S(1)}, u32[]{:S(2)}, u32[]{:S(2)}) %collective-permute-start.18) | collective-permute-done | bytes 524320 | tf_op jit(solution)/shard_map/ppermute | solution.py:28
  166.1 47.7 %collective-permute-done.34 = bf16[256,512]{1,0:T(8,128)(2,1)S(1)} collective-permute-done((bf16[256,512]{1,0:T(8,128)(2,1)S(1)}, bf16[256,512]{1,0:T(8,128)(2,1)S(1)}, u32[]{:S(2)}, u32[]{:S(2)}) %collective-permute-start.34) | collective-permute-done | bytes 262176 | tf_op jit(solution)/shard_map/ppermute | solution.py:28
  238.0 16.3 %collective-permute-done.27 = bf16[256,512]{1,0:T(8,128)(2,1)S(1)} collective-permute-done((bf16[256,512]{1,0:T(8,128)(2,1)S(1)}, bf16[256,512]{1,0:T(8,128)(2,1)S(1)}, u32[]{:S(2)}, u32[]{:S(2)}) %collective-permute-start.27) | collective-permute-done | bytes 262176 | tf_op jit(solution)/shard_map/ppermute | solution.py:408
  260.5 5.5 collective-permute-done.28
  281.2 6.7 collective-permute-done.37
  303.9 7.4 %reshape.184 = bf16[512,2816,1]{1,0,2:T(8,128)(2,1)} reshape(bf16[512,2,1408]{2,1,0:T(2,128)(2,1)} %param.19) | data formatting | bytes 5767168 | tf_op jit(solution)/shard_map/reshape | solution.py:506
  317.8 5.5 fusion.84
  381.2 7.2 %collective-permute-done.50 = bf16[256,512]{1,0:T(8,128)(2,1)S(1)} collective-permute-done((bf16[256,512]{1,0:T(8,128)(2,1)S(1)}, bf16[256,512]{1,0:T(8,128)(2,1)S(1)}, u32[]{:S(2)}, u32[]{:S(2)}) %collective-permute-start.50) | collective-permute-done | bytes 262176 | tf_op jit(solution)/shard_map/ppermute | solution.py:407
  421.5 7.3 %recurrence_back_local.1 = (bf16[1024,256]{1,0:T(8,128)(2,1)}, bf16[1024,256]{1,0:T(8,128)(2,1)}, f32[1,128]{1,0:T(1,128)}, bf16[2,4,128,128]{3,2,1,0:T(8,128)(2,1)}) custom-call(f32[1024,256]{1,0:T(8,128)} %convolution_add_fusion.7.kd, bf16[1024,256]{1,0:T(8,128)(2,1)} %copy-done.84, f32[1024,256]{1,0:T(8,128)} %get-tuple-element.49.rec_ref, ...), custom_call_target="tpu_custom_call" | custom-call | flops 3000000000 | bytes 10000000 | tf_op jit(solution)/shard_map/recurrence_back_local/pallas_call | solution.py:331
  437.9 42.9 %collective-permute-done.86 = f32[128]{0:T(128)S(1)} collective-permute-done((f32[128]{0:T(128)S(1)}, f32[128]{0:T(128)S(1)}, u32[]{:S(2)}, u32[]{:S(2)}) %collective-permute-start.86) | collective-permute-done | bytes 544 | tf_op jit(solution)/shard_map/ppermute | solution.py:28
  501.2 18.6 %recurrence_back_finish.1 = (bf16[1024,256]{1,0:T(8,128)(2,1)}, bf16[1024,256]{1,0:T(8,128)(2,1)}, bf16[1024,256]{1,0:T(8,128)(2,1)}, f32[1,256]{1,0:T(1,128)}) custom-call(s32[1]{0:T(128)} %bitcast.y_ref, f32[1024,1024]{1,0:T(8,128)} %convolution_add_fusion.2.kq.kf.ki.kg, bf16[1024,1024]{1,0:T(8,128)(2,1)} %copy-done, ...), custom_call_target="tpu_custom_call" | custom-call | flops 8000000000 | bytes 20000000 | tf_op jit(solution)/shard_map/recurrence_back_finish/pallas_call | solution.py:365
  534.4 6.0 collective-permute-done.61
  544.4 5.9 add_convert_fusion
  597.4 49.4 %collective-permute-done.95 = bf16[1408,512]{1,0:T(8,128)(2,1)S(1)} collective-permute-done((bf16[1408,512]{1,0:T(8,128)(2,1)S(1)}, bf16[1408,512]{1,0:T(8,128)(2,1)S(1)}, u32[]{:S(2)}, u32[]{:S(2)}) %collective-permute-start.95) | collective-permute-done | bytes 1441824 | tf_op jit(solution)/shard_map/ppermute | solution.py:445
  650.2 17.2 %collective-permute-done.79 = bf16[512,1024]{1,0:T(8,128)(2,1)S(1)} collective-permute-done((bf16[512,1024]{1,0:T(8,128)(2,1)S(1)}, bf16[512,1024]{1,0:T(8,128)(2,1)S(1)}, u32[]{:S(2)}, u32[]{:S(2)}) %collective-permute-start.79) | collective-permute-done | bytes 1048608 | tf_op jit(solution)/shard_map/ppermute | solution.py:445
  683.2 6.7 collective-permute-done.73
  690.9 5.7 convert_add_fusion
  696.7 7.8 %reshape.181 = f32[512,2,1408]{2,1,0:T(2,128)} reshape(f32[512,2816]{1,0:T(8,128)} %convert_add_fusion) | data formatting | bytes 11534336 | tf_op jit(solution)/shard_map/reshape | solution.py:630
  709.3 6.4 maximum_select_fusion
  (537 shorter events, 378.2 us)
Async XLA Ops:
  14.8 31.5 %collective-permute-start.8 = (f32[2,512]{1,0:T(2,128)S(1)}, f32[2,512]{1,0:T(2,128)S(1)}, u32[]{:S(2)}, u32[]{:S(2)}) collective-permute-start(f32[2,512]{1,0:T(2,128)S(1)} %pad_maximum_fusion.6), channel_id=1, source_target_pairs={{0,8},{8,0},{4,12},{12,4},{1,9},{9,1},{5,13},{13,5},{2,10},{10,2},... | collective-permute-start | bytes 12296 | tf_op jit(solution)/shard_map/ppermute | solution.py:28
  56.2 31.6 %collective-permute-start.11 = (bf16[1024,1024]{1,0:T(8,128)(2,1)}, bf16[1024,1024]{1,0:T(8,128)(2,1)S(1)}, u32[]{:S(2)}, u32[]{:S(2)}) collective-permute-start(bf16[1024,1024]{1,0:T(8,128)(2,1)} %add_convert_fusion.2), channel_id=1, source_target_pairs={{0,4},{4,0},{8,12},{12,8},{1,5},{5,1},{9,13},{13,9},{2,6},{6,2},{1... | collective-permute-start | bytes 6291464 | tf_op jit(solution)/shard_map/ppermute | solution.py:24
  144.1 82.6 %collective-permute-start.29 = (bf16[512,2816]{1,0:T(8,128)(2,1)}, bf16[512,2816]{1,0:T(8,128)(2,1)}, u32[]{:S(2)}, u32[]{:S(2)}) collective-permute-start(bf16[512,2816]{1,0:T(8,128)(2,1)} %bitcast.105), channel_id=1, source_target_pairs={{0,8},{8,0},{4,12},{12,4},{1,9},{9,1},{5,13},{13,5},{2,10},{10,2},... | collective-permute-start | bytes 8650760 | tf_op jit(solution)/shard_map/ppermute | solution.py:28
  155.4 58.4 %collective-permute-start.34 = (bf16[256,512]{1,0:T(8,128)(2,1)S(1)}, bf16[256,512]{1,0:T(8,128)(2,1)S(1)}, u32[]{:S(2)}, u32[]{:S(2)}) collective-permute-start(bf16[256,512]{1,0:T(8,128)(2,1)S(1)} %constant_dynamic-slice_fusion.3), channel_id=1, source_target_pairs={{0,8},{8,0},{4,12},{12,4},{1,9},{9,1},{5,13},{13,5},{2,10},{10,2},... | collective-permute-start | bytes 786440 | tf_op jit(solution)/shard_map/ppermute | solution.py:28
  158.2 55.8 %collective-permute-start.17 = (bf16[256,512]{1,0:T(8,128)(2,1)S(1)}, bf16[256,512]{1,0:T(8,128)(2,1)S(1)}, u32[]{:S(2)}, u32[]{:S(2)}) collective-permute-start(bf16[256,512]{1,0:T(8,128)(2,1)S(1)} %fusion.50), channel_id=1, source_target_pairs={{0,1},{1,2},{2,3},{3,0},{4,5},{5,6},{6,7},{7,4},{8,9},{9,10},{10,1... | collective-permute-start | bytes 786440 | tf_op jit(solution)/shard_map/ppermute | solution.py:425
  163.8 51.5 %collective-permute-start.21 = (bf16[256,512]{1,0:T(8,128)(2,1)S(1)}, bf16[256,512]{1,0:T(8,128)(2,1)S(1)}, u32[]{:S(2)}, u32[]{:S(2)}) collective-permute-start(bf16[256,512]{1,0:T(8,128)(2,1)S(1)} %fusion.48), channel_id=1, source_target_pairs={{1,0},{2,1},{3,2},{0,3},{5,4},{6,5},{7,6},{4,7},{9,8},{10,9},{11,1... | collective-permute-start | bytes 786440 | tf_op jit(solution)/shard_map/ppermute | solution.py:427
  165.7 50.0 %collective-permute-start.31 = (bf16[256,512]{1,0:T(8,128)(2,1)S(1)}, bf16[256,512]{1,0:T(8,128)(2,1)S(1)}, u32[]{:S(2)}, u32[]{:S(2)}) collective-permute-start(bf16[256,512]{1,0:T(8,128)(2,1)S(1)} %get-tuple-element.77), channel_id=1, source_target_pairs={{0,1},{1,2},{2,3},{3,0},{4,5},{5,6},{6,7},{7,4},{8,9},{9,10},{10,1... | collective-permute-start | bytes 786440 | tf_op jit(solution)/shard_map/ppermute | solution.py:407
  220.4 58.7 %collective-permute-start.36 = (bf16[256,512]{1,0:T(8,128)(2,1)S(1)}, bf16[256,512]{1,0:T(8,128)(2,1)S(1)}, u32[]{:S(2)}, u32[]{:S(2)}) collective-permute-start(bf16[256,512]{1,0:T(8,128)(2,1)S(1)} %collective-permute-done.35), channel_id=1, source_target_pairs={{1,0},{2,1},{3,2},{0,3},{5,4},{6,5},{7,6},{4,7},{9,8},{10,9},{11,1... | collective-permute-start | bytes 786440 | tf_op jit(solution)/shard_map/ppermute | solution.py:408
  226.7 54.4 %collective-permute-start.33 = (bf16[256,512]{1,0:T(8,128)(2,1)S(1)}, bf16[256,512]{1,0:T(8,128)(2,1)S(1)}, u32[]{:S(2)}, u32[]{:S(2)}) collective-permute-start(bf16[256,512]{1,0:T(8,128)(2,1)S(1)} %collective-permute-done.32), channel_id=1, source_target_pairs={{0,1},{1,2},{2,3},{3,0},{4,5},{5,6},{6,7},{7,4},{8,9},{9,10},{10,1... | collective-permute-start | bytes 786440 | tf_op jit(solution)/shard_map/ppermute | solution.py:407
  226.7 61.3 %collective-permute-start.38 = (bf16[1408,512]{1,0:T(8,128)(2,1)S(1)}, bf16[1408,512]{1,0:T(8,128)(2,1)S(1)}, u32[]{:S(2)}, u32[]{:S(2)}) collective-permute-start(bf16[1408,512]{1,0:T(8,128)(2,1)S(1)} %copy-done.55), channel_id=1, source_target_pairs={{0,8},{8,0},{4,12},{12,4},{1,9},{9,1},{5,13},{13,5},{2,10},{10,2},... | collective-permute-start | bytes 4325384 | tf_op jit(solution)/shard_map/ppermute | solution.py:28
  360.2 34.7 %collective-permute-start.41 = (bf16[512,1408]{1,0:T(8,128)(2,1)}, bf16[512,1408]{1,0:T(8,128)(2,1)S(1)}, u32[]{:S(2)}, u32[]{:S(2)}) collective-permute-start(bf16[512,1408]{1,0:T(8,128)(2,1)} %get-tuple-element.46), channel_id=1, source_target_pairs={{0,4},{4,0},{8,12},{12,8},{1,5},{5,1},{9,13},{13,9},{2,6},{6,2},{1... | collective-permute-start | bytes 4325384 | tf_op jit(solution)/shard_map/ppermute | solution.py:24
  374.3 170.1 %collective-permute-start.92 = (bf16[512,2816]{1,0:T(8,128)(2,1)}, bf16[512,2816]{1,0:T(8,128)(2,1)}, u32[]{:S(2)}, u32[]{:S(2)}) collective-permute-start(bf16[512,2816]{1,0:T(8,128)(2,1)} %convolution_convert_fusion), channel_id=1, source_target_pairs={{0,8},{8,0},{4,12},{12,4},{1,9},{9,1},{5,13},{13,5},{2,10},{10,2},... | collective-permute-start | bytes 8650760 | tf_op jit(solution)/shard_map/ppermute | solution.py:28
  415.8 64.9 %collective-permute-start.90 = (bf16[512,512]{1,0:T(8,128)(2,1)}, bf16[512,512]{1,0:T(8,128)(2,1)}, u32[]{:S(2)}, u32[]{:S(2)}) collective-permute-start(bf16[512,512]{1,0:T(8,128)(2,1)} %convolution_convert_fusion.4), channel_id=1, source_target_pairs={{0,8},{8,0},{4,12},{12,4},{1,9},{9,1},{5,13},{13,5},{2,10},{10,2},... | collective-permute-start | bytes 1572872 | tf_op jit(solution)/shard_map/ppermute | solution.py:28
  421.5 145.2 %collective-permute-start.94 = (bf16[1408,512]{1,0:T(8,128)(2,1)}, bf16[1408,512]{1,0:T(8,128)(2,1)}, u32[]{:S(2)}, u32[]{:S(2)}) collective-permute-start(bf16[1408,512]{1,0:T(8,128)(2,1)} %convolution_convert_fusion.1), channel_id=1, source_target_pairs={{0,8},{8,0},{4,12},{12,4},{1,9},{9,1},{5,13},{13,5},{2,10},{10,2},... | collective-permute-start | bytes 4325384 | tf_op jit(solution)/shard_map/ppermute | solution.py:28
  430.2 56.9 %collective-permute-start.59 = (bf16[256,512]{1,0:T(8,128)(2,1)S(1)}, bf16[256,512]{1,0:T(8,128)(2,1)S(1)}, u32[]{:S(2)}, u32[]{:S(2)}) collective-permute-start(bf16[256,512]{1,0:T(8,128)(2,1)S(1)} %fusion.39), channel_id=1, source_target_pairs={{1,0},{2,1},{3,2},{0,3},{5,4},{6,5},{7,6},{4,7},{9,8},{10,9},{11,1... | collective-permute-start | bytes 786440 | tf_op jit(solution)/shard_map/ppermute | solution.py:427
  434.7 46.0 %collective-permute-start.86 = (f32[128]{0:T(128)S(1)}, f32[128]{0:T(128)S(1)}, u32[]{:S(2)}, u32[]{:S(2)}) collective-permute-start(f32[128]{0:T(128)S(1)} %bitcast_add_fusion.24), channel_id=1, source_target_pairs={{0,8},{8,0},{4,12},{12,4},{1,9},{9,1},{5,13},{13,5},{2,10},{10,2},... | collective-permute-start | bytes 1544 | tf_op jit(solution)/shard_map/ppermute | solution.py:28
  493.4 30.2 %collective-permute-start.60 = (bf16[256,512]{1,0:T(8,128)(2,1)}, bf16[256,512]{1,0:T(8,128)(2,1)S(1)}, u32[]{:S(2)}, u32[]{:S(2)}) collective-permute-start(bf16[256,512]{1,0:T(8,128)(2,1)} %fusion.38), channel_id=1, source_target_pairs={{1,0},{2,1},{3,2},{0,3},{5,4},{6,5},{7,6},{4,7},{9,8},{10,9},{11,1... | collective-permute-start | bytes 786440 | tf_op jit(solution)/shard_map/ppermute | solution.py:427
  499.7 33.4 %collective-permute-start.91 = (bf16[512,512]{1,0:T(8,128)(2,1)}, bf16[512,512]{1,0:T(8,128)(2,1)S(1)}, u32[]{:S(2)}, u32[]{:S(2)}) collective-permute-start(bf16[512,512]{1,0:T(8,128)(2,1)} %fusion.7), channel_id=1, source_target_pairs={{0,16},{16,0},{1,17},{17,1},{2,18},{18,2},{3,19},{19,3},{4,20},{20... | collective-permute-start | bytes 1572872 | tf_op jit(solution)/shard_map/ppermute | solution.py:445
  540.4 36.3 %collective-permute-start.78 = (bf16[512,1024]{1,0:T(8,128)(2,1)S(1)}, bf16[512,1024]{1,0:T(8,128)(2,1)S(1)}, u32[]{:S(2)}, u32[]{:S(2)}) collective-permute-start(bf16[512,1024]{1,0:T(8,128)(2,1)S(1)} %convolution_convert_fusion.3), channel_id=1, source_target_pairs={{0,8},{8,0},{4,12},{12,4},{1,9},{9,1},{5,13},{13,5},{2,10},{10,2},... | collective-permute-start | bytes 3145736 | tf_op jit(solution)/shard_map/ppermute | solution.py:28
  550.3 140.6 %collective-permute-start.93 = (bf16[512,2816]{1,0:T(8,128)(2,1)}, bf16[512,2816]{1,0:T(8,128)(2,1)}, u32[]{:S(2)}, u32[]{:S(2)}) collective-permute-start(bf16[512,2816]{1,0:T(8,128)(2,1)} %add_convert_fusion), channel_id=1, source_target_pairs={{0,16},{16,0},{1,17},{17,1},{2,18},{18,2},{3,19},{19,3},{4,20},{20... | collective-permute-start | bytes 8650760 | tf_op jit(solution)/shard_map/ppermute | solution.py:445
  569.9 77.0 %collective-permute-start.95 = (bf16[1408,512]{1,0:T(8,128)(2,1)S(1)}, bf16[1408,512]{1,0:T(8,128)(2,1)S(1)}, u32[]{:S(2)}, u32[]{:S(2)}) collective-permute-start(bf16[1408,512]{1,0:T(8,128)(2,1)S(1)} %add_convert_fusion.3), channel_id=1, source_target_pairs={{0,16},{16,0},{1,17},{17,1},{2,18},{18,2},{3,19},{19,3},{4,20},{20... | collective-permute-start | bytes 4325384 | tf_op jit(solution)/shard_map/ppermute | solution.py:445
  578.0 89.3 %collective-permute-start.79 = (bf16[512,1024]{1,0:T(8,128)(2,1)S(1)}, bf16[512,1024]{1,0:T(8,128)(2,1)S(1)}, u32[]{:S(2)}, u32[]{:S(2)}) collective-permute-start(bf16[512,1024]{1,0:T(8,128)(2,1)S(1)} %add_convert_fusion.5), channel_id=1, source_target_pairs={{0,16},{16,0},{1,17},{17,1},{2,18},{18,2},{3,19},{19,3},{4,20},{20... | collective-permute-start | bytes 3145736 | tf_op jit(solution)/shard_map/ppermute | solution.py:445
  593.8 85.3 %collective-permute-start.80 = (bf16[512,1024]{1,0:T(8,128)(2,1)}, bf16[512,1024]{1,0:T(8,128)(2,1)}, u32[]{:S(2)}, u32[]{:S(2)}) collective-permute-start(bf16[512,1024]{1,0:T(8,128)(2,1)} %convolution_convert_fusion.2), channel_id=1, source_target_pairs={{0,8},{8,0},{4,12},{12,4},{1,9},{9,1},{5,13},{13,5},{2,10},{10,2},... | collective-permute-start | bytes 3145736 | tf_op jit(solution)/shard_map/ppermute | solution.py:28
  595.9 52.9 %collective-permute-start.74 = (f32[2,512]{1,0:T(2,128)S(1)}, f32[2,512]{1,0:T(2,128)S(1)}, u32[]{:S(2)}, u32[]{:S(2)}) collective-permute-start(f32[2,512]{1,0:T(2,128)S(1)} %pad_maximum_fusion.7), channel_id=1, source_target_pairs={{0,8},{8,0},{4,12},{12,4},{1,9},{9,1},{5,13},{13,5},{2,10},{10,2},... | collective-permute-start | bytes 12296 | tf_op jit(solution)/shard_map/ppermute | solution.py:28
  (162 other events, 2177.6 us)

commit v2 on v0

v2 whole, which is shorter than its diff:
```python
from functools import partial

import jax
import jax.numpy as jnp
from jax import lax
from jax.experimental import pallas as pl
from jax.experimental.pallas import tpu as pltpu
from jax.sharding import PartitionSpec as P

D = 2048
HD = 128
BLOCK = 64
norm_eps = 1e-06
bf16 = jnp.bfloat16
f32 = jnp.float32

CORE = [(0, 1), (1, 0), (2, 3), (3, 2)]
CHIP = [(0, 2), (2, 0), (1, 3), (3, 1)]
UP = [(0, 1), (1, 2), (2, 3), (3, 0)]
DOWN = [(1, 0), (2, 1), (3, 2), (0, 3)]


def swap_core(x):
    return lax.ppermute(x, "row", CORE)


def swap_chip(x):
    return lax.ppermute(x, "row", CHIP)


def tie(x, *others):
    return lax.optimization_barrier((x, *others))[0]


def mm(left, right):
    return lax.dot_general(left, right, (((1,), (0,)), ((), ())), preferred_element_type=f32)


def mm_nt(left, right):
    return lax.dot_general(left, right, (((1,), (1,)), ((), ())), preferred_element_type=f32)


def mm_tn(left, right):
    return lax.dot_general(left, right, (((0,), (0,)), ((), ())), preferred_element_type=f32)


def silu_slope(value, sigma):
    return sigma * (1.0 + value * (1.0 - sigma))


def split_mm(left, value):
    high = value.astype(bf16)
    low = (value - high.astype(f32)).astype(bf16)
    return mm(left, high) + mm(left, low)


def run_masks(i, idc_ref, idr_ref, prev_ref):
    s = slice(i * BLOCK, (i + 1) * BLOCK)
    idc = idc_ref[s, :]
    idr = idr_ref[0, :, s]
    prev = prev_ref[s, :]
    before = prev[0:1, :]
    last = idc[BLOCK - 1 : BLOCK, :]
    t = lax.broadcasted_iota(jnp.int32, (BLOCK, BLOCK), 0)
    u = lax.broadcasted_iota(jnp.int32, (BLOCK, BLOCK), 1)
    same = idc == idr
    heads = (idc == before).astype(f32)
    tails = (idc == last).astype(f32)
    through = (last == before).astype(f32)
    old = (idc == prev).astype(f32)
    return t, u, same, heads, tails, through, old


def run_decays(f_raw, lb, t, u):
    closed = jax.nn.sigmoid(-f_raw)
    keys = (1.0 - lb) * closed
    total = split_mm((t >= u).astype(bf16), jnp.log1p(-keys))
    middle = total[BLOCK // 2 - 1 : BLOCK // 2, :]
    final = total[BLOCK - 1 : BLOCK, :]
    return closed, keys, total, middle, final


def col(h, part=0, heads=1):
    start = (part * heads + h) * HD
    return slice(start, start + HD)


def local_kernel(
    keep_ref, recv_ref, lb_ref, idc_ref, idr_ref, prev_ref,
    inner_ref, qh_ref, kh_ref, vb_ref, decay_ref, seg_ref, low_ref, segd_ref,
):
    heads = lb_ref.shape[1] // HD
    state = [jnp.zeros((HD, HD), f32)] * heads
    passing = [jnp.ones((1, HD), f32)] * heads
    for i in range(keep_ref.shape[0] // BLOCK):
        s = slice(i * BLOCK, (i + 1) * BLOCK)
        t, u, same, head, tails, through, _ = run_masks(i, idc_ref, idr_ref, prev_ref)
        for h in range(heads):
            c = col(h)

            def raw(part):
                p = col(h, part, heads)
                return keep_ref[s, p] + recv_ref[s, p].astype(f32)

            q_raw = raw(0)
            vb = raw(2).astype(bf16)
            q = q_raw * jax.nn.sigmoid(q_raw)
            _, keys, total, middle, final = run_decays(raw(1), lb_ref[:, c], t, u)
            qt = (q * jnp.exp(total - middle)).astype(bf16)
            kt = (keys * jnp.exp(middle - total)).astype(bf16)
            scores = jnp.where(same & (t >= u), mm_nt(qt, kt), 0.0).astype(bf16)
            inner_ref[s, c] = mm(scores, vb)
            qh_ref[s, c] = (q * jnp.exp(total) * head).astype(bf16)
            kh = (keys * jnp.exp(final - total) * tails).astype(bf16)
            kh_ref[s, c] = kh
            vb_ref[s, c] = vb
            keep = jnp.exp(final) * through
            decay_ref[0, i : i + 1, c] = keep
            state[h] = keep * state[h] + mm_tn(vb, kh)
            passing[h] = passing[h] * keep
    for h in range(heads):
        seg_ref[0, h] = state[h]
        low_ref[0, h] = state[h].astype(bf16)
        segd_ref[0, :, col(h)] = passing[h]


def enter_kernel(reverse, place_ref, seg_ref, segd_ref, peer_ref, peerd_ref, out_ref):
    z, y = place_ref[0], place_ref[1]
    count, heads = seg_ref.shape[:2]
    peer_first = (y == 0) if reverse else (y == 1)
    state = [jnp.zeros((HD, HD), f32)] * heads
    for place in reversed(range(count)) if reverse else range(count):
        k = lax.rem(z - place + count, count)
        for h in range(heads):
            add = peer_ref[k, h].astype(f32)
            scale = peerd_ref[k, :, col(h)]
            s = jnp.where(peer_first, scale, 1.0) * state[h] + jnp.where(peer_first, add, 0.0)
            out_ref[k, h] = s
            s = segd_ref[k, :, col(h)] * s + seg_ref[k, h]
            state[h] = jnp.where(peer_first, 1.0, scale) * s + jnp.where(peer_first, 0.0, add)


def finish_kernel(
    inner_ref, qh_ref, kh_ref, vb_ref, decay_ref, enter_ref, keep_ref, recv_ref, gain_ref,
    gated_ref, rec_ref, st_ref,
):
    heads = enter_ref.shape[1]
    state = [enter_ref[0, h] for h in range(heads)]
    for i in range(qh_ref.shape[0] // BLOCK):
        s = slice(i * BLOCK, (i + 1) * BLOCK)
        for h in range(heads):
            c = col(h)
            low = state[h].astype(bf16)
            st_ref[0, i, h] = low
            rec = inner_ref[s, c] + mm_nt(qh_ref[s, c], low)
            rec_ref[s, c] = rec
            scale = lax.rsqrt(jnp.mean(rec * rec, axis=1, keepdims=True) + norm_eps)
            g_raw = keep_ref[s, c] + recv_ref[s, c].astype(f32)
            gate = g_raw * jax.nn.sigmoid(g_raw)
            gated_ref[s, c] = (rec * scale * gain_ref[...] * gate).astype(bf16)
            state[h] = decay_ref[0, i : i + 1, c] * state[h] + mm_tn(vb_ref[s, c], kh_ref[s, c])


def back_local_kernel(
    kd, rd, rec_ref, keep_ref, recv_ref, gain_ref, qh_ref, decay_ref,
    do_ref, dg_ref, group_ref, seg_ref, low_ref,
):
    @pl.when(pl.program_id(0) == 0)
    def _():
        group_ref[...] = jnp.zeros_like(group_ref)

    gain = gain_ref[...]
    heads = seg_ref.shape[1]
    adjoint = [jnp.zeros((HD, HD), f32)] * heads
    group = jnp.zeros((1, HD), f32)
    for i in reversed(range(qh_ref.shape[0] // BLOCK)):
        s = slice(i * BLOCK, (i + 1) * BLOCK)
        for h in range(heads):
            c = col(h)
            grad = kd[s, c] + rd[s, c].astype(f32)
            rec = rec_ref[s, c]
            scale = lax.rsqrt(jnp.mean(rec * rec, axis=1, keepdims=True) + norm_eps)
            normed = rec * scale
            g_raw = keep_ref[s, c] + recv_ref[s, c].astype(f32)
            sigma = jax.nn.sigmoid(g_raw)
            act = g_raw * sigma
            both = grad * normed
            group = group + jnp.sum(both * act, axis=0, keepdims=True)
            dg_ref[s, c] = (both * gain * silu_slope(g_raw, sigma)).astype(bf16)
            dn = grad * gain * act
            do = (scale * (dn - normed * jnp.mean(dn * normed, axis=1, keepdims=True))).astype(bf16)
            do_ref[s, c] = do
            adjoint[h] = decay_ref[0, i : i + 1, c] * adjoint[h] + mm_tn(do, qh_ref[s, c])
    group_ref[...] += group
    for h in range(heads):
        seg_ref[0, h] = adjoint[h]
        low_ref[0, h] = adjoint[h].astype(bf16)


def back_finish_kernel(
    keep_ref, recv_ref, lb_ref, idc_ref, idr_ref, prev_ref,
    qh_ref, kh_ref, vb_ref, decay_ref, st_ref, do_ref, enter_ref,
    grad_ref, bound_ref,
):
    @pl.when(pl.program_id(0) == 0)
    def _():
        bound_ref[...] = jnp.zeros_like(bound_ref)

    heads = enter_ref.shape[1]
    adjoint = [enter_ref[0, h] for h in range(heads)]
    bound = [jnp.zeros((1, HD), f32)] * heads
    for i in reversed(range(keep_ref.shape[0] // BLOCK)):
        s = slice(i * BLOCK, (i + 1) * BLOCK)
        t, u, same, head, tails, through, old = run_masks(i, idc_ref, idr_ref, prev_ref)
        causal = same & (t >= u)
        later = (same & (u >= t)).astype(bf16)
        for h in range(heads):
            c = col(h)

            def raw(part):
                p = col(h, part, heads)
                return keep_ref[s, p] + recv_ref[s, p].astype(f32)

            q_raw = raw(0)
            sigma = jax.nn.sigmoid(q_raw)
            q = q_raw * sigma
            closed, keys, total, middle, final = run_decays(raw(1), lb_ref[:, c], t, u)
            out = jnp.exp(total - middle)
            back = jnp.exp(middle - total)
            qt = (q * out).astype(bf16)
            kt = (keys * back).astype(bf16)
            scores = jnp.where(causal, mm_nt(qt, kt), 0.0).astype(bf16)
            vb = vb_ref[s, c]
            kh = kh_ref[s, c]
            do = do_ref[s, c]
            st = st_ref[0, i, h]
            low = adjoint[h].astype(bf16)
            keep = decay_ref[0, i : i + 1, c]
            ds = jnp.where(causal, mm_nt(do, vb), 0.0).astype(bf16)
            dq = mm(ds, kt) * out + mm(do, st) * (jnp.exp(total) * head)
            dkh = mm(vb, low)
            dk = mm_tn(ds, qt) * back + dkh * (jnp.exp(final - total) * tails)
            grad_ref[s, col(h, 2, heads)] = (mm_tn(scores, do) + mm_nt(kh, low)).astype(bf16)
            ends = keep * jnp.sum(adjoint[h] * st.astype(f32), axis=0, keepdims=True) + jnp.sum(
                kh.astype(f32) * dkh, axis=0, keepdims=True
            )
            dlog = split_mm(later, q * dq - keys * dk) + tails * ends
            key_total = dk - old * dlog / (1.0 - keys)
            bound[h] = bound[h] - jnp.sum(key_total * closed, axis=0, keepdims=True)
            grad_ref[s, col(h, 1, heads)] = (-key_total * keys * (1.0 - closed)).astype(bf16)
            grad_ref[s, col(h, 0, heads)] = (dq * silu_slope(q_raw, sigma)).astype(bf16)
            adjoint[h] = keep * adjoint[h] + mm_tn(do, qh_ref[s, c])
    for h in range(heads):
        bound_ref[:, col(h)] += bound[h]


def shape(dims, kind):
    return jax.ShapeDtypeStruct(dims, kind)


COST = pl.CostEstimate(flops=0, bytes_accessed=0, transcendentals=0)
SMEM = pl.BlockSpec(memory_space=pltpu.SMEM)
VMEM = pl.BlockSpec(memory_space=pltpu.VMEM)


def run_block(*dims, at=0):
    return pl.BlockSpec(dims, lambda j: (j, *([0] * (len(dims) - 2)), at))


def whole(*dims):
    return pl.BlockSpec(dims, lambda j: (0,) * len(dims))


def recurrence_local(keep, recv, bound, ids):
    runs, _, run = ids[1].shape
    width = bound.shape[1]
    heads = width // HD
    chunks = run // BLOCK
    tokens = runs * run
    return pl.pallas_call(
        local_kernel,
        grid=(runs,),
        in_specs=[
            run_block(run, 4 * width), run_block(run, 4 * width), whole(1, width),
            run_block(run, 1), run_block(1, 1, run), run_block(run, 1),
        ],
        out_specs=[run_block(run, width)] * 4
        + [run_block(1, chunks, width)]
        + [run_block(1, heads, HD, HD)] * 2
        + [run_block(1, 1, width)],
        out_shape=[
            shape((tokens, width), f32),
            shape((tokens, width), bf16),
            shape((tokens, width), bf16),
            shape((tokens, width), bf16),
            shape((runs, chunks, width), f32),
            shape((runs, heads, HD, HD), f32),
            shape((runs, heads, HD, HD), bf16),
            shape((runs, 1, width), f32),
        ],
        cost_estimate=COST,
        name="recurrence_local",
    )(keep, recv, bound, *ids)


def recurrence_enter(place, seg, segd, peer, peerd, reverse):
    return pl.pallas_call(
        partial(enter_kernel, reverse),
        in_specs=[SMEM] + [VMEM] * 4,
        out_specs=VMEM,
        out_shape=shape(seg.shape, f32),
        cost_estimate=COST,
        name="recurrence_enter_back" if reverse else "recurrence_enter",
    )(place, seg, segd, peer, peerd)


def recurrence_finish(local, enter, keep, recv, gain):
    inner, qh, kh, vb, decay = local
    runs, chunks, width = decay.shape
    heads = width // HD
    run = chunks * BLOCK
    tokens = runs * run
    cols = run_block(run, width)
    gate = run_block(run, width, at=3)
    return pl.pallas_call(
        finish_kernel,
        grid=(runs,),
        in_specs=[
            cols, cols, cols, cols, run_block(1, chunks, width), run_block(1, heads, HD, HD),
            gate, gate, whole(1, HD),
        ],
        out_specs=[cols, cols, run_block(1, chunks, heads, HD, HD)],
        out_shape=[
            shape((tokens, width), bf16),
            shape((tokens, width), f32),
            shape((runs, chunks, heads, HD, HD), bf16),
        ],
        cost_estimate=COST,
        name="recurrence_finish",
    )(inner, qh, kh, vb, decay, enter, keep, recv, gain)


def recurrence_back_local(kd, rd, rec, keep, recv, gain, qh, decay):
    runs, chunks, width = decay.shape
    heads = width // HD
    run = chunks * BLOCK
    tokens = runs * run
    cols = run_block(run, width)
    gate = run_block(run, width, at=3)
    return pl.pallas_call(
        back_local_kernel,
        grid=(runs,),
        in_specs=[
            cols, cols, cols, gate, gate, whole(1, HD), cols, run_block(1, chunks, width),
        ],
        out_specs=[cols, cols, whole(1, HD)] + [run_block(1, heads, HD, HD)] * 2,
        out_shape=[
            shape((tokens, width), bf16),
            shape((tokens, width), bf16),
            shape((1, HD), f32),
            shape((runs, heads, HD, HD), f32),
            shape((runs, heads, HD, HD), bf16),
        ],
        cost_estimate=COST,
        name="recurrence_back_local",
    )(kd, rd, rec, keep, recv, gain, qh, decay)


def recurrence_back_finish(keep, recv, bound, ids, local, states, do, enter):
    _, qh, kh, vb, decay = local
    runs, chunks, width = decay.shape
    heads = width // HD
    run = chunks * BLOCK
    tokens = runs * run
    cols = run_block(run, width)
    return pl.pallas_call(
        back_finish_kernel,
        grid=(runs,),
        in_specs=[
            run_block(run, 4 * width), run_block(run, 4 * width), whole(1, width),
            run_block(run, 1), run_block(1, 1, run), run_block(run, 1),
            cols, cols, cols, run_block(1, chunks, width),
            run_block(1, chunks, heads, HD, HD), cols, run_block(1, heads, HD, HD),
        ],
        out_specs=[run_block(run, 3 * width), whole(1, width)],
        out_shape=[shape((tokens, 3 * width), bf16), shape((1, width), f32)],
        cost_estimate=COST,
        name="recurrence_back_finish",
    )(keep, recv, bound, *ids, qh, kh, vb, decay, states, do, enter)


def swap_group(x):
    return lax.ppermute(x, "dp", [(0, 1), (1, 0)])


def up(x):
    return lax.ppermute(x, "col", UP)


def down(x):
    return lax.ppermute(x, "col", DOWN)


def step(sends, work=None, given=(), join=()):
    n = len(sends)
    arrays = lax.optimization_barrier((*(array for _, array in sends), *given))
    moved = [mover(array) for (mover, _), array in zip(sends, arrays)]
    made = tuple(work(*arrays[n:])) if work else ()
    ends = made[:1] if getattr(work, "marked", False) else made
    done = lax.optimization_barrier((*moved, *ends, *join))
    made = made[1:] if getattr(work, "marked", False) else done[n : n + len(made)]
    return list(done[:n]), list(made), list(done[n + len(ends) :])


def aside(ready, work):
    def marked(*given):
        return (jnp.ones((), f32), *work(*given))

    def run(*given):
        shapes = jax.eval_shape(marked, *given)
        return lax.cond(
            ready, marked, lambda *a: tuple(jnp.zeros(s.shape, s.dtype) for s in shapes), *given
        )

    run.marked = True
    return run


def ordered(own, other):
    return jnp.concatenate(own, 0), jnp.concatenate([other[0], *other[:0:-1]], 0)


def cut(array, count):
    each = -(-array.shape[0] // count)
    each = -(-each // 16) * 16
    return [array[at : at + each] for at in range(0, array.shape[0], each)]


def shards(
    tokens,
    segments,
    mix_gain,
    w_mix,
    lower_bound,
    group_gain,
    w_out,
    ffn_gain,
    w_ffn_in,
    w_down,
    cotangent,
):
    row = lax.axis_index("row")
    core = row % 2
    y = row // 2
    z = lax.axis_index("col")
    count = lax.axis_size("col")
    pairs = lax.axis_size("dp") == 2
    half = tokens.shape[0] // 2
    width = tokens.shape[1]
    hc = w_mix.shape[2] // 2
    units_col = w_down.shape[0]
    here = count * half
    hb = here // 2
    ready = segments[0] >= 0

    def mine(x, at, size, axis):
        return lax.dynamic_slice_in_dim(x, at * size, size, axis)

    def rows(x, at):
        return mine(x, at, hb, 0)

    def joined(first_if_zero, second_if_zero, flag, axis):
        return jnp.where(
            flag == 0,
            jnp.concatenate([first_if_zero, second_if_zero], axis),
            jnp.concatenate([second_if_zero, first_if_zero], axis),
        )

    def blocks(array):
        return [array[k * half : (k + 1) * half] for k in range(count)]

    tok_own = mine(tokens, y, half, 0)
    (tok_other,), _, _ = step([(swap_chip, mine(tokens, 1 - y, half, 0))])
    cot_own, cot_send = mine(cotangent, y, half, 0), mine(cotangent, 1 - y, half, 0)
    wm_parts = cut(w_mix, 4)
    first = swap_chip(tie(wm_parts[0], tok_other))
    gains_other = swap_chip(tie(jnp.stack([mix_gain, ffn_gain]), tok_other))
    x_own, x_other = tok_own.astype(f32), tok_other.astype(f32)
    squares = jnp.sum(x_own * x_own, axis=1) + jnp.sum(x_other * x_other, axis=1)
    squares = squares + swap_core(squares)
    mix_scale = lax.rsqrt(squares / D + norm_eps)[:, None]
    mo = [(x_own * mix_scale * mix_gain).astype(bf16)]
    mp = [(x_other * mix_scale * gains_other[0]).astype(bf16)]
    wm = [first]
    for k in range(1, count):
        sends = [(up, mo[-1]), (down, mp[-1])]
        sends.append((swap_chip, cot_send if k == 1 else wm_parts[k - 1]))
        (a, b, got), _, late = step(sends, join=wm if k == 1 else [])
        if k == 1:
            wm, cot_other = late, got
        else:
            wm.append(got)
        mo.append(a)
        mp.append(b)
    co, cp = [cot_own], [cot_other]
    (a, b, got, mo[-1], mp[-1]), _, _ = step(
        [(up, cot_own), (down, cot_other), (swap_chip, wm_parts[3])]
        + [(lambda v: v, mo[-1]), (lambda v: v, mp[-1])]
    )
    co.append(a)
    cp.append(b)
    wm_other = jnp.concatenate([*wm, got], 0)
    m_own, m_other = ordered(mo, mp)

    def columns(w, at):
        return mine(w, at, hc, 2).reshape(width, 4 * hc)

    wm_keep, wm_send = columns(w_mix, core), columns(w_mix, 1 - core)
    wm_keep_o, wm_send_o = columns(wm_other, core), columns(wm_other, 1 - core)

    names = segments.astype(f32)
    before = jnp.concatenate([jnp.full((1,), -1.0, f32), names[:-1]])

    def runs_of(array):
        array = lax.dynamic_index_in_dim(array.reshape(count, 2, half), y, 1, keepdims=False)
        places = [(z - k + count) % count for k in range(count)]
        return jnp.stack(
            [lax.dynamic_index_in_dim(array, at, 0, keepdims=False) for at in places]
        )

    names, before = runs_of(names), runs_of(before)
    ids = (names.reshape(here, 1), names.reshape(count, 1, half), before.reshape(here, 1))
    bound = mine(lower_bound, core, hc, 0).reshape(1, hc)
    gain_row = group_gain.reshape(1, HD)
    place = jnp.stack([z, y]).astype(jnp.int32)

    send = (mm(m_own, wm_send) + mm(m_other, wm_send_o)).astype(bf16)
    recv = swap_core(send)
    keep = mm(m_own, wm_keep) + mm(m_other, wm_keep_o)
    wf = w_ffn_in.reshape(width, 2 * units_col)
    pieces = cut(w_down, 2) + cut(wf, 5)
    (a, b, wo_o), local, _ = step(
        [(up, co[-1]), (down, cp[-1]), (swap_chip, w_out)],
        lambda keep, recv: recurrence_local(keep, recv, bound, ids),
        (keep, recv),
    )
    co.append(a)
    cp.append(b)
    *local, seg, low, decay = local
    (peer, peer_decay), _, _ = step([(swap_chip, low), (swap_chip, decay)])

    def finish(seg, decay, peer, peer_decay):
        enter = recurrence_enter(place, seg, decay, peer, peer_decay, False)
        return recurrence_finish(local, enter, keep, recv, gain_row)

    (a, b, got), (gated, rec, states), _ = step(
        [(up, co[-1]), (down, cp[-1]), (swap_chip, pieces[0])],
        finish,
        (seg, decay, peer, peer_decay),
    )
    co.append(a)
    cp.append(b)
    weights = [got]
    c_own, c_other = ordered(co, cp)
    gated = joined(gated, swap_core(gated), core, 1)

    def scatter(own, other, beside):
        a, b = own[1], other[-1]
        for k in range(1, count):
            sends, work, given, take = beside(k)
            moved, made, _ = step([(up, a.astype(bf16)), (down, b.astype(bf16)), *sends], work, given)
            a = moved[0].astype(f32) + own[(k + 1) % count].astype(f32)
            b = moved[1].astype(f32) + other[-(k + 1) % count].astype(f32)
            take(moved[2:], made)
        return a, b

    def gather(own, other, beside):
        own, other = [own], [other]
        for k in range(1, count):
            sends, work, given, take = beside(k)
            moved, made, _ = step([(up, own[-1]), (down, other[-1]), *sends], work, given)
            own.append(moved[0])
            other.append(moved[1])
            take(moved[2:], made)
        return ordered(own, other)

    def weights_step(k):
        return [(swap_chip, pieces[len(weights)])], None, (), lambda moved, made: weights.extend(moved)

    h_own, h_other = scatter(
        blocks(mm(gated, w_out).astype(bf16)), blocks(mm(gated, wo_o).astype(bf16)), weights_step
    )
    h_own, h_other = x_own + h_own, x_other + h_other

    squares = jnp.sum(h_own * h_own, axis=1) + jnp.sum(h_other * h_other, axis=1)
    squares = squares + swap_core(squares)
    ffn_scale = lax.rsqrt(squares / D + norm_eps)[:, None]
    n_own = (h_own * ffn_scale * ffn_gain).astype(bf16)
    n_other = (h_other * ffn_scale * gains_other[1]).astype(bf16)

    wd_o = jnp.concatenate(weights[:2], 0)
    gu_recv = swap_core(
        (mm_nt(rows(c_own, 1 - core), w_down) + mm_nt(rows(c_other, 1 - core), wd_o)).astype(bf16)
    )
    gu = mm_nt(rows(c_own, core), w_down) + mm_nt(rows(c_other, core), wd_o) + gu_recv.astype(f32)
    f_own, f_other = gather(n_own, n_other, weights_step)
    wf_o = jnp.concatenate(weights[2:], 0)
    f_own, gu = lax.optimization_barrier((f_own, gu))
    fk_own, fs_own = rows(f_own, core), rows(f_own, 1 - core)
    fk_other, fs_other = rows(f_other, core), rows(f_other, 1 - core)
    b_recv = swap_core((mm(fs_own, wf) + mm(fs_other, wf_o)).astype(bf16))
    both = mm(fk_own, wf) + mm(fk_other, wf_o) + b_recv.astype(f32)
    gate, up_part = both[:, :units_col], both[:, units_col:]
    sigma = jax.nn.sigmoid(gate)
    act = gate * sigma
    units = (act * up_part).astype(bf16)
    gb = jnp.concatenate(
        [(gu * up_part * silu_slope(gate, sigma)).astype(bf16), (gu * act).astype(bf16)], 1
    )
    gb_p = swap_core(gb)
    units_p = swap_core(tie(units, gb))
    df_kept = [mm_nt(gb, wf).astype(bf16), mm_nt(gb, wf_o).astype(bf16)]
    df_sent = [mm_nt(gb_p, wf).astype(bf16), mm_nt(gb_p, wf_o).astype(bf16)]
    ck_own, cs_own = rows(c_own, core), rows(c_own, 1 - core)
    ck_other, cs_other = rows(c_other, core), rows(c_other, 1 - core)
    down_sent = cut((mm_tn(units, ck_other) + mm_tn(units_p, cs_other)).astype(bf16), 2)

    def by_core(kept, sent):
        each = count // 2
        parts = []
        for k in range(count):
            s = slice(k % each * half, (k % each + 1) * half)
            parts.append(jnp.where(core == k // each, kept[s], sent[s]))
        return parts

    y_queue, x_queue, x_done, own_parts = [], [], [], {}

    def background(take_more=None, work=None, given=(), y_pieces=1, x_pieces=1):
        sends, keys = [], []
        for _ in range(min(y_pieces, len(y_queue))):
            key, array = y_queue.pop(0)
            keys.append(key)
            sends.append((swap_chip, array))
        n = len(sends)
        moving = [x_queue.pop(0) for _ in range(min(x_pieces, len(x_queue)))]
        if pairs:
            sends += [(swap_group, array) for _, array in moving]

        def take(moved, made):
            if take_more is not None:
                take_more(made)
            for key, got in zip(keys, moved[:n]):
                x_queue.append((key, (own_parts[key] + got.astype(f32)).astype(bf16)))
            for n_moved, (key, array) in enumerate(moving):
                if pairs:
                    value = array.astype(f32) + moved[n + n_moved].astype(f32)
                else:
                    value = lax.psum(array, "dp").astype(f32)
                x_done.append((key, value))

        return sends, work, given, take

    def queue(name, parts):
        y_queue.extend((f"{name}{n}", part) for n, part in enumerate(parts))

    def hold(name, parts):
        own_parts.update((f"{name}{n}", part) for n, part in enumerate(parts))

    queue("d", down_sent)

    def ffn_step(k):
        if k == 1:

            def take(made):
                hold("d", made[:2])
                queue("f", made[2:])

            def work(u, v, c, d, f, h, g, p):
                grad = (mm_tn(f, g) + mm_tn(h, p)).astype(bf16)
                return (*cut(mm_tn(u, c) + mm_tn(v, d), 2), *cut(grad, 4))

            given = (units, units_p, ck_own, cs_own, fk_other, fs_other, gb, gb_p)
            return background(take, aside(ready, work), given)
        if k == 2:

            def work(f, h, g, p):
                return cut(mm_tn(f, g) + mm_tn(h, p), 4)

            return background(
                lambda made: hold("f", made), aside(ready, work), (fk_own, fs_own, gb, gb_p)
            )

        def work(u, v, w, o):
            return [mm(a, b).astype(bf16) for b in (w, o) for a in (u, v)]

        return background(kept.extend, aside(ready, work), (units, units_p, w_down, wd_o))

    kept = []
    df_own, df_other = scatter(
        by_core(df_kept[0], df_sent[0]), by_core(df_kept[1], df_sent[1]), ffn_step
    )
    un_own, un_other = by_core(*kept[:2]), by_core(*kept[2:])

    gain_fo = gains_other[1]
    w_o, w_p = df_own * ffn_gain, df_other * gain_fo
    along = jnp.sum(w_o * h_own, axis=1) + jnp.sum(w_p * h_other, axis=1)
    along = along + swap_core(along)
    factor = ffn_scale**3 * along[:, None] / D
    gh_own = cot_own.astype(f32) + ffn_scale * w_o - h_own * factor
    gh_other = cot_other.astype(f32) + ffn_scale * w_p - h_other * factor
    ffn_part = jnp.sum(df_own * h_own * ffn_scale, axis=0)
    ffn_part_o = jnp.sum(df_other * h_other * ffn_scale, axis=0)
    g_own, g_other = gather(
        gh_own.astype(bf16), gh_other.astype(bf16), lambda k: background()
    )

    gg_recv = swap_core(
        (mm_nt(g_own, mine(w_out, 1 - core, hc, 0)) + mm_nt(g_other, mine(wo_o, 1 - core, hc, 0)))
        .astype(bf16)
    )
    gg_keep = mm_nt(g_own, mine(w_out, core, hc, 0)) + mm_nt(g_other, mine(wo_o, core, hc, 0))
    out_sent = mm_tn(gated, g_other).astype(bf16)
    do, d_gate, group_part, seg, low = recurrence_back_local(
        gg_keep, gg_recv, rec, keep, recv, gain_row, local[1], local[4]
    )
    (peer, d_gate_p), _, _ = step([(swap_chip, low), (swap_core, d_gate)])

    def finish_back(seg, peer):
        enter = recurrence_enter(place, seg, decay, peer, peer_decay, True)
        return recurrence_back_finish(keep, recv, bound, ids, local, states, do, enter)

    queue("o", [out_sent])
    out_a, out_b = un_own[1], un_other[-1]
    sends, _, _, take = background(y_pieces=1, x_pieces=1)
    moved, (d_three, bound_part), _ = step(
        [(up, out_a), (down, out_b), *sends], finish_back, (seg, peer)
    )
    out_a = (moved[0].astype(f32) + un_own[2].astype(f32)).astype(bf16)
    out_b = (moved[1].astype(f32) + un_other[2].astype(f32)).astype(bf16)
    hold("o", [mm_tn(gated, g_own)])
    take(moved[2:], [])

    d_three_p = swap_core(d_three)

    def part(p):
        if p == 3:
            return joined(d_gate, d_gate_p, core, 1)
        s = slice(p * hc, (p + 1) * hc)
        return joined(d_three[:, s], d_three_p[:, s], core, 1)

    sums_own = mm_nt(d_three, wm_keep[:, : 3 * hc]) + mm_nt(d_gate, wm_keep[:, 3 * hc :])
    sums_own += mm_nt(d_three_p, wm_send[:, : 3 * hc]) + mm_nt(d_gate_p, wm_send[:, 3 * hc :])
    sums_other = mm_nt(d_three, wm_keep_o[:, : 3 * hc]) + mm_nt(d_gate, wm_keep_o[:, 3 * hc :])
    sums_other += mm_nt(d_three_p, wm_send_o[:, : 3 * hc]) + mm_nt(d_gate_p, wm_send_o[:, 3 * hc :])
    parts = {name: part(p) for p, name in enumerate("qkvg")}

    for name in "gqkv":
        queue(name, [mm_tn(m_other, parts[name]).astype(bf16)])
        hold(name, [mm_tn(m_own, parts[name])])
    dx_own, dx_other = scatter(
        blocks(sums_own.astype(bf16)),
        blocks(sums_other.astype(bf16)),
        lambda k: background(None, None, (), 2 if k == 1 else 1, 2 if k == 3 else 1),
    )
    mix_part = jnp.sum(sums_own * m_own.astype(f32), axis=0) / mix_gain
    mix_part_o = jnp.sum(sums_other * m_other.astype(f32), axis=0) / gains_other[0]
    tail = jnp.concatenate([bound_part[0], group_part[0]])
    small = jnp.concatenate([mix_part, ffn_part, tail])
    small_o = jnp.concatenate([mix_part_o, ffn_part_o, tail])
    sends, _, _, take = background(None, None, (), 1, 1)
    moved, _, _ = step([(up, out_a), (down, out_b), (swap_chip, small_o), *sends])
    out_a = (moved[0].astype(f32) + un_own[3].astype(f32)).astype(bf16)
    out_b = (moved[1].astype(f32) + un_other[1].astype(f32)).astype(bf16)
    small = small + moved[2]
    take(moved[3:], [])

    w_o, w_p = dx_own * mix_gain, dx_other * gains_other[0]
    along = jnp.sum(w_o * x_own, axis=1) + jnp.sum(w_p * x_other, axis=1)
    along = along + swap_core(along)
    factor = mix_scale**3 * along[:, None] / D
    gt_own = gh_own + mix_scale * w_o - x_own * factor
    gt_other = gh_other + mix_scale * w_p - x_other * factor
    sends, _, _, take = background(None, None, (), 1, 2)
    if pairs:
        sends.append((swap_group, small))
    moved, _, _ = step([(up, out_a), (down, out_b), (swap_chip, gt_other.astype(bf16)), *sends])
    out_own = (h_own + moved[0].astype(f32) + un_own[0].astype(f32)).astype(bf16)
    out_other = (h_other + moved[1].astype(f32) + un_other[0].astype(f32)).astype(bf16)
    grad_other = moved[2].astype(f32)
    small = small + moved[-1] if pairs else lax.psum(small, "dp")
    take(moved[3:-1] if pairs else moved[3:], [])
    edge = 2 * width
    bound_sum = small[edge : edge + hc]
    wide = jnp.concatenate([small[:edge], small[edge + hc :]])
    near = lambda a: lax.ppermute(a, "col", [(i, i ^ 1) for i in range(count)])
    far = lambda a: lax.ppermute(a, "col", [(i, i ^ 2) for i in range(count)])
    sends, _, _, take = background(None, None, (), 1, 2)
    moved, _, _ = step([(swap_chip, out_other), (near, wide), *sends])
    out_other = moved[0]
    wide = wide + moved[1]
    take(moved[2:], [])
    while y_queue or x_queue:
        sends, _, _, take = background(None, None, (), 1, 2)
        moved, _, _ = step(sends) if sends else ([], [], [])
        take(moved, [])
    wide = wide + far(wide)
    turned = swap_core(jnp.concatenate([bound_sum, wide[edge:]]))
    grad_bound = joined(bound_sum, turned[:hc], core, 0)
    found = dict(x_done)

    def all_of(name, parts):
        return jnp.concatenate([found[f"{name}{n}"] for n in range(parts)], 0)

    return (
        joined(out_own, out_other, y, 0),
        joined(gt_own, grad_other, y, 0),
        wide[:width],
        jnp.stack([found["q0"], found["k0"], found["v0"], found["g0"]], 1),
        grad_bound,
        wide[edge:] + turned[hc:],
        found["o0"],
        wide[width:edge],
        all_of("f", 4).reshape(width, 2, units_col),
        all_of("d", 2),
    )


def solution(mesh):
    return jax.shard_map(
        shards,
        mesh=mesh,
        in_specs=(
            P(("dp", "col"), "row"),
            P("dp"),
            P("row"),
            P("row", None, "col"),
            P("col"),
            P(),
            P("col", "row"),
            P("row"),
            P("row", None, "col"),
            P("col", "row"),
            P(("dp", "col"), "row"),
        ),
        out_specs=(
            P(("dp", "col"), "row"),
            P(("dp", "col"), "row"),
            P("row"),
            P("row", None, "col"),
            P("col"),
            P(),
            P("col", "row"),
            P("row"),
            P("row", None, "col"),
            P("col", "row"),
        ),
        check_vma=False,
    )
```

time: 2000 us -> 626 us (0.31)
  waiting for transfers between devices: 1290 us -> 200 us
  other arithmetic: 272 us -> 57 us
  starting transfers between devices: 1.81 us -> 142 us
  local copies, waits for them, and re-layouts: 165 us -> 59.9 us
  blocking collectives: 94 us -> 0 us
  matrix products: 153 us -> 105 us
  Pallas kernels: 0 us -> 47.1 us
    psum x2 -> x0, waiting for transfers between devices: 539 us -> none  [the longest x1 392 us: shards(): both_all = lax.psum(local_both, 'row').reshape(span, 2, units_col)]
    reduce_scatter x7 -> x0, waiting for transfers between devices: 471 us -> none  [the longest x4 240 us: sum_cols(): lax.psum_scatter(contract_term(left, right, contract), 'col', scatter_dim...]
    all_gather x8 -> x0, waiting for transfers between devices: 279 us -> none  [the longest x4 160 us: gather_cols(): return lax.all_gather(local, 'col', axis=0, tiled=True)]
    ppermute x0 -> x108, waiting for transfers between devices: none -> 200 us  [the longest x24 90.4 us: up(): return lax.ppermute(x, 'col', UP)]
    ppermute x0 -> x108, starting transfers between devices: none -> 142 us  [the longest x24 83.6 us: down(): return lax.ppermute(x, 'col', DOWN)]
    psum x5 -> x0, blocking collectives: 76.4 us -> none  [the longest x1 46.5 us: shards(): lax.psum((full_mix, full_ffn, full_bound, group_part), ('dp', 'row', 'col'))]
    reduce_sum x25 -> x7, other arithmetic: 55.2 us -> 4.24 us  [the longest x1 2.22 us: shards(): ffn_part = jnp.sum(df_own * h_own * ffn_scale, axis=0)]
    dot_general x24 -> x52, matrix products: 153 us -> 105 us  [the longest x18 41.7 us: mm_tn(): lax.dot_general(left, right, (((0,), (0,)), ((), ())), preferred_element_...]
  transfers between devices with their start and end apart: 17 -> 108, of which waited for: 16 -> 63; matrix products, arithmetic and copies ran while one was open for 8% -> 24% of each run, Pallas kernels for 0% -> 7%
where the time goes in v2:
time: 626 us; the launch traced here: 617 us
  waiting for transfers between devices  200 us (32%)
  starting transfers between devices  142 us (23%)
  matrix products  105 us (17%)
  local copies, waits for them, and re-layouts  59.9 us (10%)
  other arithmetic  57 us (9%)
  Pallas kernels  47.1 us (8%)
    ppermute x24, waiting for transfers between devices, up(): return lax.ppermute(x, 'col', UP)  90.4 us
    ppermute x24, starting transfers between devices, down(): return lax.ppermute(x, 'col', DOWN)  83.6 us
    ppermute x32, waiting for transfers between devices, swap_chip(): return lax.ppermute(x, 'row', CHIP)  46.9 us
    dot_general x18, matrix products, mm_tn(): lax.dot_general(left, right, (((0,), (0,)), ((), ())), preferred_element_...  41.7 us
    ppermute x24, waiting for transfers between devices, down(): return lax.ppermute(x, 'col', DOWN)  38.4 us
    dot_general x20, matrix products, mm_nt(): lax.dot_general(left, right, (((1,), (1,)), ((), ())), preferred_element_...  35.8 us
    ppermute x32, starting transfers between devices, swap_chip(): return lax.ppermute(x, 'row', CHIP)  34.8 us
    dot_general x14, matrix products, mm(): lax.dot_general(left, right, (((1,), (0,)), ((), ())), preferred_element_...  27.7 us
  transfers between devices with their start and end apart: 108, of which 63 were waited for; matrix products, arithmetic and copies ran while one was open for 24% of the time, Pallas kernels for 7%

profile of v2, /device:TPU:0, one launch (start us, length us, event | category | flops | bytes accessed | tf_op | source)
XLA Modules:
  0.0 616.5 jit_solution(815256666114019299)
XLA Ops:
  21.1 5.5 collective-permute-done.3
  36.9 7.3 %collective-permute-done.7 = bf16[256,512]{1,0:T(8,128)(2,1)S(1)} collective-permute-done((bf16[256,512]{1,0:T(8,128)(2,1)S(1)}, bf16[256,512]{1,0:T(8,128)(2,1)S(1)}, u32[]{:S(2)}, u32[]{:S(2)}) %collective-permute-start.7) | collective-permute-done | bytes 262176 | tf_op jit(solution)/shard_map/ppermute | solution.py:397
  52.8 7.2 %collective-permute-done.10 = bf16[256,512]{1,0:T(8,128)(2,1)S(1)} collective-permute-done((bf16[256,512]{1,0:T(8,128)(2,1)S(1)}, bf16[256,512]{1,0:T(8,128)(2,1)S(1)}, u32[]{:S(2)}, u32[]{:S(2)}) %collective-permute-start.10) | collective-permute-done | bytes 262176 | tf_op jit(solution)/shard_map/ppermute | solution.py:397
  69.5 5.7 collective-permute-done.13
  98.5 14.7 %recurrence_local.1 = (f32[1024,256]{1,0:T(8,128)}, bf16[1024,256]{1,0:T(8,128)(2,1)}, bf16[1024,256]{1,0:T(8,128)(2,1)}, bf16[1024,256]{1,0:T(8,128)(2,1)}, f32...) custom-call(f32[1024,1024]{1,0:T(8,128)} %convolution_add_fusion.5.keep, ...), custom_call_target="tpu_custom_call" | custom-call | tf_op jit(solution)/shard_map/recurrence_local/pallas_call | solution.py:280
  116.3 5.2 collective-permute-done.21.peerd_ref
  128.6 5.6 recurrence_finish.1
  174.2 5.9 collective-permute-done.29
  205.6 7.2 %collective-permute-done.36 = bf16[256,512]{1,0:T(8,128)(2,1)S(1)} collective-permute-done((bf16[256,512]{1,0:T(8,128)(2,1)S(1)}, bf16[256,512]{1,0:T(8,128)(2,1)S(1)}, u32[]{:S(2)}, u32[]{:S(2)}) %collective-permute-start.36) | collective-permute-done | bytes 262176 | tf_op jit(solution)/shard_map/ppermute | solution.py:397
  223.3 5.8 collective-permute-done.39
  237.3 7.1 %collective-permute-done.42 = bf16[256,512]{1,0:T(8,128)(2,1)S(1)} collective-permute-done((bf16[256,512]{1,0:T(8,128)(2,1)S(1)}, bf16[256,512]{1,0:T(8,128)(2,1)S(1)}, u32[]{:S(2)}, u32[]{:S(2)}) %collective-permute-start.42) | collective-permute-done | bytes 262176 | tf_op jit(solution)/shard_map/ppermute | solution.py:397
  291.6 13.4 %conditional.3 = (f32[704,512]{1,0:T(8,128)S(1)}, f32[704,512]{1,0:T(8,128)S(1)}, bf16[128,2816]{1,0:T(8,128)(2,1)}, bf16[128,2816]{1,0:T(8,128)(2,1)S(1)}, bf16...) conditional(s32[]{:T(128)} %bitcast.15, () %tuple.150, (bf16[512,1408]{1,0:T(8,128)(2,1)}, ...), branch_computations={%region_4.5_spmd, %region_5.6_spmd} | conditional | flops 4432789504 | bytes 45350960 | solution.py:421
  315.7 7.2 %collective-permute-done.52 = bf16[256,512]{1,0:T(8,128)(2,1)S(1)} collective-permute-done((bf16[256,512]{1,0:T(8,128)(2,1)S(1)}, bf16[256,512]{1,0:T(8,128)(2,1)S(1)}, u32[]{:S(2)}, u32[]{:S(2)}) %collective-permute-start.52) | collective-permute-done | bytes 262176 | tf_op jit(solution)/shard_map/ppermute | solution.py:397
  332.1 7.8 %conditional.5 = (f32[128,2816]{1,0:T(8,128)S(1)}, f32[128,2816]{1,0:T(8,128)S(1)}, f32[128,2816]{1,0:T(8,128)S(1)}, f32[128,2816]{1,0:T(8,128)S(1)}) conditional(s32[]{:T(128)} %bitcast.15, () %tuple.157, (bf16[512,512]{1,0:T(8,128)(2,1)S(1)}, bf16[512,2816]{1,0:T(8,128)(2,1)}, bf16[512,512]{1,0:T(8,128)(2,1)S(1)}, ...), branch_computations={%region_10.11_spmd, %region_11.12_spmd} | conditional | flops 2954231808 | bytes 35651616 | solution.py:421
  346.6 9.6 %conditional.4 = (bf16[256,512]{1,0:T(8,128)(2,1)S(1)}, bf16[256,512]{1,0:T(8,128)(2,1)S(1)}, bf16[256,512]{1,0:T(8,128)(2,1)S(1)}, bf16[256,512]{1,0:T(8,128)(2...) conditional(s32[]{:T(128)} %bitcast.15, () %tuple.139, ...), branch_computations={%region_6.7_spmd, %region_7.8_spmd} | conditional | flops 2953838592 | bytes 17825856 | solution.py:421
  371.8 5.3 collective-permute-done.61
  394.8 7.4 %collective-permute-done.67 = bf16[128,2816]{1,0:T(8,128)(2,1)S(1)} collective-permute-done((bf16[128,2816]{1,0:T(8,128)(2,1)S(1)}, bf16[128,2816]{1,0:T(8,128)(2,1)S(1)}, u32[]{:S(2)}, u32[]{:S(2)}) %collective-permute-start.67) | collective-permute-done | bytes 720928 | tf_op jit(solution)/shard_map/ppermute | solution.py:28
  414.7 7.4 %collective-permute-done.71 = bf16[128,2816]{1,0:T(8,128)(2,1)S(1)} collective-permute-done((bf16[128,2816]{1,0:T(8,128)(2,1)S(1)}, bf16[128,2816]{1,0:T(8,128)(2,1)S(1)}, u32[]{:S(2)}, u32[]{:S(2)}) %collective-permute-start.71) | collective-permute-done | bytes 720928 | tf_op jit(solution)/shard_map/ppermute | solution.py:28
  433.8 5.2 recurrence_back_local.1
  460.9 17.5 %recurrence_back_finish.1 = (bf16[1024,768]{1,0:T(8,128)(2,1)}, f32[1,256]{1,0:T(1,128)}) custom-call(f32[1024,1024]{1,0:T(8,128)} %convolution_add_fusion.5.keep_ref, bf16[1024,1024]{1,0:T(8,128)(2,1)} %copy-done, f32[1,256]{1,0:T(1,128)} %bitcast.171, f32[1024,1]{1,0:T(8,128)} %bitcast.132, f32[4,1,256]{2,1,0:T(1,128)} %reshape.97.idr_ref, ...), custom_call_target="tpu_custom_call" | custom-call | tf_op jit(solution)/shard_map/recurrence_back_finish/pallas_call | solution.py:376
  514.9 7.8 %reshape.102 = f32[512,2,1408]{2,1,0:T(2,128)} reshape(f32[512,2816]{1,0:T(8,128)} %pad_maximum_fusion) | data formatting | bytes 11534336 | tf_op jit(solution)/shard_map/reshape | solution.py:823
  542.8 5.4 collective-permute-done.86
  560.7 6.4 %collective-permute-done.90 = bf16[256,512]{1,0:T(8,128)(2,1)S(1)} collective-permute-done((bf16[256,512]{1,0:T(8,128)(2,1)S(1)}, bf16[256,512]{1,0:T(8,128)(2,1)S(1)}, u32[]{:S(2)}, u32[]{:S(2)}) %collective-permute-start.90) | collective-permute-done | bytes 262176 | tf_op jit(solution)/shard_map/ppermute | solution.py:397
  568.8 6.5 %collective-permute-done.94 = bf16[512,512]{1,0:T(8,128)(2,1)S(1)} collective-permute-done((bf16[512,512]{1,0:T(8,128)(2,1)S(1)}, bf16[512,512]{1,0:T(8,128)(2,1)S(1)}, u32[]{:S(2)}, u32[]{:S(2)}) %collective-permute-start.94) | collective-permute-done | bytes 524320 | tf_op jit(solution)/shard_map/ppermute | solution.py:393
  (804 shorter events, 457.8 us)
Async XLA Ops:
  13.0 19.6 %collective-permute-start.6 = (bf16[128,4,512]{2,1,0:T(4,128)(2,1)S(1)}, bf16[128,4,512]{2,1,0:T(4,128)(2,1)S(1)}, u32[]{:S(2)}, u32[]{:S(2)}) collective-permute-start(bf16[128,4,512]{2,1,0:T(4,128)(2,1)S(1)} %get-tuple-element.399), channel_id=1, source_target_pairs={{0,8},{8,0},{4,12},{12,4},{1,9},{9,1},{5,13},{13,5},{2,10},{10,2},... | collective-permute-start | bytes 1572872 | tf_op jit(solution)/shard_map/ppermute | solution.py:28
  89.5 23.7 %collective-permute-start.19 = (bf16[512,512]{1,0:T(8,128)(2,1)}, bf16[512,512]{1,0:T(8,128)(2,1)}, u32[]{:S(2)}, u32[]{:S(2)}) collective-permute-start(bf16[512,512]{1,0:T(8,128)(2,1)} %param.23), channel_id=1, source_target_pairs={{0,8},{8,0},{4,12},{12,4},{1,9},{9,1},{5,13},{13,5},{2,10},{10,2},... | collective-permute-start | bytes 1572872 | tf_op jit(solution)/shard_map/ppermute | solution.py:28
  91.1 22.1 %collective-permute-start.17 = (bf16[256,512]{1,0:T(8,128)(2,1)}, bf16[256,512]{1,0:T(8,128)(2,1)}, u32[]{:S(2)}, u32[]{:S(2)}) collective-permute-start(bf16[256,512]{1,0:T(8,128)(2,1)} %collective-permute-done.13), channel_id=1, source_target_pairs={{0,1},{1,2},{2,3},{3,0},{4,5},{5,6},{6,7},{7,4},{8,9},{9,10},{10,1... | collective-permute-start | bytes 786440 | tf_op jit(solution)/shard_map/ppermute | solution.py:397
  91.5 21.7 %collective-permute-start.18 = (bf16[256,512]{1,0:T(8,128)(2,1)}, bf16[256,512]{1,0:T(8,128)(2,1)}, u32[]{:S(2)}, u32[]{:S(2)}) collective-permute-start(bf16[256,512]{1,0:T(8,128)(2,1)} %collective-permute-done.14), channel_id=1, source_target_pairs={{1,0},{2,1},{3,2},{0,3},{5,4},{6,5},{7,6},{4,7},{9,8},{10,9},{11,1... | collective-permute-start | bytes 786440 | tf_op jit(solution)/shard_map/ppermute | solution.py:401
  146.6 18.5 %collective-permute-start.28 = (bf16[704,512]{1,0:T(8,128)(2,1)}, bf16[704,512]{1,0:T(8,128)(2,1)}, u32[]{:S(2)}, u32[]{:S(2)}) collective-permute-start(bf16[704,512]{1,0:T(8,128)(2,1)} %get-tuple-element.467), channel_id=1, source_target_pairs={{0,8},{8,0},{4,12},{12,4},{1,9},{9,1},{5,13},{13,5},{2,10},{10,2},... | collective-permute-start | bytes 2162696 | tf_op jit(solution)/shard_map/ppermute | solution.py:28
  199.2 23.0 %collective-permute-start.45 = (bf16[512,1408]{1,0:T(8,128)(2,1)S(1)}, bf16[512,1408]{1,0:T(8,128)(2,1)S(1)}, u32[]{:S(2)}, u32[]{:S(2)}) collective-permute-start(bf16[512,1408]{1,0:T(8,128)(2,1)S(1)} %fusion.1), channel_id=1, source_target_pairs={{0,4},{4,0},{8,12},{12,8},{1,5},{5,1},{9,13},{13,9},{2,6},{6,2},{1... | collective-permute-start | bytes 4325384 | tf_op jit(solution)/shard_map/ppermute | solution.py:24
  284.7 20.3 %collective-permute-start.51 = (bf16[704,512]{1,0:T(8,128)(2,1)}, bf16[704,512]{1,0:T(8,128)(2,1)}, u32[]{:S(2)}, u32[]{:S(2)}) collective-permute-start(bf16[704,512]{1,0:T(8,128)(2,1)} %get-tuple-element.509), channel_id=1, source_target_pairs={{0,8},{8,0},{4,12},{12,4},{1,9},{9,1},{5,13},{13,5},{2,10},{10,2},... | collective-permute-start | bytes 2162696 | tf_op jit(solution)/shard_map/ppermute | solution.py:28
  285.9 19.2 %collective-permute-start.49 = (bf16[256,512]{1,0:T(8,128)(2,1)}, bf16[256,512]{1,0:T(8,128)(2,1)S(1)}, u32[]{:S(2)}, u32[]{:S(2)}) collective-permute-start(bf16[256,512]{1,0:T(8,128)(2,1)} %broadcast_select_fusion.5), channel_id=1, source_target_pairs={{0,1},{1,2},{2,3},{3,0},{4,5},{5,6},{6,7},{7,4},{8,9},{9,10},{10,1... | collective-permute-start | bytes 786440 | tf_op jit(solution)/shard_map/ppermute | solution.py:397
  286.2 18.8 %collective-permute-start.50 = (bf16[256,512]{1,0:T(8,128)(2,1)}, bf16[256,512]{1,0:T(8,128)(2,1)}, u32[]{:S(2)}, u32[]{:S(2)}) collective-permute-start(bf16[256,512]{1,0:T(8,128)(2,1)} %broadcast_select_fusion.1), channel_id=1, source_target_pairs={{1,0},{2,1},{3,2},{0,3},{5,4},{6,5},{7,6},{4,7},{9,8},{10,9},{11,1... | collective-permute-start | bytes 786440 | tf_op jit(solution)/shard_map/ppermute | solution.py:401
  309.4 17.4 %collective-permute-start.54 = (bf16[704,512]{1,0:T(8,128)(2,1)S(1)}, bf16[704,512]{1,0:T(8,128)(2,1)S(1)}, u32[]{:S(2)}, u32[]{:S(2)}) collective-permute-start(bf16[704,512]{1,0:T(8,128)(2,1)S(1)} %copy-done.140), channel_id=1, source_target_pairs={{0,8},{8,0},{4,12},{12,4},{1,9},{9,1},{5,13},{13,5},{2,10},{10,2},... | collective-permute-start | bytes 2162696 | tf_op jit(solution)/shard_map/ppermute | solution.py:28
  310.4 17.2 %collective-permute-start.55 = (bf16[704,512]{1,0:T(8,128)(2,1)S(1)}, bf16[704,512]{1,0:T(8,128)(2,1)}, u32[]{:S(2)}, u32[]{:S(2)}) collective-permute-start(bf16[704,512]{1,0:T(8,128)(2,1)S(1)} %add_convert_fusion.8), channel_id=1, source_target_pairs={{0,16},{16,0},{1,17},{17,1},{2,18},{18,2},{3,19},{19,3},{4,20},{20... | collective-permute-start | bytes 2162696 | tf_op jit(solution)/shard_map/ppermute | solution.py:393
  329.4 27.6 %collective-permute-start.58 = (bf16[128,2816]{1,0:T(8,128)(2,1)}, bf16[128,2816]{1,0:T(8,128)(2,1)}, u32[]{:S(2)}, u32[]{:S(2)}) collective-permute-start(bf16[128,2816]{1,0:T(8,128)(2,1)} %get-tuple-element.541), channel_id=1, source_target_pairs={{0,8},{8,0},{4,12},{12,4},{1,9},{9,1},{5,13},{13,5},{2,10},{10,2},... | collective-permute-start | bytes 2162696 | tf_op jit(solution)/shard_map/ppermute | solution.py:28
  330.6 26.4 %collective-permute-start.59 = (bf16[704,512]{1,0:T(8,128)(2,1)S(1)}, bf16[704,512]{1,0:T(8,128)(2,1)}, u32[]{:S(2)}, u32[]{:S(2)}) collective-permute-start(bf16[704,512]{1,0:T(8,128)(2,1)S(1)} %add_convert_fusion.7), channel_id=1, source_target_pairs={{0,16},{16,0},{1,17},{17,1},{2,18},{18,2},{3,19},{19,3},{4,20},{20... | collective-permute-start | bytes 2162696 | tf_op jit(solution)/shard_map/ppermute | solution.py:393
  362.5 18.4 %collective-permute-start.63 = (bf16[128,2816]{1,0:T(8,128)(2,1)S(1)}, bf16[128,2816]{1,0:T(8,128)(2,1)S(1)}, u32[]{:S(2)}, u32[]{:S(2)}) collective-permute-start(bf16[128,2816]{1,0:T(8,128)(2,1)S(1)} %copy-done.135), channel_id=1, source_target_pairs={{0,8},{8,0},{4,12},{12,4},{1,9},{9,1},{5,13},{13,5},{2,10},{10,2},... | collective-permute-start | bytes 2162696 | tf_op jit(solution)/shard_map/ppermute | solution.py:28
  363.5 18.0 %collective-permute-start.64 = (bf16[128,2816]{1,0:T(8,128)(2,1)S(1)}, bf16[128,2816]{1,0:T(8,128)(2,1)S(1)}, u32[]{:S(2)}, u32[]{:S(2)}) collective-permute-start(bf16[128,2816]{1,0:T(8,128)(2,1)S(1)} %add_convert_fusion.6), channel_id=1, source_target_pairs={{0,16},{16,0},{1,17},{17,1},{2,18},{18,2},{3,19},{19,3},{4,20},{20... | collective-permute-start | bytes 2162696 | tf_op jit(solution)/shard_map/ppermute | solution.py:393
  447.8 34.1 %collective-permute-start.76 = (bf16[256,512]{1,0:T(8,128)(2,1)}, bf16[256,512]{1,0:T(8,128)(2,1)}, u32[]{:S(2)}, u32[]{:S(2)}) collective-permute-start(bf16[256,512]{1,0:T(8,128)(2,1)} %broadcast_select_fusion.4), channel_id=1, source_target_pairs={{0,1},{1,2},{2,3},{3,0},{4,5},{5,6},{6,7},{7,4},{8,9},{9,10},{10,1... | collective-permute-start | bytes 786440 | tf_op jit(solution)/shard_map/ppermute | solution.py:397
  447.8 34.1 %collective-permute-start.77 = (bf16[256,512]{1,0:T(8,128)(2,1)}, bf16[256,512]{1,0:T(8,128)(2,1)}, u32[]{:S(2)}, u32[]{:S(2)}) collective-permute-start(bf16[256,512]{1,0:T(8,128)(2,1)} %broadcast_select_fusion), channel_id=1, source_target_pairs={{1,0},{2,1},{3,2},{0,3},{5,4},{6,5},{7,6},{4,7},{9,8},{10,9},{11,1... | collective-permute-start | bytes 786440 | tf_op jit(solution)/shard_map/ppermute | solution.py:401
  451.7 30.3 %collective-permute-start.78 = (bf16[512,512]{1,0:T(8,128)(2,1)}, bf16[512,512]{1,0:T(8,128)(2,1)}, u32[]{:S(2)}, u32[]{:S(2)}) collective-permute-start(bf16[512,512]{1,0:T(8,128)(2,1)} %convolution_convert_fusion.14), channel_id=1, source_target_pairs={{0,8},{8,0},{4,12},{12,4},{1,9},{9,1},{5,13},{13,5},{2,10},{10,2},... | collective-permute-start | bytes 1572872 | tf_op jit(solution)/shard_map/ppermute | solution.py:28
  452.8 29.1 %collective-permute-start.79 = (bf16[128,2816]{1,0:T(8,128)(2,1)}, bf16[128,2816]{1,0:T(8,128)(2,1)}, u32[]{:S(2)}, u32[]{:S(2)}) collective-permute-start(bf16[128,2816]{1,0:T(8,128)(2,1)} %add_convert_fusion.3), channel_id=1, source_target_pairs={{0,16},{16,0},{1,17},{17,1},{2,18},{18,2},{3,19},{19,3},{4,20},{20... | collective-permute-start | bytes 2162696 | tf_op jit(solution)/shard_map/ppermute | solution.py:393
  503.8 21.6 %collective-permute-start.83 = (bf16[512,512]{1,0:T(8,128)(2,1)}, bf16[512,512]{1,0:T(8,128)(2,1)}, u32[]{:S(2)}, u32[]{:S(2)}) collective-permute-start(bf16[512,512]{1,0:T(8,128)(2,1)} %convolution_convert_fusion.13), channel_id=1, source_target_pairs={{0,8},{8,0},{4,12},{12,4},{1,9},{9,1},{5,13},{13,5},{2,10},{10,2},... | collective-permute-start | bytes 1572872 | tf_op jit(solution)/shard_map/ppermute | solution.py:28
  504.7 25.0 %collective-permute-start.84 = (bf16[512,512]{1,0:T(8,128)(2,1)}, bf16[512,512]{1,0:T(8,128)(2,1)}, u32[]{:S(2)}, u32[]{:S(2)}) collective-permute-start(bf16[512,512]{1,0:T(8,128)(2,1)} %convolution_convert_fusion.12), channel_id=1, source_target_pairs={{0,8},{8,0},{4,12},{12,4},{1,9},{9,1},{5,13},{13,5},{2,10},{10,2},... | collective-permute-start | bytes 1572872 | tf_op jit(solution)/shard_map/ppermute | solution.py:28
  505.8 23.8 %collective-permute-start.85 = (bf16[512,512]{1,0:T(8,128)(2,1)}, bf16[512,512]{1,0:T(8,128)(2,1)}, u32[]{:S(2)}, u32[]{:S(2)}) collective-permute-start(bf16[512,512]{1,0:T(8,128)(2,1)} %fusion.5), channel_id=1, source_target_pairs={{0,16},{16,0},{1,17},{17,1},{2,18},{18,2},{3,19},{19,3},{4,20},{20... | collective-permute-start | bytes 1572872 | tf_op jit(solution)/shard_map/ppermute | solution.py:393
  551.1 17.7 %collective-permute-start.92 = (bf16[512,512]{1,0:T(8,128)(2,1)S(1)}, bf16[512,512]{1,0:T(8,128)(2,1)S(1)}, u32[]{:S(2)}, u32[]{:S(2)}) collective-permute-start(bf16[512,512]{1,0:T(8,128)(2,1)S(1)} %convolution_convert_fusion.10), channel_id=1, source_target_pairs={{0,8},{8,0},{4,12},{12,4},{1,9},{9,1},{5,13},{13,5},{2,10},{10,2},... | collective-permute-start | bytes 1572872 | tf_op jit(solution)/shard_map/ppermute | solution.py:28
  552.9 22.5 %collective-permute-start.94 = (bf16[512,512]{1,0:T(8,128)(2,1)S(1)}, bf16[512,512]{1,0:T(8,128)(2,1)S(1)}, u32[]{:S(2)}, u32[]{:S(2)}) collective-permute-start(bf16[512,512]{1,0:T(8,128)(2,1)S(1)} %fusion.7), channel_id=1, source_target_pairs={{0,16},{16,0},{1,17},{17,1},{2,18},{18,2},{3,19},{19,3},{4,20},{20... | collective-permute-start | bytes 1572872 | tf_op jit(solution)/shard_map/ppermute | solution.py:393
  (284 other events, 2866.2 us)

commit v3 on v2

--- a/solution.py
+++ b/solution.py
@@ -16,8 +16,6 @@
 
 CORE = [(0, 1), (1, 0), (2, 3), (3, 2)]
 CHIP = [(0, 2), (2, 0), (1, 3), (3, 1)]
-UP = [(0, 1), (1, 2), (2, 3), (3, 0)]
-DOWN = [(1, 0), (2, 1), (3, 2), (0, 3)]
 
 
 def swap_core(x):
@@ -130,7 +128,7 @@
     peer_first = (y == 0) if reverse else (y == 1)
     state = [jnp.zeros((HD, HD), f32)] * heads
     for place in reversed(range(count)) if reverse else range(count):
-        k = lax.rem(z - place + count, count)
+        k = lax.rem((z ^ (z >> 1)) - (place ^ (place >> 1)) + count, count)
         for h in range(heads):
             add = peer_ref[k, h].astype(f32)
             scale = peerd_ref[k, :, col(h)]
@@ -389,16 +387,184 @@
     )(keep, recv, bound, *ids, qh, kh, vb, decay, states, do, enter)
 
 
+def weight_kernel(pairs, *refs):
+    lefts, rights = refs[:pairs], refs[pairs : 2 * pairs]
+    *plus, out = refs[2 * pairs :]
+    total = sum(mm_tn(left[...], right[...]) for left, right in zip(lefts, rights))
+    out[...] = (total + sum(part[...].astype(f32) for part in plus)).astype(out.dtype)
+
+
+def weight_gradients(lefts, rights, plus=(), rows=None, columns=None, tile=256):
+    at, tall = rows or (0, lefts[0].shape[1])
+    first, wide = columns or (0, rights[0].shape[1])
+    tiles = wide // tile
+    out = pl.BlockSpec((tall, tile), lambda j: (0, j))
+    return pl.pallas_call(
+        partial(weight_kernel, len(lefts)),
+        grid=(tiles,),
+        in_specs=[pl.BlockSpec((left.shape[0], tall), lambda j: (0, at)) for left in lefts]
+        + [pl.BlockSpec((r.shape[0], tile), lambda j: (0, first * tiles + j)) for r in rights]
+        + [out] * len(plus),
+        out_specs=out,
+        out_shape=shape((tall, wide), bf16),
+        cost_estimate=COST,
+        name="weight_gradients",
+    )(*lefts, *rights, *plus)
+
+
+def pieces_kernel(pairs, *refs):
+    lefts, rights, outs = refs[:pairs], refs[pairs : 2 * pairs], refs[2 * pairs :]
+    total = sum(mm_tn(left[...], right[...]) for left, right in zip(lefts, rights))
+    each = outs[0].shape[0]
+    for n, out in enumerate(outs):
+        out[...] = total[n * each : (n + 1) * each].astype(out.dtype)
+
+
+def weight_gradient_pieces(lefts, rights, kind, pieces, tile=256):
+    tall, wide = lefts[0].shape[1] // pieces, rights[0].shape[1]
+    return pl.pallas_call(
+        partial(pieces_kernel, len(lefts)),
+        grid=(wide // tile,),
+        in_specs=[whole(*left.shape) for left in lefts]
+        + [pl.BlockSpec((right.shape[0], tile), lambda j: (0, j)) for right in rights],
+        out_specs=[pl.BlockSpec((tall, tile), lambda j: (0, j))] * pieces,
+        out_shape=[shape((tall, wide), kind)] * pieces,
+        cost_estimate=COST,
+        name="weight_gradient_pieces",
+    )(*lefts, *rights)
+
+
+def sum_kernel(own_ref, got_ref, out_ref):
+    out_ref[...] = (own_ref[...] + got_ref[...].astype(f32)).astype(bf16)
+
+
+def rounded_sum(own, got):
+    return pl.pallas_call(
+        sum_kernel,
+        in_specs=[VMEM] * 2,
+        out_specs=VMEM,
+        out_shape=shape(own.shape, bf16),
+        cost_estimate=COST,
+        name="rounded_sum",
+    )(own, got)
+
+
+def halves_kernel(pieces, *refs):
+    *given, out_ref = refs
+    each = len(given) // pieces
+    wide = out_ref.shape[2]
+    rows = out_ref.shape[0]
+    for n in range(pieces):
+
+        @pl.when(pl.program_id(0) == n)
+        def _():
+            at = pl.ds(pl.multiple_of(pl.program_id(1) * rows, rows), rows)
+            for part in range(out_ref.shape[1]):
+                cols = slice(part * wide, (part + 1) * wide)
+                value = sum(ref[at, cols].astype(f32) for ref in given[n * each : (n + 1) * each])
+                out_ref[:, part, :] = value
+
+
+def halves_of_rows(pieces, parts, rows=32):
+    tall, wide = pieces[0][0].shape
+    steps = tall // rows
+    given = [array for piece in pieces for array in piece]
+    return pl.pallas_call(
+        partial(halves_kernel, len(pieces)),
+        grid=(len(pieces), steps),
+        in_specs=[pl.BlockSpec(a.shape, lambda n, j: (0, 0)) for a in given],
+        out_specs=pl.BlockSpec((rows, parts, wide // parts), lambda n, j: (n * steps + j, 0, 0)),
+        out_shape=shape((len(pieces) * tall, parts, wide // parts), f32),
+        cost_estimate=COST,
+        compiler_params=pltpu.CompilerParams(vmem_limit_bytes=40 * 2**20),
+        name="halves_of_rows",
+    )(*given)
+
+
+def stack_kernel(parts, *refs):
+    *given, out_ref = refs
+    each = len(given) // parts
+    for part in range(parts):
+        out_ref[:, part, :] = sum(
+            ref[...].astype(f32) for ref in given[part * each : (part + 1) * each]
+        )
+
+
+def stacked(parts, rows=64):
+    tall, wide = parts[0][0].shape
+    given = [array for part in parts for array in part]
+    return pl.pallas_call(
+        partial(stack_kernel, len(parts)),
+        grid=(tall // rows,),
+        in_specs=[pl.BlockSpec((rows, wide), lambda j: (j, 0))] * len(given),
+        out_specs=pl.BlockSpec((rows, len(parts), wide), lambda j: (j, 0, 0)),
+        out_shape=shape((tall, len(parts), wide), f32),
+        cost_estimate=COST,
+        name="stacked",
+    )(*given)
+
+
+def product_kernel(right_ref, *refs):
+    lefts, outs = refs[: len(refs) // 2], refs[len(refs) // 2 :]
+    for left, out in zip(lefts, outs):
+        out[...] = mm(left[...], right_ref[...]).astype(out.dtype)
+
+
+def products(lefts, right, tile=256):
+    wide = right.shape[1]
+    return pl.pallas_call(
+        product_kernel,
+        grid=(wide // tile,),
+        in_specs=[pl.BlockSpec((right.shape[0], tile), lambda j: (0, j))]
+        + [whole(*left.shape) for left in lefts],
+        out_specs=[pl.BlockSpec((left.shape[0], tile), lambda j: (0, j)) for left in lefts],
+        out_shape=[shape((left.shape[0], wide), bf16) for left in lefts],
+        cost_estimate=COST,
+        name="products",
+    )(right, *lefts)
+
+
+def heads_kernel(core_ref, left_ref, own_ref, peer_ref, *refs):
+    *plus, out_ref = refs
+    half = own_ref.shape[1]
+    core = core_ref[0]
+    for right_ref, at in ((own_ref, core), (peer_ref, 1 - core)):
+        cols = pl.ds(pl.multiple_of(at * half, half), half)
+        total = mm_tn(left_ref[...], right_ref[...])
+        for part in plus:
+            total = total + part[:, cols].astype(f32)
+        out_ref[:, cols] = total.astype(out_ref.dtype)
+
+
+def head_gradients(core, left, own, peer, part, half, kind, plus=()):
+    block = pl.BlockSpec((own.shape[0], half), lambda j: (0, part))
+    out = whole(left.shape[1], 2 * half)
+    return pl.pallas_call(
+        heads_kernel,
+        grid=(1,),
+        in_specs=[SMEM, whole(*left.shape), block, block] + [out] * len(plus),
+        out_specs=out,
+        out_shape=shape((left.shape[1], 2 * half), kind),
+        cost_estimate=COST,
+        name="head_gradients",
+    )(core, left, own, peer, *plus)
+
+
 def swap_group(x):
     return lax.ppermute(x, "dp", [(0, 1), (1, 0)])
 
 
+def folded(place):
+    return place ^ (place >> 1)
+
+
 def up(x):
-    return lax.ppermute(x, "col", UP)
-
-
-def down(x):
-    return lax.ppermute(x, "col", DOWN)
+    count = lax.axis_size("col")
+    return lax.ppermute(x, "col", [(folded(n), folded((n + 1) % count)) for n in range(count)])
+
+
+def paired(own, other):
+    return jnp.concatenate([own, other], 1)
 
 
 def step(sends, work=None, given=(), join=()):
@@ -406,28 +572,16 @@
     arrays = lax.optimization_barrier((*(array for _, array in sends), *given))
     moved = [mover(array) for (mover, _), array in zip(sends, arrays)]
     made = tuple(work(*arrays[n:])) if work else ()
-    ends = made[:1] if getattr(work, "marked", False) else made
-    done = lax.optimization_barrier((*moved, *ends, *join))
-    made = made[1:] if getattr(work, "marked", False) else done[n : n + len(made)]
-    return list(done[:n]), list(made), list(done[n + len(ends) :])
-
-
-def aside(ready, work):
-    def marked(*given):
-        return (jnp.ones((), f32), *work(*given))
-
-    def run(*given):
-        shapes = jax.eval_shape(marked, *given)
-        return lax.cond(
-            ready, marked, lambda *a: tuple(jnp.zeros(s.shape, s.dtype) for s in shapes), *given
-        )
-
-    run.marked = True
-    return run
-
-
-def ordered(own, other):
-    return jnp.concatenate(own, 0), jnp.concatenate([other[0], *other[:0:-1]], 0)
+    done = lax.optimization_barrier((*moved, *made, *join))
+    return list(done[:n]), list(done[n : n + len(made)]), list(done[n + len(made) :])
+
+
+def ordered(runs):
+    width = runs[0].shape[1] // 2
+    return (
+        jnp.concatenate([run[:, :width] for run in runs], 0),
+        jnp.concatenate([run[:, width:] for run in runs], 0),
+    )
 
 
 def cut(array, count):
@@ -461,7 +615,6 @@
     units_col = w_down.shape[0]
     here = count * half
     hb = here // 2
-    ready = segments[0] >= 0
 
     def mine(x, at, size, axis):
         return lax.dynamic_slice_in_dim(x, at * size, size, axis)
@@ -489,28 +642,25 @@
     squares = jnp.sum(x_own * x_own, axis=1) + jnp.sum(x_other * x_other, axis=1)
     squares = squares + swap_core(squares)
     mix_scale = lax.rsqrt(squares / D + norm_eps)[:, None]
-    mo = [(x_own * mix_scale * mix_gain).astype(bf16)]
-    mp = [(x_other * mix_scale * gains_other[0]).astype(bf16)]
+    m = [
+        paired(x_own * mix_scale * mix_gain, x_other * mix_scale * gains_other[0]).astype(bf16)
+    ]
     wm = [first]
     for k in range(1, count):
-        sends = [(up, mo[-1]), (down, mp[-1])]
-        sends.append((swap_chip, cot_send if k == 1 else wm_parts[k - 1]))
-        (a, b, got), _, late = step(sends, join=wm if k == 1 else [])
+        sends = [(up, m[-1]), (swap_chip, cot_send if k == 1 else wm_parts[k - 1])]
+        (a, got), _, late = step(sends, join=wm if k == 1 else [])
         if k == 1:
             wm, cot_other = late, got
         else:
             wm.append(got)
-        mo.append(a)
-        mp.append(b)
-    co, cp = [cot_own], [cot_other]
-    (a, b, got, mo[-1], mp[-1]), _, _ = step(
-        [(up, cot_own), (down, cot_other), (swap_chip, wm_parts[3])]
-        + [(lambda v: v, mo[-1]), (lambda v: v, mp[-1])]
-    )
-    co.append(a)
-    cp.append(b)
+        m.append(a)
+    c = [paired(cot_own, cot_other)]
+    (a, got, m[-1]), _, _ = step(
+        [(up, c[0]), (swap_chip, wm_parts[3]), (lambda v: v, m[-1])]
+    )
+    c.append(a)
     wm_other = jnp.concatenate([*wm, got], 0)
-    m_own, m_other = ordered(mo, mp)
+    m_own, m_other = ordered(m)
 
     def columns(w, at):
         return mine(w, at, hc, 2).reshape(width, 4 * hc)
@@ -523,7 +673,7 @@
 
     def runs_of(array):
         array = lax.dynamic_index_in_dim(array.reshape(count, 2, half), y, 1, keepdims=False)
-        places = [(z - k + count) % count for k in range(count)]
+        places = [folded((folded(z) - k + count) % count) for k in range(count)]
         return jnp.stack(
             [lax.dynamic_index_in_dim(array, at, 0, keepdims=False) for at in places]
         )
@@ -539,13 +689,12 @@
     keep = mm(m_own, wm_keep) + mm(m_other, wm_keep_o)
     wf = w_ffn_in.reshape(width, 2 * units_col)
     pieces = cut(w_down, 2) + cut(wf, 5)
-    (a, b, wo_o), local, _ = step(
-        [(up, co[-1]), (down, cp[-1]), (swap_chip, w_out)],
+    (a, wo_o), local, _ = step(
+        [(up, c[-1]), (swap_chip, w_out)],
         lambda keep, recv: recurrence_local(keep, recv, bound, ids),
         (keep, recv),
     )
-    co.append(a)
-    cp.append(b)
+    c.append(a)
     *local, seg, low, decay = local
     (peer, peer_decay), _, _ = step([(swap_chip, low), (swap_chip, decay)])
 
@@ -553,36 +702,36 @@
         enter = recurrence_enter(place, seg, decay, peer, peer_decay, False)
         return recurrence_finish(local, enter, keep, recv, gain_row)
 
-    (a, b, got), (gated, rec, states), _ = step(
-        [(up, co[-1]), (down, cp[-1]), (swap_chip, pieces[0])],
+    (a, got), (gated, rec, states), _ = step(
+        [(up, c[-1]), (swap_chip, pieces[0])],
         finish,
         (seg, decay, peer, peer_decay),
     )
-    co.append(a)
-    cp.append(b)
+    c.append(a)
     weights = [got]
-    c_own, c_other = ordered(co, cp)
+    c_own, c_other = ordered(c)
     gated = joined(gated, swap_core(gated), core, 1)
 
     def scatter(own, other, beside):
-        a, b = own[1], other[-1]
+        sent = paired(own[1], other[1]).astype(bf16)
         for k in range(1, count):
             sends, work, given, take = beside(k)
-            moved, made, _ = step([(up, a.astype(bf16)), (down, b.astype(bf16)), *sends], work, given)
-            a = moved[0].astype(f32) + own[(k + 1) % count].astype(f32)
-            b = moved[1].astype(f32) + other[-(k + 1) % count].astype(f32)
-            take(moved[2:], made)
+            moved, made, _ = step([(up, sent), *sends], work, given)
+            at = (k + 1) % count
+            a = moved[0][:, :width].astype(f32) + own[at].astype(f32)
+            b = moved[0][:, width:].astype(f32) + other[at].astype(f32)
+            sent = paired(a, b).astype(bf16)
+            take(moved[1:], made)
         return a, b
 
     def gather(own, other, beside):
-        own, other = [own], [other]
+        runs = [paired(own, other)]
         for k in range(1, count):
             sends, work, given, take = beside(k)
-            moved, made, _ = step([(up, own[-1]), (down, other[-1]), *sends], work, given)
-            own.append(moved[0])
-            other.append(moved[1])
-            take(moved[2:], made)
-        return ordered(own, other)
+            moved, made, _ = step([(up, runs[-1]), *sends], work, given)
+            runs.append(moved[0])
+            take(moved[1:], made)
+        return ordered(runs)
 
     def weights_step(k):
         return [(swap_chip, pieces[len(weights)])], None, (), lambda moved, made: weights.extend(moved)
@@ -623,7 +772,12 @@
     df_sent = [mm_nt(gb_p, wf).astype(bf16), mm_nt(gb_p, wf_o).astype(bf16)]
     ck_own, cs_own = rows(c_own, core), rows(c_own, 1 - core)
     ck_other, cs_other = rows(c_other, core), rows(c_other, 1 - core)
-    down_sent = cut((mm_tn(units, ck_other) + mm_tn(units_p, cs_other)).astype(bf16), 2)
+    wide = width // 2
+    down_sent = [
+        (mm_tn(units, ck_other[:, at : at + wide]) + mm_tn(units_p, cs_other[:, at : at + wide]))
+        .astype(bf16)
+        for at in (0, wide)
+    ]
 
     def by_core(kept, sent):
         each = count // 2
@@ -633,73 +787,82 @@
             parts.append(jnp.where(core == k // each, kept[s], sent[s]))
         return parts
 
-    y_queue, x_queue, x_done, own_parts = [], [], [], {}
-
-    def background(take_more=None, work=None, given=(), y_pieces=1, x_pieces=1):
-        sends, keys = [], []
+    y_queue, x_queue, landed, found = [], [], {}, {}
+
+    def background(work=None, given=(), takes=None, y_pieces=1, x_pieces=1):
+        sends, keys, moving = [], [], []
         for _ in range(min(y_pieces, len(y_queue))):
             key, array = y_queue.pop(0)
             keys.append(key)
             sends.append((swap_chip, array))
         n = len(sends)
-        moving = [x_queue.pop(0) for _ in range(min(x_pieces, len(x_queue)))]
+        for _ in range(min(x_pieces, len(x_queue))):
+            moving.append(x_queue.pop(0))
         if pairs:
             sends += [(swap_group, array) for _, array in moving]
 
         def take(moved, made):
-            if take_more is not None:
-                take_more(made)
-            for key, got in zip(keys, moved[:n]):
-                x_queue.append((key, (own_parts[key] + got.astype(f32)).astype(bf16)))
-            for n_moved, (key, array) in enumerate(moving):
+            if takes is not None:
+                takes(made)
+            landed.update(zip(keys, moved[:n]))
+            for at, (key, array) in enumerate(moving):
                 if pairs:
-                    value = array.astype(f32) + moved[n + n_moved].astype(f32)
+                    found[key] = (array, moved[n + at])
                 else:
-                    value = lax.psum(array, "dp").astype(f32)
-                x_done.append((key, value))
+                    found[key] = (array,)
 
         return sends, work, given, take
+
+    def total(key, *after):
+        parts = found[key]
+        if after:
+            parts = lax.optimization_barrier((*parts, *after))[: len(parts)]
+        if pairs:
+            return parts[0].astype(f32) + parts[1].astype(f32)
+        return lax.psum(parts[0], "dp").astype(f32)
 
     def queue(name, parts):
         y_queue.extend((f"{name}{n}", part) for n, part in enumerate(parts))
 
-    def hold(name, parts):
-        own_parts.update((f"{name}{n}", part) for n, part in enumerate(parts))
+    feed_own = []
+
+    def down_gradient(n):
+        def work(u, v, c, d, got):
+            return [weight_gradients([u, v], [c, d], [got], columns=(n, wide))]
+
+        return work, (units, units_p, ck_own, cs_own, landed[f"d{n}"])
+
+    def ready_for_group(*keys):
+        return lambda made: x_queue.extend(zip(keys, made))
 
     queue("d", down_sent)
 
     def ffn_step(k):
         if k == 1:
 
-            def take(made):
-                hold("d", made[:2])
-                queue("f", made[2:])
-
-            def work(u, v, c, d, f, h, g, p):
-                grad = (mm_tn(f, g) + mm_tn(h, p)).astype(bf16)
-                return (*cut(mm_tn(u, c) + mm_tn(v, d), 2), *cut(grad, 4))
-
-            given = (units, units_p, ck_own, cs_own, fk_other, fs_other, gb, gb_p)
-            return background(take, aside(ready, work), given)
-        if k == 2:
-
             def work(f, h, g, p):
-                return cut(mm_tn(f, g) + mm_tn(h, p), 4)
+                return weight_gradient_pieces([f, h], [g, p], bf16, 4)
 
             return background(
-                lambda made: hold("f", made), aside(ready, work), (fk_own, fs_own, gb, gb_p)
+                work, (fk_other, fs_other, gb, gb_p), lambda made: queue("f", made)
             )
-
-        def work(u, v, w, o):
-            return [mm(a, b).astype(bf16) for b in (w, o) for a in (u, v)]
-
-        return background(kept.extend, aside(ready, work), (units, units_p, w_down, wd_o))
+        own, given = down_gradient(k - 2)
+        if k == 3:
+            return background(own, given, ready_for_group("d1"))
+
+        def work(f, h, g, p, *given):
+            return [*own(*given), *weight_gradient_pieces([f, h], [g, p], f32, 4)]
+
+        def takes(made):
+            x_queue.append(("d0", made[0]))
+            feed_own.extend(made[1:])
+
+        return background(work, (fk_own, fs_own, gb, gb_p, *given), takes)
 
     kept = []
     df_own, df_other = scatter(
         by_core(df_kept[0], df_sent[0]), by_core(df_kept[1], df_sent[1]), ffn_step
     )
-    un_own, un_other = by_core(*kept[:2]), by_core(*kept[2:])
 
     gain_fo = gains_other[1]
     w_o, w_p = df_own * ffn_gain, df_other * gain_fo
@@ -710,69 +873,154 @@
     gh_other = cot_other.astype(f32) + ffn_scale * w_p - h_other * factor
     ffn_part = jnp.sum(df_own * h_own * ffn_scale, axis=0)
     ffn_part_o = jnp.sum(df_other * h_other * ffn_scale, axis=0)
-    g_own, g_other = gather(
-        gh_own.astype(bf16), gh_other.astype(bf16), lambda k: background()
-    )
+
+    def back_step(k):
+        given = (feed_own[k - 1], landed[f"f{k - 1}"])
+        if k == 3:
+            return background(lambda a, b: [rounded_sum(a, b)], given, ready_for_group("f2"))
+
+        def work(u, v, w, a, b):
+            return [*products([u, v], w), rounded_sum(a, b)]
+
+        def takes(made):
+            kept.extend(made[:2])
+            x_queue.append((f"f{k - 1}", made[2]))
+
+        return background(work, (units, units_p, w_down if k == 1 else wd_o, *given), takes)
+
+    g_own, g_other = gather(gh_own.astype(bf16), gh_other.astype(bf16), back_step)
+    un_own, un_other = by_core(*kept[:2]), by_core(*kept[2:])
 
     gg_recv = swap_core(
         (mm_nt(g_own, mine(w_out, 1 - core, hc, 0)) + mm_nt(g_other, mine(wo_o, 1 - core, hc, 0)))
         .astype(bf16)
     )
     gg_keep = mm_nt(g_own, mine(w_out, core, hc, 0)) + mm_nt(g_other, mine(wo_o, core, hc, 0))
-    out_sent = mm_tn(gated, g_other).astype(bf16)
     do, d_gate, group_part, seg, low = recurrence_back_local(
         gg_keep, gg_recv, rec, keep, recv, gain_row, local[1], local[4]
     )
-    (peer, d_gate_p), _, _ = step([(swap_chip, low), (swap_core, d_gate)])
-
-    def finish_back(seg, peer):
+    core_here = core.astype(jnp.int32).reshape(1)
+
+    def gate_gradients(gate, left, grad, right):
+        gate_p = swap_core(gate)
+        sent = weight_gradients([left], [grad])
+        return [gate_p, sent, head_gradients(core_here, right, gate, gate_p, 0, hc, bf16)]
+
+    (peer,), (d_gate_p, out_sent, gate_sent), _ = step(
+        [(swap_chip, low)], gate_gradients, (d_gate, gated, g_other, m_other)
+    )
+
+    def finish_back(seg, peer, own, got):
         enter = recurrence_enter(place, seg, decay, peer, peer_decay, True)
-        return recurrence_back_finish(keep, recv, bound, ids, local, states, do, enter)
+        return [
+            *recurrence_back_finish(keep, recv, bound, ids, local, states, do, enter),
+            rounded_sum(own, got),
+        ]
 
     queue("o", [out_sent])
-    out_a, out_b = un_own[1], un_other[-1]
-    sends, _, _, take = background(y_pieces=1, x_pieces=1)
-    moved, (d_three, bound_part), _ = step(
-        [(up, out_a), (down, out_b), *sends], finish_back, (seg, peer)
-    )
-    out_a = (moved[0].astype(f32) + un_own[2].astype(f32)).astype(bf16)
-    out_b = (moved[1].astype(f32) + un_other[2].astype(f32)).astype(bf16)
-    hold("o", [mm_tn(gated, g_own)])
-    take(moved[2:], [])
+    queue("g", [gate_sent])
+    out_run = paired(un_own[1], un_other[1])
+    sends, _, _, take = background(y_pieces=2)
+    moved, (d_three, bound_part, feed_last), _ = step(
+        [(up, out_run), *sends], finish_back, (seg, peer, feed_own[3], landed["f3"])
+    )
+    x_queue.append(("f3", feed_last))
+    d_gate, d_gate_p = lax.optimization_barrier((d_gate, d_gate_p, d_three))[:2]
+
+    def out_sum(moved, at):
+        a = moved[:, :width].astype(f32) + un_own[at].astype(f32)
+        return a, moved[:, width:].astype(f32) + un_other[at].astype(f32)
+
+    out_run = paired(*out_sum(moved[0], 2)).astype(bf16)
+    take(moved[1:], [])
 
     d_three_p = swap_core(d_three)
 
-    def part(p):
-        if p == 3:
-            return joined(d_gate, d_gate_p, core, 1)
-        s = slice(p * hc, (p + 1) * hc)
-        return joined(d_three[:, s], d_three_p[:, s], core, 1)
-
-    sums_own = mm_nt(d_three, wm_keep[:, : 3 * hc]) + mm_nt(d_gate, wm_keep[:, 3 * hc :])
-    sums_own += mm_nt(d_three_p, wm_send[:, : 3 * hc]) + mm_nt(d_gate_p, wm_send[:, 3 * hc :])
-    sums_other = mm_nt(d_three, wm_keep_o[:, : 3 * hc]) + mm_nt(d_gate, wm_keep_o[:, 3 * hc :])
-    sums_other += mm_nt(d_three_p, wm_send_o[:, : 3 * hc]) + mm_nt(d_gate_p, wm_send_o[:, 3 * hc :])
-    parts = {name: part(p) for p, name in enumerate("qkvg")}
-
-    for name in "gqkv":
-        queue(name, [mm_tn(m_other, parts[name]).astype(bf16)])
-        hold(name, [mm_tn(m_own, parts[name])])
-    dx_own, dx_other = scatter(
-        blocks(sums_own.astype(bf16)),
-        blocks(sums_other.astype(bf16)),
-        lambda k: background(None, None, (), 2 if k == 1 else 1, 2 if k == 3 else 1),
-    )
+    dp_keep = jnp.concatenate([d_three, d_gate], 1)
+    sums_own, sums_other = mm_nt(dp_keep, wm_keep), mm_nt(dp_keep, wm_keep_o)
+    dp_send = jnp.concatenate([d_three_p, d_gate_p], 1)
+    sums_own, sums_other = sums_own + mm_nt(dp_send, wm_send), sums_other + mm_nt(dp_send, wm_send_o)
+    own, other = blocks(sums_own.astype(bf16)), blocks(sums_other.astype(bf16))
     mix_part = jnp.sum(sums_own * m_own.astype(f32), axis=0) / mix_gain
     mix_part_o = jnp.sum(sums_other * m_other.astype(f32), axis=0) / gains_other[0]
     tail = jnp.concatenate([bound_part[0], group_part[0]])
     small = jnp.concatenate([mix_part, ffn_part, tail])
     small_o = jnp.concatenate([mix_part_o, ffn_part_o, tail])
-    sends, _, _, take = background(None, None, (), 1, 1)
-    moved, _, _ = step([(up, out_a), (down, out_b), (swap_chip, small_o), *sends])
-    out_a = (moved[0].astype(f32) + un_own[3].astype(f32)).astype(bf16)
-    out_b = (moved[1].astype(f32) + un_other[1].astype(f32)).astype(bf16)
+
+    def heads_of(left, three, three_p, part, kind):
+        return head_gradients(core_here, left, three, three_p, part, hc, kind)
+
+    def first_gradients(three, three_p, right, heads, grad, left, gate, gate_p, o_got, g_got):
+        sent = [heads_of(right, three, three_p, p, bf16) for p in range(3)]
+        out = weight_gradients([heads], [grad], [o_got])
+        gates = head_gradients(core_here, left, gate, gate_p, 0, hc, bf16, [g_got])
+        return [*sent, out, gates]
+
+    sends, _, _, take = background()
+    dx_run = paired(own[1], other[1])
+    moved, made, _ = step(
+        [(up, dx_run), (up, out_run), (swap_chip, small_o), *sends],
+        first_gradients,
+        (d_three, d_three_p, m_other, gated, g_own, m_own, d_gate, d_gate_p)
+        + (landed["o0"], landed["g0"]),
+    )
     small = small + moved[2]
     take(moved[3:], [])
+    x_queue.extend(zip(("o0", "g0"), made[3:]))
+    for name, value in zip("qkv", made):
+        queue(name, [value])
+
+    def dx_sum(moved, at):
+        a = moved[:, :width].astype(f32) + own[at].astype(f32)
+        return a, moved[:, width:].astype(f32) + other[at].astype(f32)
+
+    dx_run = paired(*dx_sum(moved[0], 2)).astype(bf16)
+    out_run = paired(*out_sum(moved[1], 3)).astype(bf16)
+    sends, work, given, take = background(
+        lambda three, three_p, left: [heads_of(left, three, three_p, p, f32) for p in range(3)],
+        (d_three, d_three_p, m_own),
+        y_pieces=2,
+        x_pieces=2,
+    )
+    if pairs:
+        sends.append((swap_group, small))
+    moved, made, _ = step([(up, dx_run), (up, out_run), *sends], work, given)
+    small = small + moved[-1] if pairs else lax.psum(small, "dp")
+    take(moved[2:-1] if pairs else moved[2:], made)
+    of_parts = dict(zip(("q0", "k0", "v0"), made))
+
+    def reduced(key):
+        x_queue.append((key, (of_parts[key] + landed[key].astype(f32)).astype(bf16)))
+
+    reduced("q0")
+    reduced("k0")
+    dx_run = paired(*dx_sum(moved[0], 3)).astype(bf16)
+    out_own, out_other = out_sum(moved[1], 0)
+    out_own, out_other = (h_own + out_own).astype(bf16), (h_other + out_other).astype(bf16)
+    edge = 2 * width
+    bound_sum = small[edge : edge + hc]
+    wide = jnp.concatenate([small[:edge], small[edge + hc :]])
+    near = lambda a: lax.ppermute(a, "col", [(i, i ^ 1) for i in range(count)])
+    far = lambda a: lax.ppermute(a, "col", [(i, i ^ 2) for i in range(count)])
+    ffn_pieces = [found[f"f{n}"] if pairs else (total(f"f{n}"),) for n in range(4)]
+    each = len(ffn_pieces[0])
+
+    def whole_ffn(*given):
+        return [
+            halves_of_rows([given[n * each : (n + 1) * each] for n in range(4)], 2)
+        ]
+
+    sends, _, _, take = background(x_pieces=2)
+    moved, (ffn_whole,), _ = step(
+        [(up, dx_run), (near, wide), (swap_chip, out_other), *sends],
+        whole_ffn,
+        [array for found_piece in ffn_pieces for array in found_piece],
+    )
+    wide = wide + moved[1]
+    out_other = moved[2]
+    take(moved[3:], [])
+    reduced("v0")
+    dx_own, dx_other = dx_sum(moved[0], 0)
 
     w_o, w_p = dx_own * mix_gain, dx_other * gains_other[0]
     along = jnp.sum(w_o * x_own, axis=1) + jnp.sum(w_p * x_other, axis=1)
@@ -780,48 +1028,29 @@
     factor = mix_scale**3 * along[:, None] / D
     gt_own = gh_own + mix_scale * w_o - x_own * factor
     gt_other = gh_other + mix_scale * w_p - x_other * factor
-    sends, _, _, take = background(None, None, (), 1, 2)
-    if pairs:
-        sends.append((swap_group, small))
-    moved, _, _ = step([(up, out_a), (down, out_b), (swap_chip, gt_other.astype(bf16)), *sends])
-    out_own = (h_own + moved[0].astype(f32) + un_own[0].astype(f32)).astype(bf16)
-    out_other = (h_other + moved[1].astype(f32) + un_other[0].astype(f32)).astype(bf16)
-    grad_other = moved[2].astype(f32)
-    small = small + moved[-1] if pairs else lax.psum(small, "dp")
-    take(moved[3:-1] if pairs else moved[3:], [])
-    edge = 2 * width
-    bound_sum = small[edge : edge + hc]
-    wide = jnp.concatenate([small[:edge], small[edge + hc :]])
-    near = lambda a: lax.ppermute(a, "col", [(i, i ^ 1) for i in range(count)])
-    far = lambda a: lax.ppermute(a, "col", [(i, i ^ 2) for i in range(count)])
-    sends, _, _, take = background(None, None, (), 1, 2)
-    moved, _, _ = step([(swap_chip, out_other), (near, wide), *sends])
-    out_other = moved[0]
+    sends, _, _, take = background(x_pieces=2)
+    moved, _, _ = step([(swap_chip, gt_other.astype(bf16)), (far, wide), *sends])
+    grad_other = moved[0].astype(f32)
     wide = wide + moved[1]
     take(moved[2:], [])
     while y_queue or x_queue:
-        sends, _, _, take = background(None, None, (), 1, 2)
+        sends, _, _, take = background(x_pieces=2)
         moved, _, _ = step(sends) if sends else ([], [], [])
         take(moved, [])
-    wide = wide + far(wide)
     turned = swap_core(jnp.concatenate([bound_sum, wide[edge:]]))
     grad_bound = joined(bound_sum, turned[:hc], core, 0)
-    found = dict(x_done)
-
-    def all_of(name, parts):
-        return jnp.concatenate([found[f"{name}{n}"] for n in range(parts)], 0)
 
     return (
         joined(out_own, out_other, y, 0),
         joined(gt_own, grad_other, y, 0),
         wide[:width],
-        jnp.stack([found["q0"], found["k0"], found["v0"], found["g0"]], 1),
+        stacked([found[key] if pairs else (total(key),) for key in ("q0", "k0", "v0", "g0")]),
         grad_bound,
         wide[edge:] + turned[hc:],
-        found["o0"],
+        total("o0"),
         wide[width:edge],
-        all_of("f", 4).reshape(width, 2, units_col),
-        all_of("d", 2),
+        ffn_whole,
+        jnp.concatenate([total("d0"), total("d1")], 1),
     )
 
 

time: 626 us -> 581 us (0.928)
  Pallas kernels: 47.1 us -> 143 us
  starting transfers between devices: 142 us -> 82.7 us
  matrix products: 105 us -> 46.8 us
  local copies, waits for them, and re-layouts: 59.9 us -> 48.4 us
    pallas_call x0 -> x22, Pallas kernels: none -> 96.3 us  [the longest x8 25.4 us: head_gradients(): pl.pallas_call(heads_kernel, grid=(1,), in_specs=[SMEM, whole(*left.shape...]
    ppermute x48 -> x24, starting transfers between devices: 93.6 us -> 25.2 us  [up(): lax.ppermute(x, 'col', [(folded(n), folded((n + 1) % count)) for n in ran...]
    dot_general x18 -> x4, matrix products: 41.7 us -> 6.01 us  [mm_tn(): lax.dot_general(left, right, (((0,), (0,)), ((), ())), preferred_element_...]
    convert_element_type x27 -> x7, other arithmetic: 19.1 us -> 4.69 us  [the longest x3 2.78 us: reduced(): (of_parts[key] + landed[key].astype(f32)).astype(bf16)]
    dot_general x20 -> x16, matrix products: 35.8 us -> 22.8 us  [mm_nt(): lax.dot_general(left, right, (((1,), (1,)), ((), ())), preferred_element_...]
    concatenate x5 -> x25, other arithmetic: 6.24 us -> 17.6 us  [the longest x16 8.51 us: paired(): return jnp.concatenate([own, other], 1)]
    dot_general x14 -> x10, matrix products: 27.7 us -> 18 us  [mm(): lax.dot_general(left, right, (((1,), (0,)), ((), ())), preferred_element_...]
    ppermute x12, waiting for transfers between devices: 12.2 us -> 3.68 us  [swap_group(): return lax.ppermute(x, 'dp', [(0, 1), (1, 0)])]
  transfers between devices with their start and end apart: 108 -> 84, of which waited for: 63 -> 50; matrix products, arithmetic and copies ran while one was open for 24% -> 14% of each run, Pallas kernels for 7% -> 24%
where the time goes in v3:
time: 581 us; the launch traced here: 571 us
  waiting for transfers between devices  195 us (34%)
  Pallas kernels  143 us (25%)
  starting transfers between devices  82.7 us (14%)
  other arithmetic  51.5 us (9%)
  local copies, waits for them, and re-layouts  48.4 us (8%)
  matrix products  46.8 us (8%)
    ppermute x24, waiting for transfers between devices, up(): lax.ppermute(x, 'col', [(folded(n), folded((n + 1) % count)) for n in ran...  128 us
    ppermute x32, waiting for transfers between devices, swap_chip(): return lax.ppermute(x, 'row', CHIP)  48.8 us
    ppermute x32, starting transfers between devices, swap_chip(): return lax.ppermute(x, 'row', CHIP)  35.5 us
    pallas_call x8, Pallas kernels, head_gradients(): pl.pallas_call(heads_kernel, grid=(1,), in_specs=[SMEM, whole(*left.shape...  25.4 us
    ppermute x24, starting transfers between devices, up(): lax.ppermute(x, 'col', [(folded(n), folded((n + 1) % count)) for n in ran...  25.2 us
    unnamed x346, local copies, waits for them, and re-layouts  24.3 us
    dot_general x16, matrix products, mm_nt(): lax.dot_general(left, right, (((1,), (1,)), ((), ())), preferred_element_...  22.8 us
    pallas_call x2, Pallas kernels, weight_gradient_pieces(): pl.pallas_call(partial(pieces_kernel, len(lefts)), grid=(wide // tile,),...  21.4 us
  transfers between devices with their start and end apart: 84, of which 50 were waited for; matrix products, arithmetic and copies ran while one was open for 14% of the time, Pallas kernels for 24%

profile of v3, /device:TPU:0, one launch (start us, length us, event | category | flops | bytes accessed | tf_op | source)
XLA Modules:
  0.0 570.6 jit_solution(517830806520577590)
XLA Ops:
  18.6 14.1 %collective-permute-done.4 = bf16[256,512]{1,0:T(8,128)(2,1)S(1)} collective-permute-done((bf16[256,512]{1,0:T(8,128)(2,1)S(1)}, bf16[256,512]{1,0:T(8,128)(2,1)S(1)}, u32[]{:S(2)}, u32[]{:S(2)}) %collective-permute-start.4) | collective-permute-done | bytes 262176 | tf_op jit(solution)/shard_map/ppermute | solution.py:26
  34.9 12.1 %collective-permute-done.6 = bf16[256,1024]{1,0:T(8,128)(2,1)} collective-permute-done((bf16[256,1024]{1,0:T(8,128)(2,1)S(1)}, bf16[256,1024]{1,0:T(8,128)(2,1)}, u32[]{:S(2)}, u32[]{:S(2)}) %collective-permute-start.6) | collective-permute-done | bytes 524320 | tf_op jit(solution)/shard_map/ppermute | solution.py:563
  50.5 10.1 %collective-permute-done.8 = bf16[256,1024]{1,0:T(8,128)(2,1)} collective-permute-done((bf16[256,1024]{1,0:T(8,128)(2,1)}, bf16[256,1024]{1,0:T(8,128)(2,1)}, u32[]{:S(2)}, u32[]{:S(2)}) %collective-permute-start.8) | collective-permute-done | bytes 524320 | tf_op jit(solution)/shard_map/ppermute | solution.py:563
  66.0 7.7 %collective-permute-done.10 = bf16[256,1024]{1,0:T(8,128)(2,1)} collective-permute-done((bf16[256,1024]{1,0:T(8,128)(2,1)S(1)}, bf16[256,1024]{1,0:T(8,128)(2,1)}, u32[]{:S(2)}, u32[]{:S(2)}) %collective-permute-start.10) | collective-permute-done | bytes 524320 | tf_op jit(solution)/shard_map/ppermute | solution.py:563
  93.1 14.7 %recurrence_local.1 = (f32[1024,256]{1,0:T(8,128)}, bf16[1024,256]{1,0:T(8,128)(2,1)}, bf16[1024,256]{1,0:T(8,128)(2,1)}, bf16[1024,256]{1,0:T(8,128)(2,1)}, f32...) custom-call(f32[1024,1024]{1,0:T(8,128)} %convolution_add_fusion.4.keep, ...), custom_call_target="tpu_custom_call" | custom-call | tf_op jit(solution)/shard_map/recurrence_local/pallas_call | solution.py:278
  110.9 5.4 collective-permute-done.16.peerd_ref
  122.1 5.6 recurrence_finish.1
  168.3 9.9 %collective-permute-done.22 = bf16[256,1024]{1,0:T(8,128)(2,1)S(1)} collective-permute-done((bf16[256,1024]{1,0:T(8,128)(2,1)S(1)}, bf16[256,1024]{1,0:T(8,128)(2,1)S(1)}, u32[]{:S(2)}, u32[]{:S(2)}) %collective-permute-start.22) | collective-permute-done | bytes 524320 | tf_op jit(solution)/shard_map/ppermute | solution.py:563
  183.4 9.4 %collective-permute-done.24 = bf16[256,1024]{1,0:T(8,128)(2,1)S(1)} collective-permute-done((bf16[256,1024]{1,0:T(8,128)(2,1)S(1)}, bf16[256,1024]{1,0:T(8,128)(2,1)S(1)}, u32[]{:S(2)}, u32[]{:S(2)}) %collective-permute-start.24) | collective-permute-done | bytes 524320 | tf_op jit(solution)/shard_map/ppermute | solution.py:563
  198.2 13.7 %collective-permute-done.27 = bf16[256,1024]{1,0:T(8,128)(2,1)S(1)} collective-permute-done((bf16[256,1024]{1,0:T(8,128)(2,1)S(1)}, bf16[256,1024]{1,0:T(8,128)(2,1)S(1)}, u32[]{:S(2)}, u32[]{:S(2)}) %collective-permute-start.27) | collective-permute-done | bytes 524320 | tf_op jit(solution)/shard_map/ppermute | solution.py:563
  215.9 13.0 %collective-permute-done.29 = bf16[256,1024]{1,0:T(8,128)(2,1)S(1)} collective-permute-done((bf16[256,1024]{1,0:T(8,128)(2,1)S(1)}, bf16[256,1024]{1,0:T(8,128)(2,1)S(1)}, u32[]{:S(2)}, u32[]{:S(2)}) %collective-permute-start.29) | collective-permute-done | bytes 524320 | tf_op jit(solution)/shard_map/ppermute | solution.py:563
  230.8 7.4 %collective-permute-done.32 = bf16[64,2816]{1,0:T(8,128)(2,1)S(1)} collective-permute-done((bf16[64,2816]{1,0:T(8,128)(2,1)S(1)}, bf16[64,2816]{1,0:T(8,128)(2,1)S(1)}, u32[]{:S(2)}, u32[]{:S(2)}) %collective-permute-start.32) | collective-permute-done | bytes 360480 | tf_op jit(solution)/shard_map/ppermute | solution.py:26
  274.3 10.6 %weight_gradient_pieces.2 = (bf16[128,2816]{1,0:T(8,128)(2,1)}, bf16[128,2816]{1,0:T(8,128)(2,1)}, bf16[128,2816]{1,0:T(8,128)(2,1)}, bf16[128,2816]{1,0:T(8,128)(2,1)}) custom-call(bf16[512,512]{1,0:T(8,128)(2,1)} %copy-done.39, bf16[512,512]{1,0:T(8,128)(2,1)} %copy-done.40, bf16[512,2816]{1,0:T(8,128)(2,1)} %copy-done.15, bf16[512,2816]{1,0:T(8,128)(2,1)} %copy-done.26), custom_call_target="tpu_custom_call" | custom-call | tf_op jit(solution)/shard_map/weight_gradient_pieces/pallas_call | solution.py:425
  290.9 10.8 %weight_gradient_pieces.3 = (f32[128,2816]{1,0:T(8,128)}, f32[128,2816]{1,0:T(8,128)}, f32[128,2816]{1,0:T(8,128)}, f32[128,2816]{1,0:T(8,128)}) custom-call(bf16[512,512]{1,0:T(8,128)(2,1)} %copy-done.50, bf16[512,512]{1,0:T(8,128)(2,1)} %copy-done.51, bf16[512,2816]{1,0:T(8,128)(2,1)} %copy-done.15, bf16[512,2816]{1,0:T(8,128)(2,1)} %copy-done.26), custom_call_target="tpu_custom_call" | custom-call | tf_op jit(solution)/shard_map/weight_gradient_pieces/pallas_call | solution.py:425
  315.6 8.4 %collective-permute-done.41 = bf16[256,1024]{1,0:T(8,128)(2,1)S(1)} collective-permute-done((bf16[256,1024]{1,0:T(8,128)(2,1)S(1)}, bf16[256,1024]{1,0:T(8,128)(2,1)S(1)}, u32[]{:S(2)}, u32[]{:S(2)}) %collective-permute-start.41) | collective-permute-done | bytes 524320 | tf_op jit(solution)/shard_map/ppermute | solution.py:563
  340.5 7.2 %collective-permute-done.45 = bf16[256,1024]{1,0:T(8,128)(2,1)} collective-permute-done((bf16[256,1024]{1,0:T(8,128)(2,1)}, bf16[256,1024]{1,0:T(8,128)(2,1)}, u32[]{:S(2)}, u32[]{:S(2)}) %collective-permute-start.45) | collective-permute-done | bytes 524320 | tf_op jit(solution)/shard_map/ppermute | solution.py:563
  359.6 5.8 %collective-permute-done.48 = bf16[256,1024]{1,0:T(8,128)(2,1)} collective-permute-done((bf16[256,1024]{1,0:T(8,128)(2,1)}, bf16[256,1024]{1,0:T(8,128)(2,1)}, u32[]{:S(2)}, u32[]{:S(2)}) %collective-permute-start.48) | collective-permute-done | bytes 524320 | tf_op jit(solution)/shard_map/ppermute | solution.py:563
  394.8 5.2 recurrence_back_local.1
  420.3 17.4 %recurrence_back_finish.1 = (bf16[1024,768]{1,0:T(8,128)(2,1)}, f32[1,256]{1,0:T(1,128)}) custom-call(f32[1024,1024]{1,0:T(8,128)} %convolution_add_fusion.4.keep_ref, bf16[1024,1024]{1,0:T(8,128)(2,1)} %copy-done.14, f32[1,256]{1,0:T(1,128)} %bitcast.143, f32[1024,1]{1,0:T(8,128)} %bitcast.105, f32[4,1,256]{2,1,0:T(1,128)} %reshape.93.idr_ref, ...), custom_call_target="tpu_custom_call" | custom-call | tf_op jit(solution)/shard_map/recurrence_back_finish/pallas_call | solution.py:374
  475.6 6.0 %collective-permute-done.63 = bf16[256,1024]{1,0:T(8,128)(2,1)} collective-permute-done((bf16[256,1024]{1,0:T(8,128)(2,1)}, bf16[256,1024]{1,0:T(8,128)(2,1)}, u32[]{:S(2)}, u32[]{:S(2)}) %collective-permute-start.63) | collective-permute-done | bytes 524320 | tf_op jit(solution)/shard_map/ppermute | solution.py:563
  493.3 9.0 %collective-permute-done.66 = bf16[256,1024]{1,0:T(8,128)(2,1)} collective-permute-done((bf16[256,1024]{1,0:T(8,128)(2,1)}, bf16[256,1024]{1,0:T(8,128)(2,1)}, u32[]{:S(2)}, u32[]{:S(2)}) %collective-permute-start.66) | collective-permute-done | bytes 524320 | tf_op jit(solution)/shard_map/ppermute | solution.py:563
  528.3 4.9 collective-permute-done.74
  536.1 8.2 %halves_of_rows.1 = f32[512,2,1408]{2,1,0:T(2,128)} custom-call(bf16[128,2816]{1,0:T(8,128)(2,1)S(1)} %copy-done, bf16[128,2816]{1,0:T(8,128)(2,1)S(1)} %copy-done.5, bf16[128,2816]{1,0:T(8,128)(2,1)S(1)} %copy-done.1, bf16[128,2816]{1,0:T(8,128)(2,1)S(1)} %copy-done.7, bf16[128,2816]{1,0:T(8,128)(2,1)S(1)} %copy-done.2, bf16[128,2816]{1,0:T(8,128)(2,1)S(1)} %copy-done.9, ...), custom_call_target="tpu_custom_call" | custom-call | tf_op jit(solution)/shard_map/halves_of_rows/pallas_call | solution.py:472
  562.3 6.9 %stacked.1 = f32[512,4,512]{2,1,0:T(4,128)} custom-call(bf16[512,512]{1,0:T(8,128)(2,1)} %copy-done.88, bf16[512,512]{1,0:T(8,128)(2,1)} %copy-done.142, bf16[512,512]{1,0:T(8,128)(2,1)} %copy-done.87, bf16[512,512]{1,0:T(8,128)(2,1)} %copy-done.143, bf16[512,512]{1,0:T(8,128)(2,1)} %copy-done.89, bf16[512,512]{1,0:T(8,128)(2,1)} %copy-done.144, ...), custom_call_target="tpu_custom_call" | custom-call | tf_op jit(solution)/shard_map/stacked/pallas_call | solution.py:496
  (675 shorter events, 343.7 us)
Async XLA Ops:
  13.0 19.6 %collective-permute-start.5 = (bf16[128,4,512]{2,1,0:T(4,128)(2,1)S(1)}, bf16[128,4,512]{2,1,0:T(4,128)(2,1)S(1)}, u32[]{:S(2)}, u32[]{:S(2)}) collective-permute-start(bf16[128,4,512]{2,1,0:T(4,128)(2,1)S(1)} %get-tuple-element.295), channel_id=1, source_target_pairs={{0,8},{8,0},{4,12},{12,4},{1,9},{9,1},{5,13},{13,5},{2,10},{10,2},... | collective-permute-start | bytes 1572872 | tf_op jit(solution)/shard_map/ppermute | solution.py:26
  87.0 20.8 %collective-permute-start.13 = (bf16[256,1024]{1,0:T(8,128)(2,1)}, bf16[256,1024]{1,0:T(8,128)(2,1)}, u32[]{:S(2)}, u32[]{:S(2)}) collective-permute-start(bf16[256,1024]{1,0:T(8,128)(2,1)} %collective-permute-done.10), channel_id=1, source_target_pairs={{0,1},{1,3},{3,2},{2,0},{4,5},{5,7},{7,6},{6,4},{8,9},{9,11},{11,1... | collective-permute-start | bytes 1572872 | tf_op jit(solution)/shard_map/ppermute | solution.py:563
  88.9 18.9 %collective-permute-start.14 = (bf16[512,512]{1,0:T(8,128)(2,1)}, bf16[512,512]{1,0:T(8,128)(2,1)}, u32[]{:S(2)}, u32[]{:S(2)}) collective-permute-start(bf16[512,512]{1,0:T(8,128)(2,1)} %param.17), channel_id=1, source_target_pairs={{0,8},{8,0},{4,12},{12,4},{1,9},{9,1},{5,13},{13,5},{2,10},{10,2},... | collective-permute-start | bytes 1572872 | tf_op jit(solution)/shard_map/ppermute | solution.py:26
  143.1 18.5 %collective-permute-start.21 = (bf16[704,512]{1,0:T(8,128)(2,1)}, bf16[704,512]{1,0:T(8,128)(2,1)}, u32[]{:S(2)}, u32[]{:S(2)}) collective-permute-start(bf16[704,512]{1,0:T(8,128)(2,1)} %get-tuple-element.350), channel_id=1, source_target_pairs={{0,8},{8,0},{4,12},{12,4},{1,9},{9,1},{5,13},{13,5},{2,10},{10,2},... | collective-permute-start | bytes 2162696 | tf_op jit(solution)/shard_map/ppermute | solution.py:26
  183.3 30.3 %collective-permute-start.33 = (bf16[512,1408]{1,0:T(8,128)(2,1)S(1)}, bf16[512,1408]{1,0:T(8,128)(2,1)S(1)}, u32[]{:S(2)}, u32[]{:S(2)}) collective-permute-start(bf16[512,1408]{1,0:T(8,128)(2,1)S(1)} %fusion.1), channel_id=1, source_target_pairs={{0,4},{4,0},{8,12},{12,8},{1,5},{5,1},{9,13},{13,9},{2,6},{6,2},{1... | collective-permute-start | bytes 4325384 | tf_op jit(solution)/shard_map/ppermute | solution.py:22
  269.2 18.5 %collective-permute-start.38 = (bf16[1408,256]{1,0:T(8,128)(2,1)}, bf16[1408,256]{1,0:T(8,128)(2,1)}, u32[]{:S(2)}, u32[]{:S(2)}) collective-permute-start(bf16[1408,256]{1,0:T(8,128)(2,1)} %fusion.3), channel_id=1, source_target_pairs={{0,8},{8,0},{4,12},{12,4},{1,9},{9,1},{5,13},{13,5},{2,10},{10,2},... | collective-permute-start | bytes 2162696 | tf_op jit(solution)/shard_map/ppermute | solution.py:26
  289.8 17.7 %collective-permute-start.40 = (bf16[1408,256]{1,0:T(8,128)(2,1)}, bf16[1408,256]{1,0:T(8,128)(2,1)}, u32[]{:S(2)}, u32[]{:S(2)}) collective-permute-start(bf16[1408,256]{1,0:T(8,128)(2,1)} %fusion.4), channel_id=1, source_target_pairs={{0,8},{8,0},{4,12},{12,4},{1,9},{9,1},{5,13},{13,5},{2,10},{10,2},... | collective-permute-start | bytes 2162696 | tf_op jit(solution)/shard_map/ppermute | solution.py:26
  330.3 18.5 %collective-permute-start.46 = (bf16[128,2816]{1,0:T(8,128)(2,1)}, bf16[128,2816]{1,0:T(8,128)(2,1)}, u32[]{:S(2)}, u32[]{:S(2)}) collective-permute-start(bf16[128,2816]{1,0:T(8,128)(2,1)} %get-tuple-element.423), channel_id=1, source_target_pairs={{0,8},{8,0},{4,12},{12,4},{1,9},{9,1},{5,13},{13,5},{2,10},{10,2},... | collective-permute-start | bytes 2162696 | tf_op jit(solution)/shard_map/ppermute | solution.py:26
  331.5 18.0 %collective-permute-start.47 = (bf16[1408,256]{1,0:T(8,128)(2,1)S(1)}, bf16[1408,256]{1,0:T(8,128)(2,1)S(1)}, u32[]{:S(2)}, u32[]{:S(2)}) collective-permute-start(bf16[1408,256]{1,0:T(8,128)(2,1)S(1)} %copy-done.63), channel_id=1, source_target_pairs={{0,16},{16,0},{1,17},{17,1},{2,18},{18,2},{3,19},{19,3},{4,20},{20... | collective-permute-start | bytes 2162696 | tf_op jit(solution)/shard_map/ppermute | solution.py:554
  411.7 26.7 %collective-permute-start.60 = (bf16[128,2816]{1,0:T(8,128)(2,1)S(1)}, bf16[128,2816]{1,0:T(8,128)(2,1)S(1)}, u32[]{:S(2)}, u32[]{:S(2)}) collective-permute-start(bf16[128,2816]{1,0:T(8,128)(2,1)S(1)} %copy-done.2), channel_id=1, source_target_pairs={{0,16},{16,0},{1,17},{17,1},{2,18},{18,2},{3,19},{19,3},{4,20},{20... | collective-permute-start | bytes 2162696 | tf_op jit(solution)/shard_map/ppermute | solution.py:554
  413.1 24.7 %collective-permute-start.57 = (bf16[256,1024]{1,0:T(8,128)(2,1)}, bf16[256,1024]{1,0:T(8,128)(2,1)}, u32[]{:S(2)}, u32[]{:S(2)}) collective-permute-start(bf16[256,1024]{1,0:T(8,128)(2,1)} %pad_maximum_fusion.20), channel_id=1, source_target_pairs={{0,1},{1,3},{3,2},{2,0},{4,5},{5,7},{7,6},{6,4},{8,9},{9,11},{11,1... | collective-permute-start | bytes 1572872 | tf_op jit(solution)/shard_map/ppermute | solution.py:563
  413.7 24.1 %collective-permute-start.58 = (bf16[512,512]{1,0:T(8,128)(2,1)}, bf16[512,512]{1,0:T(8,128)(2,1)}, u32[]{:S(2)}, u32[]{:S(2)}) collective-permute-start(bf16[512,512]{1,0:T(8,128)(2,1)} %weight_gradients.6), channel_id=1, source_target_pairs={{0,8},{8,0},{4,12},{12,4},{1,9},{9,1},{5,13},{13,5},{2,10},{10,2},... | collective-permute-start | bytes 1572872 | tf_op jit(solution)/shard_map/ppermute | solution.py:26
  414.8 23.6 %collective-permute-start.59 = (bf16[512,512]{1,0:T(8,128)(2,1)}, bf16[512,512]{1,0:T(8,128)(2,1)}, u32[]{:S(2)}, u32[]{:S(2)}) collective-permute-start(bf16[512,512]{1,0:T(8,128)(2,1)} %head_gradients.8), channel_id=1, source_target_pairs={{0,8},{8,0},{4,12},{12,4},{1,9},{9,1},{5,13},{13,5},{2,10},{10,2},... | collective-permute-start | bytes 1572872 | tf_op jit(solution)/shard_map/ppermute | solution.py:26
  454.7 26.9 %collective-permute-start.65 = (bf16[128,2816]{1,0:T(8,128)(2,1)S(1)}, bf16[128,2816]{1,0:T(8,128)(2,1)}, u32[]{:S(2)}, u32[]{:S(2)}) collective-permute-start(bf16[128,2816]{1,0:T(8,128)(2,1)S(1)} %copy-done.3), channel_id=1, source_target_pairs={{0,16},{16,0},{1,17},{17,1},{2,18},{18,2},{3,19},{19,3},{4,20},{20... | collective-permute-start | bytes 2162696 | tf_op jit(solution)/shard_map/ppermute | solution.py:554
  455.4 20.1 %collective-permute-start.62 = (bf16[256,1024]{1,0:T(8,128)(2,1)}, bf16[256,1024]{1,0:T(8,128)(2,1)}, u32[]{:S(2)}, u32[]{:S(2)}) collective-permute-start(bf16[256,1024]{1,0:T(8,128)(2,1)} %pad_maximum_fusion.21), channel_id=1, source_target_pairs={{0,1},{1,3},{3,2},{2,0},{4,5},{5,7},{7,6},{6,4},{8,9},{9,11},{11,1... | collective-permute-start | bytes 1572872 | tf_op jit(solution)/shard_map/ppermute | solution.py:563
  456.7 24.9 %collective-permute-start.63 = (bf16[256,1024]{1,0:T(8,128)(2,1)}, bf16[256,1024]{1,0:T(8,128)(2,1)}, u32[]{:S(2)}, u32[]{:S(2)}) collective-permute-start(bf16[256,1024]{1,0:T(8,128)(2,1)} %pad_maximum_fusion.22), channel_id=1, source_target_pairs={{0,1},{1,3},{3,2},{2,0},{4,5},{5,7},{7,6},{6,4},{8,9},{9,11},{11,1... | collective-permute-start | bytes 1572872 | tf_op jit(solution)/shard_map/ppermute | solution.py:563
  488.0 28.1 %collective-permute-start.67 = (bf16[256,1024]{1,0:T(8,128)(2,1)}, bf16[256,1024]{1,0:T(8,128)(2,1)}, u32[]{:S(2)}, u32[]{:S(2)}) collective-permute-start(bf16[256,1024]{1,0:T(8,128)(2,1)} %pad_maximum_fusion.24), channel_id=1, source_target_pairs={{0,1},{1,3},{3,2},{2,0},{4,5},{5,7},{7,6},{6,4},{8,9},{9,11},{11,1... | collective-permute-start | bytes 1572872 | tf_op jit(solution)/shard_map/ppermute | solution.py:563
  490.7 25.4 %collective-permute-start.68 = (bf16[512,512]{1,0:T(8,128)(2,1)}, bf16[512,512]{1,0:T(8,128)(2,1)}, u32[]{:S(2)}, u32[]{:S(2)}) collective-permute-start(bf16[512,512]{1,0:T(8,128)(2,1)} %head_gradients.9), channel_id=1, source_target_pairs={{0,8},{8,0},{4,12},{12,4},{1,9},{9,1},{5,13},{13,5},{2,10},{10,2},... | collective-permute-start | bytes 1572872 | tf_op jit(solution)/shard_map/ppermute | solution.py:26
  491.9 24.3 %collective-permute-start.69 = (bf16[512,512]{1,0:T(8,128)(2,1)}, bf16[512,512]{1,0:T(8,128)(2,1)}, u32[]{:S(2)}, u32[]{:S(2)}) collective-permute-start(bf16[512,512]{1,0:T(8,128)(2,1)} %head_gradients.10), channel_id=1, source_target_pairs={{0,8},{8,0},{4,12},{12,4},{1,9},{9,1},{5,13},{13,5},{2,10},{10,2},... | collective-permute-start | bytes 1572872 | tf_op jit(solution)/shard_map/ppermute | solution.py:26
  492.7 23.4 %collective-permute-start.70 = (bf16[512,512]{1,0:T(8,128)(2,1)}, bf16[512,512]{1,0:T(8,128)(2,1)}, u32[]{:S(2)}, u32[]{:S(2)}) collective-permute-start(bf16[512,512]{1,0:T(8,128)(2,1)} %weight_gradients.7), channel_id=1, source_target_pairs={{0,16},{16,0},{1,17},{17,1},{2,18},{18,2},{3,19},{19,3},{4,20},{20... | collective-permute-start | bytes 1572872 | tf_op jit(solution)/shard_map/ppermute | solution.py:554
  521.8 22.5 %collective-permute-start.73 = (bf16[256,1024]{1,0:T(8,128)(2,1)S(1)}, bf16[256,1024]{1,0:T(8,128)(2,1)S(1)}, u32[]{:S(2)}, u32[]{:S(2)}) collective-permute-start(bf16[256,1024]{1,0:T(8,128)(2,1)S(1)} %pad_maximum_fusion.25), channel_id=1, source_target_pairs={{0,1},{1,3},{3,2},{2,0},{4,5},{5,7},{7,6},{6,4},{8,9},{9,11},{11,1... | collective-permute-start | bytes 1572872 | tf_op jit(solution)/shard_map/ppermute | solution.py:563
  521.9 22.4 %collective-permute-start.76 = (bf16[512,512]{1,0:T(8,128)(2,1)S(1)}, bf16[512,512]{1,0:T(8,128)(2,1)S(1)}, u32[]{:S(2)}, u32[]{:S(2)}) collective-permute-start(bf16[512,512]{1,0:T(8,128)(2,1)S(1)} %copy-done.141), channel_id=1, source_target_pairs={{0,8},{8,0},{4,12},{12,4},{1,9},{9,1},{5,13},{13,5},{2,10},{10,2},... | collective-permute-start | bytes 1572872 | tf_op jit(solution)/shard_map/ppermute | solution.py:26
  522.9 21.4 %collective-permute-start.77 = (bf16[512,512]{1,0:T(8,128)(2,1)S(1)}, bf16[512,512]{1,0:T(8,128)(2,1)S(1)}, u32[]{:S(2)}, u32[]{:S(2)}) collective-permute-start(bf16[512,512]{1,0:T(8,128)(2,1)S(1)} %add_convert_fusion.4.refs_0_), channel_id=1, source_target_pairs={{0,16},{16,0},{1,17},{17,1},{2,18},{18,2},{3,19},{19,3},{4,20},{20... | collective-permute-start | bytes 1572872 | tf_op jit(solution)/shard_map/ppermute | solution.py:554
  524.4 19.9 %collective-permute-start.78 = (bf16[512,512]{1,0:T(8,128)(2,1)S(1)}, bf16[512,512]{1,0:T(8,128)(2,1)S(1)}, u32[]{:S(2)}, u32[]{:S(2)}) collective-permute-start(bf16[512,512]{1,0:T(8,128)(2,1)S(1)} %add_convert_fusion.3.refs_2_), channel_id=1, source_target_pairs={{0,16},{16,0},{1,17},{17,1},{2,18},{18,2},{3,19},{19,3},{4,20},{20... | collective-permute-start | bytes 1572872 | tf_op jit(solution)/shard_map/ppermute | solution.py:554
  (222 other events, 2072.0 us)

commit v4 on v3

--- a/solution.py
+++ b/solution.py
@@ -197,7 +197,7 @@
 
 def back_finish_kernel(
     keep_ref, recv_ref, lb_ref, idc_ref, idr_ref, prev_ref,
-    qh_ref, kh_ref, vb_ref, decay_ref, st_ref, do_ref, enter_ref,
+    qh_ref, kh_ref, vb_ref, decay_ref, st_ref, do_ref, enter_ref, gate_ref,
     grad_ref, bound_ref,
 ):
     @pl.when(pl.program_id(0) == 0)
@@ -205,6 +205,7 @@
         bound_ref[...] = jnp.zeros_like(bound_ref)
 
     heads = enter_ref.shape[1]
+    grad_ref[:, 3 * gate_ref.shape[1] :] = gate_ref[...]
     adjoint = [enter_ref[0, h] for h in range(heads)]
     bound = [jnp.zeros((1, HD), f32)] * heads
     for i in reversed(range(keep_ref.shape[0] // BLOCK)):
@@ -364,7 +365,7 @@
     )(kd, rd, rec, keep, recv, gain, qh, decay)
 
 
-def recurrence_back_finish(keep, recv, bound, ids, local, states, do, enter):
+def recurrence_back_finish(keep, recv, bound, ids, local, states, do, enter, gate):
     _, qh, kh, vb, decay = local
     runs, chunks, width = decay.shape
     heads = width // HD
@@ -378,13 +379,13 @@
             run_block(run, 4 * width), run_block(run, 4 * width), whole(1, width),
             run_block(run, 1), run_block(1, 1, run), run_block(run, 1),
             cols, cols, cols, run_block(1, chunks, width),
-            run_block(1, chunks, heads, HD, HD), cols, run_block(1, heads, HD, HD),
+            run_block(1, chunks, heads, HD, HD), cols, run_block(1, heads, HD, HD), cols,
         ],
-        out_specs=[run_block(run, 3 * width), whole(1, width)],
-        out_shape=[shape((tokens, 3 * width), bf16), shape((1, width), f32)],
+        out_specs=[run_block(run, 4 * width), whole(1, width)],
+        out_shape=[shape((tokens, 4 * width), bf16), shape((1, width), f32)],
         cost_estimate=COST,
         name="recurrence_back_finish",
-    )(keep, recv, bound, *ids, qh, kh, vb, decay, states, do, enter)
+    )(keep, recv, bound, *ids, qh, kh, vb, decay, states, do, enter, gate)
 
 
 def weight_kernel(pairs, *refs):
@@ -481,20 +482,21 @@
     )(*given)
 
 
-def stack_kernel(parts, *refs):
+def stack_kernel(counts, *refs):
     *given, out_ref = refs
-    each = len(given) // parts
-    for part in range(parts):
-        out_ref[:, part, :] = sum(
-            ref[...].astype(f32) for ref in given[part * each : (part + 1) * each]
-        )
+    for part, count in enumerate(counts):
+        refs_here, given = given[:count], given[count:]
+        if count:
+            out_ref[:, part, :] = sum(ref[...].astype(f32) for ref in refs_here)
+        else:
+            out_ref[:, part, :] = jnp.zeros((out_ref.shape[0], out_ref.shape[2]), f32)
 
 
 def stacked(parts, rows=64):
     tall, wide = parts[0][0].shape
     given = [array for part in parts for array in part]
     return pl.pallas_call(
-        partial(stack_kernel, len(parts)),
+        partial(stack_kernel, [len(part) for part in parts]),
         grid=(tall // rows,),
         in_specs=[pl.BlockSpec((rows, wide), lambda j: (j, 0))] * len(given),
         out_specs=pl.BlockSpec((rows, len(parts), wide), lambda j: (j, 0, 0)),
@@ -524,30 +526,51 @@
     )(right, *lefts)
 
 
-def heads_kernel(core_ref, left_ref, own_ref, peer_ref, *refs):
+def heads_kernel(first, half, core_ref, left_ref, own_ref, peer_ref, *refs):
     *plus, out_ref = refs
-    half = own_ref.shape[1]
     core = core_ref[0]
-    for right_ref, at in ((own_ref, core), (peer_ref, 1 - core)):
-        cols = pl.ds(pl.multiple_of(at * half, half), half)
-        total = mm_tn(left_ref[...], right_ref[...])
-        for part in plus:
-            total = total + part[:, cols].astype(f32)
-        out_ref[:, cols] = total.astype(out_ref.dtype)
-
-
-def head_gradients(core, left, own, peer, part, half, kind, plus=()):
-    block = pl.BlockSpec((own.shape[0], half), lambda j: (0, part))
-    out = whole(left.shape[1], 2 * half)
-    return pl.pallas_call(
-        heads_kernel,
-        grid=(1,),
-        in_specs=[SMEM, whole(*left.shape), block, block] + [out] * len(plus),
-        out_specs=out,
-        out_shape=shape((left.shape[1], 2 * half), kind),
+    tall = left_ref.shape[1]
+    for part in range(out_ref.shape[0] // tall):
+        rows = slice(part * tall, (part + 1) * tall)
+        given = slice((first + part) * half, (first + part + 1) * half)
+        for right_ref, at in ((own_ref, core), (peer_ref, 1 - core)):
+            cols = pl.ds(pl.multiple_of(at * half, half), half)
+            total = mm_tn(left_ref[...], right_ref[:, given])
+            for more in plus:
+                total = total + more[rows, cols].astype(f32)
+            out_ref[rows, cols] = total.astype(out_ref.dtype)
+
+
+def head_gradients(core, left, own, peer, first, half, kind, plus=(), parts=1):
+    return pl.pallas_call(
+        partial(heads_kernel, first, half),
+        in_specs=[SMEM] + [VMEM] * (3 + len(plus)),
+        out_specs=VMEM,
+        out_shape=shape((parts * left.shape[1], 2 * half), kind),
         cost_estimate=COST,
         name="head_gradients",
     )(core, left, own, peer, *plus)
+
+
+def fill_kernel(part, *refs):
+    base_ref, *given, out_ref = refs
+    out_ref[...] = base_ref[...]
+    out_ref[:, part, :] = sum(ref[...].astype(f32) for ref in given)
+
+
+def filled(base, part, given, rows=64):
+    tall, parts, wide = base.shape
+    block = pl.BlockSpec((rows, parts, wide), lambda j: (j, 0, 0))
+    return pl.pallas_call(
+        partial(fill_kernel, part),
+        grid=(tall // rows,),
+        in_specs=[block] + [pl.BlockSpec((rows, wide), lambda j: (j, 0))] * len(given),
+        out_specs=block,
+        out_shape=shape(base.shape, f32),
+        input_output_aliases={0: 0},
+        cost_estimate=COST,
+        name="filled",
+    )(base, *given)
 
 
 def swap_group(x):
@@ -910,10 +933,10 @@
         [(swap_chip, low)], gate_gradients, (d_gate, gated, g_other, m_other)
     )
 
-    def finish_back(seg, peer, own, got):
+    def finish_back(seg, peer, gate, own, got):
         enter = recurrence_enter(place, seg, decay, peer, peer_decay, True)
         return [
-            *recurrence_back_finish(keep, recv, bound, ids, local, states, do, enter),
+            *recurrence_back_finish(keep, recv, bound, ids, local, states, do, enter, gate),
             rounded_sum(own, got),
         ]
 
@@ -921,11 +944,10 @@
     queue("g", [gate_sent])
     out_run = paired(un_own[1], un_other[1])
     sends, _, _, take = background(y_pieces=2)
-    moved, (d_three, bound_part, feed_last), _ = step(
-        [(up, out_run), *sends], finish_back, (seg, peer, feed_own[3], landed["f3"])
+    moved, (dp_keep, bound_part, feed_last), _ = step(
+        [(up, out_run), *sends], finish_back, (seg, peer, d_gate, feed_own[3], landed["f3"])
     )
     x_queue.append(("f3", feed_last))
-    d_gate, d_gate_p = lax.optimization_barrier((d_gate, d_gate_p, d_three))[:2]
 
     def out_sum(moved, at):
         a = moved[:, :width].astype(f32) + un_own[at].astype(f32)
@@ -934,11 +956,8 @@
     out_run = paired(*out_sum(moved[0], 2)).astype(bf16)
     take(moved[1:], [])
 
-    d_three_p = swap_core(d_three)
-
-    dp_keep = jnp.concatenate([d_three, d_gate], 1)
+    dp_send = swap_core(dp_keep)
     sums_own, sums_other = mm_nt(dp_keep, wm_keep), mm_nt(dp_keep, wm_keep_o)
-    dp_send = jnp.concatenate([d_three_p, d_gate_p], 1)
     sums_own, sums_other = sums_own + mm_nt(dp_send, wm_send), sums_other + mm_nt(dp_send, wm_send_o)
     own, other = blocks(sums_own.astype(bf16)), blocks(sums_other.astype(bf16))
     mix_part = jnp.sum(sums_own * m_own.astype(f32), axis=0) / mix_gain
@@ -947,28 +966,26 @@
     small = jnp.concatenate([mix_part, ffn_part, tail])
     small_o = jnp.concatenate([mix_part_o, ffn_part_o, tail])
 
-    def heads_of(left, three, three_p, part, kind):
-        return head_gradients(core_here, left, three, three_p, part, hc, kind)
-
-    def first_gradients(three, three_p, right, heads, grad, left, gate, gate_p, o_got, g_got):
-        sent = [heads_of(right, three, three_p, p, bf16) for p in range(3)]
+    def heads_of(left, keep, send, first, parts, kind, plus=()):
+        return head_gradients(core_here, left, keep, send, first, hc, kind, plus, parts)
+
+    def first_gradients(keep, send, right, heads, grad, left, o_got, g_got):
+        sent = [heads_of(right, keep, send, 0, 2, bf16), heads_of(right, keep, send, 2, 1, bf16)]
         out = weight_gradients([heads], [grad], [o_got])
-        gates = head_gradients(core_here, left, gate, gate_p, 0, hc, bf16, [g_got])
-        return [*sent, out, gates]
+        return [*sent, out, heads_of(left, keep, send, 3, 1, bf16, [g_got])]
 
     sends, _, _, take = background()
     dx_run = paired(own[1], other[1])
     moved, made, _ = step(
         [(up, dx_run), (up, out_run), (swap_chip, small_o), *sends],
         first_gradients,
-        (d_three, d_three_p, m_other, gated, g_own, m_own, d_gate, d_gate_p)
-        + (landed["o0"], landed["g0"]),
+        (dp_keep, dp_send, m_other, gated, g_own, m_own, landed["o0"], landed["g0"]),
     )
     small = small + moved[2]
     take(moved[3:], [])
-    x_queue.extend(zip(("o0", "g0"), made[3:]))
-    for name, value in zip("qkv", made):
-        queue(name, [value])
+    x_queue.extend(zip(("o0", "g0"), made[2:]))
+    queue("qk", [made[0]])
+    queue("v", [made[1]])
 
     def dx_sum(moved, at):
         a = moved[:, :width].astype(f32) + own[at].astype(f32)
@@ -976,24 +993,25 @@
 
     dx_run = paired(*dx_sum(moved[0], 2)).astype(bf16)
     out_run = paired(*out_sum(moved[1], 3)).astype(bf16)
+    def own_gradients(keep, send, left):
+        return [
+            heads_of(left, keep, send, 0, 2, f32), heads_of(left, keep, send, 2, 1, f32)
+        ]
+
     sends, work, given, take = background(
-        lambda three, three_p, left: [heads_of(left, three, three_p, p, f32) for p in range(3)],
-        (d_three, d_three_p, m_own),
-        y_pieces=2,
-        x_pieces=2,
+        own_gradients, (dp_keep, dp_send, m_own), x_pieces=2
     )
     if pairs:
         sends.append((swap_group, small))
     moved, made, _ = step([(up, dx_run), (up, out_run), *sends], work, given)
     small = small + moved[-1] if pairs else lax.psum(small, "dp")
     take(moved[2:-1] if pairs else moved[2:], made)
-    of_parts = dict(zip(("q0", "k0", "v0"), made))
+    of_parts = dict(zip(("qk0", "v0"), made))
 
     def reduced(key):
         x_queue.append((key, (of_parts[key] + landed[key].astype(f32)).astype(bf16)))
 
-    reduced("q0")
-    reduced("k0")
+    reduced("qk0")
     dx_run = paired(*dx_sum(moved[0], 3)).astype(bf16)
     out_own, out_other = out_sum(moved[1], 0)
     out_own, out_other = (h_own + out_own).astype(bf16), (h_other + out_other).astype(bf16)
@@ -1028,15 +1046,31 @@
     factor = mix_scale**3 * along[:, None] / D
     gt_own = gh_own + mix_scale * w_o - x_own * factor
     gt_other = gh_other + mix_scale * w_p - x_other * factor
+    def two_parts(key):
+        arrays = found[key] if pairs else (total(key),)
+        return [[array[at : at + width] for array in arrays] for at in (0, width)]
+
+    def one_part(key):
+        return list(found[key]) if pairs else [total(key)]
+
+    query, forget = two_parts("qk0")
+    most = [query, forget, one_part("g0")]
+    counts = [len(part) for part in most]
+
+    def most_of(*given):
+        parts = [given[sum(counts[:n]) : sum(counts[: n + 1])] for n in range(3)]
+        return [stacked([parts[0], parts[1], (), parts[2]])]
+
     sends, _, _, take = background(x_pieces=2)
-    moved, _, _ = step([(swap_chip, gt_other.astype(bf16)), (far, wide), *sends])
+    moved, (mix_whole,), _ = step(
+        [(swap_chip, gt_other.astype(bf16)), (far, wide), *sends],
+        most_of,
+        [array for part in most for array in part],
+    )
     grad_other = moved[0].astype(f32)
     wide = wide + moved[1]
     take(moved[2:], [])
-    while y_queue or x_queue:
-        sends, _, _, take = background(x_pieces=2)
-        moved, _, _ = step(sends) if sends else ([], [], [])
-        take(moved, [])
+    mix_whole = filled(mix_whole, 2, one_part("v0"))
     turned = swap_core(jnp.concatenate([bound_sum, wide[edge:]]))
     grad_bound = joined(bound_sum, turned[:hc], core, 0)
 
@@ -1044,7 +1078,7 @@
         joined(out_own, out_other, y, 0),
         joined(gt_own, grad_other, y, 0),
         wide[:width],
-        stacked([found[key] if pairs else (total(key),) for key in ("q0", "k0", "v0", "g0")]),
+        mix_whole,
         grad_bound,
         wide[edge:] + turned[hc:],
         total("o0"),

time: 581 us -> 574 us (0.988)
  Pallas kernels: 143 us -> 150 us
  starting transfers between devices: 82.7 us -> 76.8 us
    pallas_call x9 -> x8, Pallas kernels: 32.3 us -> 39.3 us  [the longest x6 25.8 us: head_gradients(): pl.pallas_call(partial(heads_kernel, first, half), in_specs=[SMEM] + [VME...]
    unnamed x346 -> x328, local copies, waits for them, and re-layouts: 24.3 us -> 20 us
    ppermute x12 -> x11, starting transfers between devices: 15.1 us -> 12.8 us  [swap_group(): return lax.ppermute(x, 'dp', [(0, 1), (1, 0)])]
    ppermute x32 -> x31, starting transfers between devices: 35.5 us -> 34.4 us  [swap_chip(): return lax.ppermute(x, 'row', CHIP)]
    ppermute x32 -> x31, waiting for transfers between devices: 48.8 us -> 48.9 us  [swap_chip(): return lax.ppermute(x, 'row', CHIP)]
  transfers between devices with their start and end apart: 84 -> 82, of which waited for: 50 -> 51; matrix products, arithmetic and copies ran while one was open for 14% -> 14% of each run, Pallas kernels for 24% -> 26%
where the time goes in v4:
time: 574 us; the launch traced here: 564 us
  waiting for transfers between devices  191 us (33%)
  Pallas kernels  150 us (26%)
  starting transfers between devices  76.8 us (13%)
  other arithmetic  49.6 us (9%)
  matrix products  46.8 us (8%)
  local copies, waits for them, and re-layouts  46 us (8%)
    ppermute x24, waiting for transfers between devices, up(): lax.ppermute(x, 'col', [(folded(n), folded((n + 1) % count)) for n in ran...  126 us
    ppermute x31, waiting for transfers between devices, swap_chip(): return lax.ppermute(x, 'row', CHIP)  48.9 us
    ppermute x31, starting transfers between devices, swap_chip(): return lax.ppermute(x, 'row', CHIP)  34.4 us
    ppermute x24, starting transfers between devices, up(): lax.ppermute(x, 'col', [(folded(n), folded((n + 1) % count)) for n in ran...  25.8 us
    pallas_call x6, Pallas kernels, head_gradients(): pl.pallas_call(partial(heads_kernel, first, half), in_specs=[SMEM] + [VME...  25.8 us
    dot_general x16, matrix products, mm_nt(): lax.dot_general(left, right, (((1,), (1,)), ((), ())), preferred_element_...  22.8 us
    pallas_call x2, Pallas kernels, weight_gradient_pieces(): pl.pallas_call(partial(pieces_kernel, len(lefts)), grid=(wide // tile,),...  21.4 us
    unnamed x328, local copies, waits for them, and re-layouts  20 us
  transfers between devices with their start and end apart: 82, of which 51 were waited for; matrix products, arithmetic and copies ran while one was open for 14% of the time, Pallas kernels for 26%

profile of v4, /device:TPU:0, one launch (start us, length us, event | category | flops | bytes accessed | tf_op | source)
XLA Modules:
  0.0 564.0 jit_solution(16407255121307394879)
XLA Ops:
  18.6 14.1 %collective-permute-done.4 = bf16[256,512]{1,0:T(8,128)(2,1)S(1)} collective-permute-done((bf16[256,512]{1,0:T(8,128)(2,1)S(1)}, bf16[256,512]{1,0:T(8,128)(2,1)S(1)}, u32[]{:S(2)}, u32[]{:S(2)}) %collective-permute-start.4) | collective-permute-done | bytes 262176 | tf_op jit(solution)/shard_map/ppermute | solution.py:26
  34.9 12.1 %collective-permute-done.6 = bf16[256,1024]{1,0:T(8,128)(2,1)} collective-permute-done((bf16[256,1024]{1,0:T(8,128)(2,1)S(1)}, bf16[256,1024]{1,0:T(8,128)(2,1)}, u32[]{:S(2)}, u32[]{:S(2)}) %collective-permute-start.6) | collective-permute-done | bytes 524320 | tf_op jit(solution)/shard_map/ppermute | solution.py:586
  50.5 10.1 %collective-permute-done.8 = bf16[256,1024]{1,0:T(8,128)(2,1)} collective-permute-done((bf16[256,1024]{1,0:T(8,128)(2,1)}, bf16[256,1024]{1,0:T(8,128)(2,1)}, u32[]{:S(2)}, u32[]{:S(2)}) %collective-permute-start.8) | collective-permute-done | bytes 524320 | tf_op jit(solution)/shard_map/ppermute | solution.py:586
  66.0 7.7 %collective-permute-done.10 = bf16[256,1024]{1,0:T(8,128)(2,1)} collective-permute-done((bf16[256,1024]{1,0:T(8,128)(2,1)S(1)}, bf16[256,1024]{1,0:T(8,128)(2,1)}, u32[]{:S(2)}, u32[]{:S(2)}) %collective-permute-start.10) | collective-permute-done | bytes 524320 | tf_op jit(solution)/shard_map/ppermute | solution.py:586
  93.1 14.7 %recurrence_local.1 = (f32[1024,256]{1,0:T(8,128)}, bf16[1024,256]{1,0:T(8,128)(2,1)}, bf16[1024,256]{1,0:T(8,128)(2,1)}, bf16[1024,256]{1,0:T(8,128)(2,1)}, f32...) custom-call(f32[1024,1024]{1,0:T(8,128)} %convolution_add_fusion.4.keep, ...), custom_call_target="tpu_custom_call" | custom-call | tf_op jit(solution)/shard_map/recurrence_local/pallas_call | solution.py:279
  110.8 5.5 collective-permute-done.16.peerd_ref
  122.0 5.6 recurrence_finish.1
  168.3 9.9 %collective-permute-done.22 = bf16[256,1024]{1,0:T(8,128)(2,1)S(1)} collective-permute-done((bf16[256,1024]{1,0:T(8,128)(2,1)S(1)}, bf16[256,1024]{1,0:T(8,128)(2,1)S(1)}, u32[]{:S(2)}, u32[]{:S(2)}) %collective-permute-start.22) | collective-permute-done | bytes 524320 | tf_op jit(solution)/shard_map/ppermute | solution.py:586
  183.4 9.4 %collective-permute-done.24 = bf16[256,1024]{1,0:T(8,128)(2,1)S(1)} collective-permute-done((bf16[256,1024]{1,0:T(8,128)(2,1)S(1)}, bf16[256,1024]{1,0:T(8,128)(2,1)S(1)}, u32[]{:S(2)}, u32[]{:S(2)}) %collective-permute-start.24) | collective-permute-done | bytes 524320 | tf_op jit(solution)/shard_map/ppermute | solution.py:586
  198.1 13.8 %collective-permute-done.27 = bf16[256,1024]{1,0:T(8,128)(2,1)S(1)} collective-permute-done((bf16[256,1024]{1,0:T(8,128)(2,1)S(1)}, bf16[256,1024]{1,0:T(8,128)(2,1)S(1)}, u32[]{:S(2)}, u32[]{:S(2)}) %collective-permute-start.27) | collective-permute-done | bytes 524320 | tf_op jit(solution)/shard_map/ppermute | solution.py:586
  215.8 13.0 %collective-permute-done.29 = bf16[256,1024]{1,0:T(8,128)(2,1)S(1)} collective-permute-done((bf16[256,1024]{1,0:T(8,128)(2,1)S(1)}, bf16[256,1024]{1,0:T(8,128)(2,1)S(1)}, u32[]{:S(2)}, u32[]{:S(2)}) %collective-permute-start.29) | collective-permute-done | bytes 524320 | tf_op jit(solution)/shard_map/ppermute | solution.py:586
  230.7 7.4 %collective-permute-done.32 = bf16[64,2816]{1,0:T(8,128)(2,1)S(1)} collective-permute-done((bf16[64,2816]{1,0:T(8,128)(2,1)S(1)}, bf16[64,2816]{1,0:T(8,128)(2,1)S(1)}, u32[]{:S(2)}, u32[]{:S(2)}) %collective-permute-start.32) | collective-permute-done | bytes 360480 | tf_op jit(solution)/shard_map/ppermute | solution.py:26
  274.2 10.6 %weight_gradient_pieces.2 = (bf16[128,2816]{1,0:T(8,128)(2,1)}, bf16[128,2816]{1,0:T(8,128)(2,1)}, bf16[128,2816]{1,0:T(8,128)(2,1)}, bf16[128,2816]{1,0:T(8,128)(2,1)}) custom-call(bf16[512,512]{1,0:T(8,128)(2,1)} %copy-done.40, bf16[512,512]{1,0:T(8,128)(2,1)} %copy-done.41, bf16[512,2816]{1,0:T(8,128)(2,1)} %copy-done.15, bf16[512,2816]{1,0:T(8,128)(2,1)} %copy-done.26), custom_call_target="tpu_custom_call" | custom-call | tf_op jit(solution)/shard_map/weight_gradient_pieces/pallas_call | solution.py:426
  290.8 10.8 %weight_gradient_pieces.3 = (f32[128,2816]{1,0:T(8,128)}, f32[128,2816]{1,0:T(8,128)}, f32[128,2816]{1,0:T(8,128)}, f32[128,2816]{1,0:T(8,128)}) custom-call(bf16[512,512]{1,0:T(8,128)(2,1)} %copy-done.48, bf16[512,512]{1,0:T(8,128)(2,1)} %copy-done.49, bf16[512,2816]{1,0:T(8,128)(2,1)} %copy-done.15, bf16[512,2816]{1,0:T(8,128)(2,1)} %copy-done.26), custom_call_target="tpu_custom_call" | custom-call | tf_op jit(solution)/shard_map/weight_gradient_pieces/pallas_call | solution.py:426
  315.5 8.4 %collective-permute-done.41 = bf16[256,1024]{1,0:T(8,128)(2,1)S(1)} collective-permute-done((bf16[256,1024]{1,0:T(8,128)(2,1)S(1)}, bf16[256,1024]{1,0:T(8,128)(2,1)S(1)}, u32[]{:S(2)}, u32[]{:S(2)}) %collective-permute-start.41) | collective-permute-done | bytes 524320 | tf_op jit(solution)/shard_map/ppermute | solution.py:586
  340.4 7.2 %collective-permute-done.45 = bf16[256,1024]{1,0:T(8,128)(2,1)} collective-permute-done((bf16[256,1024]{1,0:T(8,128)(2,1)}, bf16[256,1024]{1,0:T(8,128)(2,1)}, u32[]{:S(2)}, u32[]{:S(2)}) %collective-permute-start.45) | collective-permute-done | bytes 524320 | tf_op jit(solution)/shard_map/ppermute | solution.py:586
  359.5 5.9 %collective-permute-done.48 = bf16[256,1024]{1,0:T(8,128)(2,1)} collective-permute-done((bf16[256,1024]{1,0:T(8,128)(2,1)}, bf16[256,1024]{1,0:T(8,128)(2,1)}, u32[]{:S(2)}, u32[]{:S(2)}) %collective-permute-start.48) | collective-permute-done | bytes 524320 | tf_op jit(solution)/shard_map/ppermute | solution.py:586
  393.9 5.3 recurrence_back_local.1
  418.2 17.4 %recurrence_back_finish.1 = (bf16[1024,1024]{1,0:T(8,128)(2,1)}, f32[1,256]{1,0:T(1,128)}) custom-call(f32[1024,1024]{1,0:T(8,128)} %convolution_add_fusion.4.keep_ref, bf16[1024,1024]{1,0:T(8,128)(2,1)} %copy-done.14, f32[1,256]{1,0:T(1,128)} %bitcast.143, f32[1024,1]{1,0:T(8,128)} %bitcast.105, f32[4,1,256]{2,1,0:T(1,128)} %reshape.93.idr_ref, ...), custom_call_target="tpu_custom_call" | custom-call | tf_op jit(solution)/shard_map/recurrence_back_finish/pallas_call | solution.py:375
  472.0 5.5 collective-permute-done.63
  501.8 7.3 %collective-permute-done.67 = bf16[256,1024]{1,0:T(8,128)(2,1)} collective-permute-done((bf16[256,1024]{1,0:T(8,128)(2,1)}, bf16[256,1024]{1,0:T(8,128)(2,1)}, u32[]{:S(2)}, u32[]{:S(2)}) %collective-permute-start.67) | collective-permute-done | bytes 524320 | tf_op jit(solution)/shard_map/ppermute | solution.py:586
  523.1 8.2 %halves_of_rows.1 = f32[512,2,1408]{2,1,0:T(2,128)} custom-call(bf16[128,2816]{1,0:T(8,128)(2,1)S(1)} %copy-done, bf16[128,2816]{1,0:T(8,128)(2,1)S(1)} %copy-done.5, bf16[128,2816]{1,0:T(8,128)(2,1)S(1)} %copy-done.1, bf16[128,2816]{1,0:T(8,128)(2,1)S(1)} %copy-done.7, bf16[128,2816]{1,0:T(8,128)(2,1)S(1)} %copy-done.2, bf16[128,2816]{1,0:T(8,128)(2,1)S(1)} %copy-done.9, ...), custom_call_target="tpu_custom_call" | custom-call | tf_op jit(solution)/shard_map/halves_of_rows/pallas_call | solution.py:473
  546.4 6.6 %stacked.1.refs_0_ = f32[512,4,512]{2,1,0:T(4,128)} custom-call(bf16[512,512]{1,0:T(8,128)(2,1)} %get-tuple-element.554.refs_0_, bf16[512,512]{1,0:T(8,128)(2,1)} %get-tuple-element.555.refs_1_, bf16[512,512]{1,0:T(8,128)(2,1)} %get-tuple-element.556.refs_2_, bf16[512,512]{1,0:T(8,128)(2,1)} %get-tuple-element.557.refs_3_, ...), custom_call_target="tpu_custom_call" | custom-call | tf_op jit(solution)/shard_map/stacked/pallas_call | solution.py:498
  555.8 6.9 %filled.1 = f32[512,4,512]{2,1,0:T(4,128)} custom-call(f32[512,4,512]{2,1,0:T(4,128)} %stacked.1.refs_0_, bf16[512,512]{1,0:T(8,128)(2,1)} %copy-done.84, bf16[512,512]{1,0:T(8,128)(2,1)} %copy-done.137), custom_call_target="tpu_custom_call", output_to_operand_aliasing={{}: (0, {})} | custom-call | tf_op jit(solution)/shard_map/filled/pallas_call | solution.py:564
  (651 shorter events, 337.8 us)
Async XLA Ops:
  13.0 19.6 %collective-permute-start.5 = (bf16[128,4,512]{2,1,0:T(4,128)(2,1)S(1)}, bf16[128,4,512]{2,1,0:T(4,128)(2,1)S(1)}, u32[]{:S(2)}, u32[]{:S(2)}) collective-permute-start(bf16[128,4,512]{2,1,0:T(4,128)(2,1)S(1)} %get-tuple-element.292), channel_id=1, source_target_pairs={{0,8},{8,0},{4,12},{12,4},{1,9},{9,1},{5,13},{13,5},{2,10},{10,2},... | collective-permute-start | bytes 1572872 | tf_op jit(solution)/shard_map/ppermute | solution.py:26
  15.2 17.5 %collective-permute-start.3 = (bf16[256,1024]{1,0:T(8,128)(2,1)S(1)}, bf16[256,1024]{1,0:T(8,128)(2,1)S(1)}, u32[]{:S(2)}, u32[]{:S(2)}) collective-permute-start(bf16[256,1024]{1,0:T(8,128)(2,1)S(1)} %pad_maximum_fusion.10), channel_id=1, source_target_pairs={{0,1},{1,3},{3,2},{2,0},{4,5},{5,7},{7,6},{6,4},{8,9},{9,11},{11,1... | collective-permute-start | bytes 1572872 | tf_op jit(solution)/shard_map/ppermute | solution.py:586
  87.0 20.7 %collective-permute-start.13 = (bf16[256,1024]{1,0:T(8,128)(2,1)}, bf16[256,1024]{1,0:T(8,128)(2,1)}, u32[]{:S(2)}, u32[]{:S(2)}) collective-permute-start(bf16[256,1024]{1,0:T(8,128)(2,1)} %collective-permute-done.10), channel_id=1, source_target_pairs={{0,1},{1,3},{3,2},{2,0},{4,5},{5,7},{7,6},{6,4},{8,9},{9,11},{11,1... | collective-permute-start | bytes 1572872 | tf_op jit(solution)/shard_map/ppermute | solution.py:586
  88.9 18.8 %collective-permute-start.14 = (bf16[512,512]{1,0:T(8,128)(2,1)}, bf16[512,512]{1,0:T(8,128)(2,1)}, u32[]{:S(2)}, u32[]{:S(2)}) collective-permute-start(bf16[512,512]{1,0:T(8,128)(2,1)} %param.17), channel_id=1, source_target_pairs={{0,8},{8,0},{4,12},{12,4},{1,9},{9,1},{5,13},{13,5},{2,10},{10,2},... | collective-permute-start | bytes 1572872 | tf_op jit(solution)/shard_map/ppermute | solution.py:26
  143.1 18.5 %collective-permute-start.21 = (bf16[704,512]{1,0:T(8,128)(2,1)}, bf16[704,512]{1,0:T(8,128)(2,1)}, u32[]{:S(2)}, u32[]{:S(2)}) collective-permute-start(bf16[704,512]{1,0:T(8,128)(2,1)} %get-tuple-element.347), channel_id=1, source_target_pairs={{0,8},{8,0},{4,12},{12,4},{1,9},{9,1},{5,13},{13,5},{2,10},{10,2},... | collective-permute-start | bytes 2162696 | tf_op jit(solution)/shard_map/ppermute | solution.py:26
  183.3 30.3 %collective-permute-start.33 = (bf16[512,1408]{1,0:T(8,128)(2,1)S(1)}, bf16[512,1408]{1,0:T(8,128)(2,1)S(1)}, u32[]{:S(2)}, u32[]{:S(2)}) collective-permute-start(bf16[512,1408]{1,0:T(8,128)(2,1)S(1)} %fusion.1), channel_id=1, source_target_pairs={{0,4},{4,0},{8,12},{12,8},{1,5},{5,1},{9,13},{13,9},{2,6},{6,2},{1... | collective-permute-start | bytes 4325384 | tf_op jit(solution)/shard_map/ppermute | solution.py:22
  269.2 18.5 %collective-permute-start.38 = (bf16[1408,256]{1,0:T(8,128)(2,1)}, bf16[1408,256]{1,0:T(8,128)(2,1)}, u32[]{:S(2)}, u32[]{:S(2)}) collective-permute-start(bf16[1408,256]{1,0:T(8,128)(2,1)} %fusion.3), channel_id=1, source_target_pairs={{0,8},{8,0},{4,12},{12,4},{1,9},{9,1},{5,13},{13,5},{2,10},{10,2},... | collective-permute-start | bytes 2162696 | tf_op jit(solution)/shard_map/ppermute | solution.py:26
  289.8 17.7 %collective-permute-start.40 = (bf16[1408,256]{1,0:T(8,128)(2,1)}, bf16[1408,256]{1,0:T(8,128)(2,1)}, u32[]{:S(2)}, u32[]{:S(2)}) collective-permute-start(bf16[1408,256]{1,0:T(8,128)(2,1)} %fusion.4), channel_id=1, source_target_pairs={{0,8},{8,0},{4,12},{12,4},{1,9},{9,1},{5,13},{13,5},{2,10},{10,2},... | collective-permute-start | bytes 2162696 | tf_op jit(solution)/shard_map/ppermute | solution.py:26
  330.2 18.5 %collective-permute-start.46 = (bf16[128,2816]{1,0:T(8,128)(2,1)}, bf16[128,2816]{1,0:T(8,128)(2,1)}, u32[]{:S(2)}, u32[]{:S(2)}) collective-permute-start(bf16[128,2816]{1,0:T(8,128)(2,1)} %get-tuple-element.420), channel_id=1, source_target_pairs={{0,8},{8,0},{4,12},{12,4},{1,9},{9,1},{5,13},{13,5},{2,10},{10,2},... | collective-permute-start | bytes 2162696 | tf_op jit(solution)/shard_map/ppermute | solution.py:26
  331.4 18.0 %collective-permute-start.47 = (bf16[1408,256]{1,0:T(8,128)(2,1)S(1)}, bf16[1408,256]{1,0:T(8,128)(2,1)S(1)}, u32[]{:S(2)}, u32[]{:S(2)}) collective-permute-start(bf16[1408,256]{1,0:T(8,128)(2,1)S(1)} %copy-done.59), channel_id=1, source_target_pairs={{0,16},{16,0},{1,17},{17,1},{2,18},{18,2},{3,19},{19,3},{4,20},{20... | collective-permute-start | bytes 2162696 | tf_op jit(solution)/shard_map/ppermute | solution.py:577
  409.4 26.5 %collective-permute-start.60 = (bf16[128,2816]{1,0:T(8,128)(2,1)S(1)}, bf16[128,2816]{1,0:T(8,128)(2,1)S(1)}, u32[]{:S(2)}, u32[]{:S(2)}) collective-permute-start(bf16[128,2816]{1,0:T(8,128)(2,1)S(1)} %copy-done.2), channel_id=1, source_target_pairs={{0,16},{16,0},{1,17},{17,1},{2,18},{18,2},{3,19},{19,3},{4,20},{20... | collective-permute-start | bytes 2162696 | tf_op jit(solution)/shard_map/ppermute | solution.py:577
  410.8 24.8 %collective-permute-start.57 = (bf16[256,1024]{1,0:T(8,128)(2,1)}, bf16[256,1024]{1,0:T(8,128)(2,1)}, u32[]{:S(2)}, u32[]{:S(2)}) collective-permute-start(bf16[256,1024]{1,0:T(8,128)(2,1)} %pad_maximum_fusion.20), channel_id=1, source_target_pairs={{0,1},{1,3},{3,2},{2,0},{4,5},{5,7},{7,6},{6,4},{8,9},{9,11},{11,1... | collective-permute-start | bytes 1572872 | tf_op jit(solution)/shard_map/ppermute | solution.py:586
  411.5 24.1 %collective-permute-start.58 = (bf16[512,512]{1,0:T(8,128)(2,1)}, bf16[512,512]{1,0:T(8,128)(2,1)}, u32[]{:S(2)}, u32[]{:S(2)}) collective-permute-start(bf16[512,512]{1,0:T(8,128)(2,1)} %weight_gradients.6), channel_id=1, source_target_pairs={{0,8},{8,0},{4,12},{12,4},{1,9},{9,1},{5,13},{13,5},{2,10},{10,2},... | collective-permute-start | bytes 1572872 | tf_op jit(solution)/shard_map/ppermute | solution.py:26
  412.4 23.4 %collective-permute-start.59 = (bf16[512,512]{1,0:T(8,128)(2,1)}, bf16[512,512]{1,0:T(8,128)(2,1)}, u32[]{:S(2)}, u32[]{:S(2)}) collective-permute-start(bf16[512,512]{1,0:T(8,128)(2,1)} %head_gradients.6), channel_id=1, source_target_pairs={{0,8},{8,0},{4,12},{12,4},{1,9},{9,1},{5,13},{13,5},{2,10},{10,2},... | collective-permute-start | bytes 1572872 | tf_op jit(solution)/shard_map/ppermute | solution.py:26
  450.5 26.9 %collective-permute-start.65 = (bf16[128,2816]{1,0:T(8,128)(2,1)S(1)}, bf16[128,2816]{1,0:T(8,128)(2,1)}, u32[]{:S(2)}, u32[]{:S(2)}) collective-permute-start(bf16[128,2816]{1,0:T(8,128)(2,1)S(1)} %copy-done.3), channel_id=1, source_target_pairs={{0,16},{16,0},{1,17},{17,1},{2,18},{18,2},{3,19},{19,3},{4,20},{20... | collective-permute-start | bytes 2162696 | tf_op jit(solution)/shard_map/ppermute | solution.py:577
  451.2 20.7 %collective-permute-start.62 = (bf16[256,1024]{1,0:T(8,128)(2,1)}, bf16[256,1024]{1,0:T(8,128)(2,1)}, u32[]{:S(2)}, u32[]{:S(2)}) collective-permute-start(bf16[256,1024]{1,0:T(8,128)(2,1)} %pad_maximum_fusion.21), channel_id=1, source_target_pairs={{0,1},{1,3},{3,2},{2,0},{4,5},{5,7},{7,6},{6,4},{8,9},{9,11},{11,1... | collective-permute-start | bytes 1572872 | tf_op jit(solution)/shard_map/ppermute | solution.py:586
  452.5 24.9 %collective-permute-start.63 = (bf16[256,1024]{1,0:T(8,128)(2,1)}, bf16[256,1024]{1,0:T(8,128)(2,1)}, u32[]{:S(2)}, u32[]{:S(2)}) collective-permute-start(bf16[256,1024]{1,0:T(8,128)(2,1)} %pad_maximum_fusion.22), channel_id=1, source_target_pairs={{0,1},{1,3},{3,2},{2,0},{4,5},{5,7},{7,6},{6,4},{8,9},{9,11},{11,1... | collective-permute-start | bytes 1572872 | tf_op jit(solution)/shard_map/ppermute | solution.py:586
  454.4 17.5 %collective-permute-start.64 = (f32[1408]{0:T(1024)S(1)}, f32[1408]{0:T(1024)S(1)}, u32[]{:S(2)}, u32[]{:S(2)}) collective-permute-start(f32[1408]{0:T(1024)S(1)} %pad_maximum_fusion.27), channel_id=1, source_target_pairs={{0,8},{8,0},{4,12},{12,4},{1,9},{9,1},{5,13},{13,5},{2,10},{10,2},... | collective-permute-start | bytes 16904 | tf_op jit(solution)/shard_map/ppermute | solution.py:26
  482.0 28.8 %collective-permute-start.68 = (bf16[1024,512]{1,0:T(8,128)(2,1)}, bf16[1024,512]{1,0:T(8,128)(2,1)}, u32[]{:S(2)}, u32[]{:S(2)}) collective-permute-start(bf16[1024,512]{1,0:T(8,128)(2,1)} %head_gradients.7), channel_id=1, source_target_pairs={{0,8},{8,0},{4,12},{12,4},{1,9},{9,1},{5,13},{13,5},{2,10},{10,2},... | collective-permute-start | bytes 3145736 | tf_op jit(solution)/shard_map/ppermute | solution.py:26
  484.3 17.4 %collective-permute-start.66 = (bf16[256,1024]{1,0:T(8,128)(2,1)}, bf16[256,1024]{1,0:T(8,128)(2,1)}, u32[]{:S(2)}, u32[]{:S(2)}) collective-permute-start(bf16[256,1024]{1,0:T(8,128)(2,1)} %pad_maximum_fusion.23), channel_id=1, source_target_pairs={{0,1},{1,3},{3,2},{2,0},{4,5},{5,7},{7,6},{6,4},{8,9},{9,11},{11,1... | collective-permute-start | bytes 1572872 | tf_op jit(solution)/shard_map/ppermute | solution.py:586
  484.8 24.3 %collective-permute-start.67 = (bf16[256,1024]{1,0:T(8,128)(2,1)}, bf16[256,1024]{1,0:T(8,128)(2,1)}, u32[]{:S(2)}, u32[]{:S(2)}) collective-permute-start(bf16[256,1024]{1,0:T(8,128)(2,1)} %pad_maximum_fusion.24), channel_id=1, source_target_pairs={{0,1},{1,3},{3,2},{2,0},{4,5},{5,7},{7,6},{6,4},{8,9},{9,11},{11,1... | collective-permute-start | bytes 1572872 | tf_op jit(solution)/shard_map/ppermute | solution.py:586
  487.6 21.5 %collective-permute-start.69 = (bf16[512,512]{1,0:T(8,128)(2,1)}, bf16[512,512]{1,0:T(8,128)(2,1)}, u32[]{:S(2)}, u32[]{:S(2)}) collective-permute-start(bf16[512,512]{1,0:T(8,128)(2,1)} %weight_gradients.7), channel_id=1, source_target_pairs={{0,16},{16,0},{1,17},{17,1},{2,18},{18,2},{3,19},{19,3},{4,20},{20... | collective-permute-start | bytes 1572872 | tf_op jit(solution)/shard_map/ppermute | solution.py:577
  488.1 22.7 %collective-permute-start.70 = (bf16[512,512]{1,0:T(8,128)(2,1)}, bf16[512,512]{1,0:T(8,128)(2,1)}, u32[]{:S(2)}, u32[]{:S(2)}) collective-permute-start(bf16[512,512]{1,0:T(8,128)(2,1)} %head_gradients.9.refs_4_), channel_id=1, source_target_pairs={{0,16},{16,0},{1,17},{17,1},{2,18},{18,2},{3,19},{19,3},{4,20},{20... | collective-permute-start | bytes 1572872 | tf_op jit(solution)/shard_map/ppermute | solution.py:577
  515.3 22.1 %collective-permute-start.76 = (bf16[1024,512]{1,0:T(8,128)(2,1)S(1)}, bf16[1024,512]{1,0:T(8,128)(2,1)S(1)}, u32[]{:S(2)}, u32[]{:S(2)}) collective-permute-start(bf16[1024,512]{1,0:T(8,128)(2,1)S(1)} %add_convert_fusion.2), channel_id=1, source_target_pairs={{0,16},{16,0},{1,17},{17,1},{2,18},{18,2},{3,19},{19,3},{4,20},{20... | collective-permute-start | bytes 3145736 | tf_op jit(solution)/shard_map/ppermute | solution.py:577
  (212 other events, 2028.2 us)
